TPU v7x, 128 devices: a whole 4x4x4 slice. The times are simulated.
128 devices in a mesh: occ: 8 (over x, core), vir: 16 (over y, z).
Axes of the slice: x: 4, y: 4, z: 4, core: 2. Of those that a mesh axis runs over, the one named last changes fastest.
Arguments:
- right_prev: bfloat16 [8192, 32768], P(None, ('vir', 'occ')), may hold values from -6 to 6
- amplitudes: bfloat16 [8192, 8192], P('occ', 'vir'), may hold values from -6 to 6
- integrals: bfloat16 [16, 4096, 2048], P('vir'), may hold values from -0.09375 to 0.09375
- send_tiles: int32 [16, 16, 2], replicated, may hold values from 0 to 3, as said below
- pair_count: int32 [16, 16], replicated, may hold values from 0 to 2, as said below
Outputs:
- residual: float32 [8192, 32768], P(None, ('vir', 'occ'))
Inputs may be any that keep to these rules, and one draw needn't show every extreme that they name: `send_tiles`: the 2 slots of one sender and one owner name distinct tiles. `pair_count`: one owner receives 2 live slots from every sender.
All inputs are finite; a program needn't handle non-finite values.
Results may differ from a plain program's by a relative error of at most 0.0017.
Values may be sent and summed in bfloat16 or wider, within the bound.
No kernel may reach another device: no remote copies, remote signals or barrier semaphores. Data moves between devices by JAX's collectives and lax.ppermute only.
A program may use at most 128 MiB of HBM per device.

v0:
```python
import jax
import jax.numpy as jnp
from jax import lax
from jax.sharding import PartitionSpec as P

TILE = 128
CAP = 2


def local(right_prev, amplitudes, integrals, send_tiles, pair_count):
    row_count = amplitudes.shape[0]
    vir_size = lax.axis_size("vir")
    own_index = lax.axis_index("vir")
    amp_tiles = amplitudes.reshape(row_count, -1, TILE)
    slot_ids = jnp.arange(CAP, dtype=jnp.int32)
    gathered = lax.all_gather(amp_tiles, "vir", axis=1, tiled=True)
    chosen = lax.dynamic_index_in_dim(send_tiles, own_index, 1, keepdims=False)
    counts = lax.dynamic_index_in_dim(pair_count, own_index, 1, keepdims=False)
    columns = (
        jnp.arange(vir_size, dtype=jnp.int32)[:, None] * amp_tiles.shape[1] + chosen
    ).reshape(-1)
    live_slots = (slot_ids[None, :] < counts[:, None]).reshape(-1)
    picked = jnp.take(gathered, columns, axis=1)
    picked = jnp.where(live_slots[None, :, None], picked, jnp.zeros_like(picked))
    received = picked.reshape(row_count, -1)
    ladder = jnp.dot(received, integrals[0], preferred_element_type=jnp.float32).astype(
        jnp.bfloat16
    )
    relaid = lax.all_to_all(ladder, "occ", split_axis=1, concat_axis=0, tiled=True)
    return right_prev.astype(jnp.float32) + relaid.astype(jnp.float32)


def solution(mesh):
    in_specs = (P(None, ("vir", "occ")), P("occ", "vir"), P("vir", None, None), P(), P())
    out_specs = P(None, ("vir", "occ"))
    return jax.shard_map(local, mesh=mesh, in_specs=in_specs, out_specs=out_specs, check_vma=False)
```

profile of v0, /device:TPU:1, one launch (start us, length us, event | category | flops | bytes accessed | tf_op | source)
XLA Modules:
  0.0 243.5 jit_solution(12418351800210398530)
XLA Ops:
  6.5 0.0 copy-start
  6.5 0.0 all-gather.2.cloned.1.call-start
  6.5 1.5 copy.12
  8.0 1.3 copy.13
  9.3 0.0 all-gather.2.cloned.1.call-update
  9.4 0.1 add.57
  9.5 0.1 add.62
  9.6 0.1 add.58
  9.6 0.0 copy-done
  9.7 0.4 dynamic-slice_reduce_fusion
  10.1 0.1 squeeze.12
  10.2 0.1 squeeze.11
  10.3 0.9 dynamic-slice_reduce_fusion.1
  11.1 0.1 iota_compare_fusion
  11.2 0.1 lt.54
  11.4 112.8 %all-gather.2.cloned.1.call-done = bf16[1024,64,128]{2,0,1:T(8,128)(2,1)} async-done(((bf16[1024,4,128]{2,0,1:T(8,128)(2,1)}), bf16[1024,64,128]{2,0,1:T(8,128)(2,1)}) %all-gather.2.cloned.1.call-update) | async-done | bytes 16777232 | tf_op jit(solution)/shard_map/all_gather | solution.py:16
  124.2 11.0 %gather_fusion = bf16[32,1024,128]{2,1,0:T(8,128)(2,1)} fusion(bf16[1024,64,128]{2,0,1:T(8,128)(2,1)} %all-gather.2.cloned.1.call-done, s32[1024]{0:T(1024)S(1)} %pad_clamp_fusion), kind=kCustom, calls=%fused_computation | custom fusion | bytes 16777344 | tf_op jit(solution)/shard_map/jit(_take)/gather | solution.py:23
  135.1 7.8 %select_bitcast_fusion = bf16[1024,32,128]{2,0,1:T(8,128)(2,1)} fusion(bf16[32,1024,128]{2,1,0:T(8,128)(2,1)} %gather_fusion, pred[32]{0:T(512)(128)(4,1)S(1)} %lt.54, pred[32]{0:T(512)(128)(4,1)S(1)} %compare_and_fusion), kind=kLoop, calls=%fused_computation.4 | loop fusion | flops 8388608 | bytes 16777280 | tf_op jit(solution)/shard_map/jit(_where)/select_n | solution.py:24
  142.9 12.0 %copy.14 = bf16[1024,32,128]{0,2,1:T(8,128)(2,1)} copy(bf16[1024,32,128]{2,0,1:T(8,128)(2,1)} %select_bitcast_fusion) | data formatting | bytes 16777216 | tf_op jit(solution)/shard_map/jit(_where)/select_n | solution.py:24
  154.8 22.8 %fusion.2 = bf16[1024,2048]{1,0:T(8,128)(2,1)S(1)} fusion(bf16[1024,4096]{0,1:T(8,128)(2,1)} %bitcast.21, bf16[1,4096,2048]{2,1,0:T(8,128)(2,1)} %param.7), kind=kOutput, calls=%fused_computation.6 | convolution fusion | flops 17181966336 | bytes 29360128 | tf_op jit(solution)/shard_map/dot_general | solution.py:26
  177.7 0.0 copy-start.2
  177.7 0.3 copy.18
  178.0 0.0 copy-start.1
  178.0 54.3 %all_to_all.13 = bf16[1024,8,256]{2,0,1:T(8,128)(2,1)S(1)} all-to-all(bf16[1024,8,256]{2,0,1:T(8,128)(2,1)S(1)} %bitcast.20), channel_id=1, replica_groups=mesh['occ'=8,'vir'=16] {'occ'}, dimensions={1} | all-to-all | bytes 8388608 | tf_op jit(solution)/shard_map/all_to_all | solution.py:29
  232.3 0.0 copy-done.2
  232.3 4.3 %bitcast_add_fusion = f32[8192,256]{1,0:T(8,128)} fusion(bf16[8192,256]{1,0:T(8,128)(2,1)S(1)} %copy-done.2, bf16[1024,8,256]{2,0,1:T(8,128)(2,1)S(1)} %all_to_all.13), kind=kLoop, calls=%fused_computation.3 | loop fusion | flops 6291456 | bytes 16777216 | tf_op jit(solution)/shard_map/add | solution.py:30
  236.6 0.0 copy-done.1
  (4 shorter events, 0.0 us)
Async XLA Ops:
  6.5 3.1 %copy-start = (s32[16,16,2]{1,2,0:T(2,128)S(1)}, s32[16,16,2]{1,2,0:T(2,128)}, u32[]{:S(2)}) copy-start(s32[16,16,2]{1,2,0:T(2,128)} %param.8) | copy-start | bytes 6148
  6.5 117.6 %all-gather.2.cloned.1.call-start = ((), (), s32[]{:S(2)}) async-start(), calls=%async_computation.1 | async-start | bytes 17825792 | tf_op jit(solution)/shard_map/all_gather | solution.py:16
  177.7 54.6 %copy-start.2 = (bf16[8192,256]{1,0:T(8,128)(2,1)S(1)}, bf16[8192,256]{1,0:T(8,128)(2,1)}, u32[]{:S(2)}) copy-start(bf16[8192,256]{1,0:T(8,128)(2,1)} %param.5) | copy-start | bytes 12582916
  178.0 58.7 %copy-start.1 = (s32[16,16,2]{1,2,0:T(2,128)S(1)}, s32[16,16,2]{1,2,0:T(2,128)}, u32[]{:S(2)}) copy-start(s32[16,16,2]{1,2,0:T(2,128)} %param.8) | copy-start | bytes 6148
Sparse Core Ops, SparseCore 0:
  9.5 114.6 all-gather.1
where the time goes:
time: 244 us; the launch traced here: 243 us
  waiting for transfers between devices  113 us (46%)
  blocking collectives  54.3 us (22%)
  local copies, waits for them, and re-layouts  27.8 us (11%)
  matrix products  22.8 us (9%)
  between operations  13.5 us (6%)
  other arithmetic  12.2 us (5%)
    all_gather x1, waiting for transfers between devices, local(): gathered = lax.all_gather(amp_tiles, 'vir', axis=1, tiled=True)  113 us
    all_to_all x1, blocking collectives, local(): lax.all_to_all(ladder, 'occ', split_axis=1, concat_axis=0, tiled=True)  54.3 us
    dot_general x1, matrix products, local(): jnp.dot(received, integrals[0], preferred_element_type=jnp.float32)  22.8 us
    select_n x1, local copies, waits for them, and re-layouts, local(): jnp.where(live_slots[None, :, None], picked, jnp.zeros_like(picked))  12 us
    gather x1, local copies, waits for them, and re-layouts, local(): picked = jnp.take(gathered, columns, axis=1)  11 us
    select_n x1, other arithmetic, local(): jnp.where(live_slots[None, :, None], picked, jnp.zeros_like(picked))  7.76 us
  transfers between devices with their start and end apart: 1, of which 1 were waited for; matrix products, arithmetic and copies ran while one was open for 1% of the time, Pallas kernels for 0%

commit v1 on v0

v1 whole, which is shorter than its diff:
```python
import functools

import jax
import jax.numpy as jnp
from jax import lax
from jax.experimental import pallas as pl
from jax.experimental.pallas import tpu as pltpu
from jax.sharding import PartitionSpec as P

TILE = 128
CAP = 2
WAVES = ((256, 256), (256, 256))
NV = 16
NX = 4
YA, YB, ZA, ZB = 4, 12, 1, 3
ORDERS = (
    ((YA, YB, ZA, ZB), (ZA, ZB, YA, YB)),
    ((YB, YA, ZB, ZA), (ZB, ZA, YB, YA)),
)
HOPS = (2, 1, 3, 0)
VMEM = pl.BlockSpec(memory_space=pltpu.VMEM)
SMEM = pl.BlockSpec(memory_space=pltpu.SMEM)
ANY = pl.BlockSpec(memory_space=pl.ANY)


def flip(array, masks):
    pairs = [
        (o * NV + v, o * NV + (v ^ masks[o % 2]))
        for o in range(2 * NX)
        for v in range(NV)
    ]
    return lax.ppermute(array, ("occ", "vir"), pairs)


def hop(array, dx):
    pairs = [(o, (o + 2 * dx) % (2 * NX)) for o in range(2 * NX)]
    return lax.ppermute(array, "occ", pairs)


def swap(array):
    return lax.ppermute(array, "occ", [(o, o ^ 1) for o in range(2 * NX)])


def after(value, *others):
    return lax.optimization_barrier((value, *others))[0]


def near_memory(array):
    return pltpu.with_memory_space_constraint(array, pltpu.VMEM)


def sources(me, masks, core):
    d = [jnp.where(core == 0, masks[0][i], masks[1][i]) for i in range(3)]
    out = []
    for p in range(8):
        s = me
        for bit in range(3):
            if p >> bit & 1:
                s = s ^ d[bit]
        out.append(s)
    return out


def pack_kernel(masks, meta, sent, near, far, out):
    me, core = meta[0], meta[1]
    partner = me ^ jnp.where(core == 0, masks[0][3], masks[1][3])
    for p, s in enumerate(sources(me, masks, core)):
        for k in range(CAP):
            t = sent[(s * NV + partner) * CAP + k]
            ref = near if p < 4 else far
            out[p * CAP + k] = ref[(p % 4) * 4 + t]


def pack(meta, sent, near, far, masks):
    return pl.pallas_call(
        functools.partial(pack_kernel, masks),
        out_shape=pltpu.VMEM((16, near.shape[1], TILE), near.dtype),
        in_specs=[SMEM, SMEM, VMEM, VMEM],
        out_specs=VMEM,
        cost_estimate=pl.CostEstimate(
            flops=0, bytes_accessed=4 * near.size, transcendentals=0
        ),
        compiler_params=pltpu.CompilerParams(vmem_limit_bytes=8 << 20),
        name="pack",
    )(meta, sent, near_memory(near), near_memory(far))


def ladder_kernel(masks, meta, sent, live, near, far, last, weights, *refs):
    outs, lhs = refs[:4], refs[4]
    me, core = meta[0], meta[1]
    d4 = jnp.where(core == 0, masks[0][3], masks[1][3])
    for p, s in enumerate(sources(me, masks, core)):
        ref = near if p < 4 else far
        for k in range(CAP):
            t = sent[(s * NV + me) * CAP + k]
            for sender, tile in (
                (s, ref[(p % 4) * 4 + t]),
                (s ^ d4, last[p * CAP + k]),
            ):
                at = pl.multiple_of((sender * CAP + k) * TILE, TILE)
                keep = k < live[sender * NV + me]
                lhs[:, pl.ds(at, TILE)] = jnp.where(keep, tile, jnp.zeros_like(tile))
    width = weights.shape[1] // NX
    half = width // 2
    for j, dx in enumerate(HOPS):
        at = pl.multiple_of((meta[2] + dx) % NX * width, width)
        product = jnp.dot(
            lhs[...], weights[:, pl.ds(at, width)], preferred_element_type=jnp.float32
        ).astype(jnp.bfloat16)
        outs[j][core] = product[:, :half]
        outs[j][1 - core] = product[:, half:]


def ladder(meta, sent, live, near, far, last, weights, masks):
    rows, depth, width = near.shape[1], weights.shape[0], weights.shape[1] // 8
    return pl.pallas_call(
        functools.partial(ladder_kernel, masks),
        out_shape=[pltpu.VMEM((2, rows, width), jnp.bfloat16)] * 4,
        in_specs=[SMEM] * 3 + [VMEM] * 4,
        out_specs=[VMEM] * 4,
        scratch_shapes=[pltpu.VMEM((rows, depth), jnp.bfloat16)],
        cost_estimate=pl.CostEstimate(
            flops=2 * rows * depth * width * 8,
            bytes_accessed=2 * rows * depth,
            transcendentals=0,
        ),
        compiler_params=pltpu.CompilerParams(vmem_limit_bytes=12 << 20),
        name="ladder",
    )(meta, sent, live, near_memory(near), near_memory(far), near_memory(last), weights)


def add_kernel(base, n_rows, meta, prev, m0, m1, m2, m3, swapped, *refs):
    out, sums, sems = refs[-3:]
    rows = sums.shape[1]
    moved = (m0, m1, m2, m3)
    copies = []
    for j, dx in enumerate(HOPS):
        for b in range(2):
            source = (meta[2] + NX - dx) % NX * 2 + (meta[1] ^ b)
            at = pl.ds(pl.multiple_of(source * n_rows + base, 64), rows)
            block = moved[j][0] if b == 0 else swapped[j]
            i = 2 * j + b
            sums[i] = prev[at].astype(jnp.float32) + block.astype(jnp.float32)
            copy = pltpu.make_async_copy(sums.at[i], out.at[at], sems.at[i])
            copy.start()
            copies.append(copy)
    for copy in copies:
        copy.wait()


def add(meta, prev, pieces, swapped, total, base, n_rows):
    rows, width = swapped.shape[1], swapped.shape[2]
    args = [meta, prev, *map(near_memory, pieces), near_memory(swapped)]
    specs = [SMEM] + [VMEM] * 6
    aliases = {}
    if total is not None:
        aliases = {len(args): 0}
        args.append(total)
        specs.append(ANY)
    return pl.pallas_call(
        functools.partial(add_kernel, base, n_rows),
        out_shape=jax.ShapeDtypeStruct(prev.shape, jnp.float32),
        in_specs=specs,
        out_specs=ANY,
        scratch_shapes=[
            pltpu.VMEM((8, rows, width), jnp.float32),
            pltpu.SemaphoreType.DMA((8,)),
        ],
        input_output_aliases=aliases,
        cost_estimate=pl.CostEstimate(
            flops=8 * rows * width, bytes_accessed=32 * rows * width, transcendentals=0
        ),
        compiler_params=pltpu.CompilerParams(vmem_limit_bytes=8 << 20),
        name="residual",
    )(*args)


def local(right_prev, amplitudes, integrals, send_tiles, pair_count):
    n_rows = amplitudes.shape[0]
    occ, vir = lax.axis_index("occ"), lax.axis_index("vir")
    meta = jnp.stack([vir, occ % 2, occ // 2]).astype(jnp.int32)
    sent, live = send_tiles.reshape(-1), pair_count.reshape(-1)
    weights = near_memory(integrals[0])
    prev = near_memory(right_prev)
    tiles = amplitudes.reshape(n_rows, 4, TILE).transpose(1, 0, 2)

    waves = []
    base = 0
    for sizes in WAVES:
        wave = []
        for masks, rows in zip(ORDERS, sizes):
            step = [(masks[0][i], masks[1][i]) for i in range(4)]
            wave.append([masks, step, base, tiles[:, base : base + rows]])
            base += rows
        waves.append(wave)
    total = None
    earlier = [()] * 3
    for wave in waves:
        helds, fars, results = [w[3] for w in wave], [], []
        for i in range(2):
            got = [flip(after(h, *earlier[i]), w[1][i]) for w, h in zip(wave, helds)]
            earlier[i] = got
            helds = [jnp.concatenate(pair) for pair in zip(helds, got)]
        fars = [flip(after(h, *earlier[2]), w[1][2]) for w, h in zip(wave, helds)]
        earlier[2] = fars
        lasts = [
            flip(pack(meta, sent, h, f, w[0]), w[1][3]) for w, h, f in zip(wave, helds, fars)
        ]
        for (masks, _, base, _), h, f, last in zip(wave, helds, fars, lasts):
            blocks = ladder(meta, sent, live, h, f, last, weights, masks)
            moved = [hop(block, dx) for block, dx in zip(blocks, HOPS) if dx]
            moved.append(blocks[3])
            swapped = swap(jnp.stack([block[1] for block in moved]))
            total = add(meta, prev, moved, swapped, total, base, n_rows)
    return total


def solution(mesh):
    in_specs = (P(None, ("vir", "occ")), P("occ", "vir"), P("vir", None, None), P(), P())
    out_specs = P(None, ("vir", "occ"))
    return jax.shard_map(local, mesh=mesh, in_specs=in_specs, out_specs=out_specs, check_vma=False)
```

time: 244 us -> 147 us (0.60)
  waiting for transfers between devices: 113 us -> 37.7 us
  blocking collectives: 54.3 us -> 0 us
  starting transfers between devices: 0.01 us -> 47.7 us
  Pallas kernels: 0 us -> 43.1 us
  matrix products: 22.8 us -> 0 us
  local copies, waits for them, and re-layouts: 27.8 us -> 11.5 us
  between operations: 13.5 us -> 0.73 us
  other arithmetic: 12.2 us -> 5.92 us
    all_gather x1 -> x0, waiting for transfers between devices: 113 us -> none  [local(): gathered = lax.all_gather(amp_tiles, 'vir', axis=1, tiled=True)]
    all_to_all x1 -> x0, blocking collectives: 54.3 us -> none  [local(): lax.all_to_all(ladder, 'occ', split_axis=1, concat_axis=0, tiled=True)]
    ppermute x0 -> x32, starting transfers between devices: none -> 47.7 us  [the longest x16 20.4 us: flip(): return lax.ppermute(array, ('occ', 'vir'), pairs)]
    pallas_call x0 -> x12, Pallas kernels: none -> 43.1 us  [the longest x4 27.4 us: ladder(): pl.pallas_call(functools.partial(ladder_kernel, masks), out_shape=[pltpu....]
    ppermute x0 -> x32, waiting for transfers between devices: none -> 37.7 us  [the longest x16 34.1 us: flip(): return lax.ppermute(array, ('occ', 'vir'), pairs)]
    dot_general x1 -> x0, matrix products: 22.8 us -> none  [local(): jnp.dot(received, integrals[0], preferred_element_type=jnp.float32)]
    select_n x1 -> x0, local copies, waits for them, and re-layouts: 12 us -> none  [local(): jnp.where(live_slots[None, :, None], picked, jnp.zeros_like(picked))]
    gather x1 -> x0, local copies, waits for them, and re-layouts: 11 us -> none  [local(): picked = jnp.take(gathered, columns, axis=1)]
  transfers between devices with their start and end apart: 1 -> 32, of which waited for: 1 -> 10; matrix products, arithmetic and copies ran while one was open for 1% -> 5% of each run, Pallas kernels for 0% -> 28%
where the time goes in v1:
time: 147 us
  starting transfers between devices  47.7 us (32%)
  Pallas kernels  43.1 us (29%)
  waiting for transfers between devices  37.7 us (26%)
  local copies, waits for them, and re-layouts  11.5 us (8%)
  other arithmetic  5.92 us (4%)
    ppermute x16, waiting for transfers between devices, flip(): return lax.ppermute(array, ('occ', 'vir'), pairs)  34.1 us
    pallas_call x4, Pallas kernels, ladder(): pl.pallas_call(functools.partial(ladder_kernel, masks), out_shape=[pltpu....  27.4 us
    ppermute x16, starting transfers between devices, flip(): return lax.ppermute(array, ('occ', 'vir'), pairs)  20.4 us
    ppermute x12, starting transfers between devices, hop(): return lax.ppermute(array, 'occ', pairs)  16.1 us
    ppermute x4, starting transfers between devices, swap(): return lax.ppermute(array, 'occ', [(o, o ^ 1) for o in range(2 * NX)])  11.3 us
    unnamed x40, local copies, waits for them, and re-layouts  10.4 us
    pallas_call x4, Pallas kernels, pack(): pl.pallas_call(functools.partial(pack_kernel, masks), out_shape=pltpu.VME...  7.84 us
    pallas_call x4, Pallas kernels, add(): pl.pallas_call(functools.partial(add_kernel, base, n_rows), out_shape=jax...  7.82 us
  transfers between devices with their start and end apart: 32, of which 10 were waited for; matrix products, arithmetic and copies ran while one was open for 5% of the time, Pallas kernels for 28%

profile of v1, /device:TPU:1, one launch (start us, length us, event | category | flops | bytes accessed | tf_op | source)
XLA Modules:
  0.0 146.7 jit_solution(10145879759678883044)
XLA Ops:
  0.0 1.5 %copy.10 = bf16[1024,512]{0,1:T(8,128)(2,1)S(1)} copy(bf16[1024,512]{1,0:T(8,128)(2,1)} %param.6) | data formatting | bytes 2097152 | tf_op args[1]
  1.5 0.7 copy.11
  2.2 0.1 fusion
  2.3 2.5 %collective-permute-start = (bf16[4,256,128]{2,1,0:T(8,128)(2,1)S(1)}, bf16[4,256,128]{2,1,0:T(8,128)(2,1)S(1)}, u32[]{:S(2)}, u32[]{:S(2)}) collective-permute-start(bf16[4,256,128]{2,1,0:T(8,128)(2,1)S(1)} %get-tuple-element.51), channel_id=1, source_target_pairs={{0,4},{1,5},{2,6},{3,7},{4,0},{5,1},{6,2},{7,3},{8,12},{9,13},{10,... | collective-permute-start | bytes 786440 | tf_op jit(solution)/shard_map/ppermute | solution.py:32
  4.8 2.2 %collective-permute-start.1 = (bf16[4,256,128]{2,1,0:T(8,128)(2,1)S(1)}, bf16[4,256,128]{2,1,0:T(8,128)(2,1)S(1)}, u32[]{:S(2)}, u32[]{:S(2)}) collective-permute-start(bf16[4,256,128]{2,1,0:T(8,128)(2,1)S(1)} %get-tuple-element.50), channel_id=1, source_target_pairs={{0,12},{1,13},{2,14},{3,15},{4,8},{5,9},{6,10},{7,11},{8,4},{9,5},... | collective-permute-start | bytes 786440 | tf_op jit(solution)/shard_map/ppermute | solution.py:32
  7.0 1.8 %collective-permute-done = bf16[4,256,128]{2,1,0:T(8,128)(2,1)S(1)} collective-permute-done((bf16[4,256,128]{2,1,0:T(8,128)(2,1)S(1)}, bf16[4,256,128]{2,1,0:T(8,128)(2,1)S(1)}, u32[]{:S(2)}, u32[]{:S(2)}) %collective-permute-start) | collective-permute-done | bytes 262176 | tf_op jit(solution)/shard_map/ppermute | solution.py:32
  8.9 3.7 %collective-permute-start.3 = (bf16[8,256,128]{2,1,0:T(8,128)(2,1)S(1)}, bf16[8,256,128]{2,1,0:T(8,128)(2,1)S(1)}, u32[]{:S(2)}, u32[]{:S(2)}) collective-permute-start(bf16[8,256,128]{2,1,0:T(8,128)(2,1)S(1)} %pad_maximum_fusion.5), channel_id=1, source_target_pairs={{0,12},{1,13},{2,14},{3,15},{4,8},{5,9},{6,10},{7,11},{8,4},{9,5},... | collective-permute-start | bytes 1572872 | tf_op jit(solution)/shard_map/ppermute | solution.py:32
  12.6 0.1 collective-permute-start.4
  12.7 1.5 collective-permute-start.14
  14.2 5.3 %collective-permute-done.3 = bf16[8,256,128]{2,1,0:T(8,128)(2,1)S(1)} collective-permute-done((bf16[8,256,128]{2,1,0:T(8,128)(2,1)S(1)}, bf16[8,256,128]{2,1,0:T(8,128)(2,1)S(1)}, u32[]{:S(2)}, u32[]{:S(2)}) %collective-permute-start.3) | collective-permute-done | bytes 524320 | tf_op jit(solution)/shard_map/ppermute | solution.py:32
  19.4 0.1 pad_maximum_fusion.1.near
  19.5 1.5 %collective-permute-done.4 = bf16[8,256,128]{2,1,0:T(8,128)(2,1)S(1)} collective-permute-done((bf16[8,256,128]{2,1,0:T(8,128)(2,1)S(1)}, bf16[8,256,128]{2,1,0:T(8,128)(2,1)S(1)}, u32[]{:S(2)}, u32[]{:S(2)}) %collective-permute-start.4) | collective-permute-done | bytes 524320 | tf_op jit(solution)/shard_map/ppermute | solution.py:32
  21.0 0.1 pad_maximum_fusion.2.near
  21.2 2.8 %collective-permute-start.7 = (bf16[16,256,128]{2,1,0:T(8,128)(2,1)S(1)}, bf16[16,256,128]{2,1,0:T(8,128)(2,1)}, u32[]{:S(2)}, u32[]{:S(2)}) collective-permute-start(bf16[16,256,128]{2,1,0:T(8,128)(2,1)S(1)} %pad_maximum_fusion.2.near), channel_id=1, source_target_pairs={{0,3},{1,2},{2,1},{3,0},{4,7},{5,6},{6,5},{7,4},{8,11},{9,10},{10,... | collective-permute-start | bytes 3145736 | tf_op jit(solution)/shard_map/ppermute | solution.py:32
  24.0 1.2 collective-permute-start.2
  25.2 0.9 pad_maximum_fusion.8
  26.1 1.5 %collective-permute-start.15 = (bf16[8,256,128]{2,1,0:T(8,128)(2,1)}, bf16[8,256,128]{2,1,0:T(8,128)(2,1)}, u32[]{:S(2)}, u32[]{:S(2)}) collective-permute-start(bf16[8,256,128]{2,1,0:T(8,128)(2,1)} %pad_maximum_fusion.8), channel_id=1, source_target_pairs={{0,12},{1,13},{2,14},{3,15},{4,8},{5,9},{6,10},{7,11},{8,4},{9,5},... | collective-permute-start | bytes 1572872 | tf_op jit(solution)/shard_map/ppermute | solution.py:32
  27.5 5.9 %collective-permute-done.2 = bf16[4,256,128]{2,1,0:T(8,128)(2,1)S(1)} collective-permute-done((bf16[4,256,128]{2,1,0:T(8,128)(2,1)S(1)}, bf16[4,256,128]{2,1,0:T(8,128)(2,1)S(1)}, u32[]{:S(2)}, u32[]{:S(2)}) %collective-permute-start.2) | collective-permute-done | bytes 262176 | tf_op jit(solution)/shard_map/ppermute | solution.py:32
  33.4 0.9 pad_maximum_fusion.4
  34.4 0.9 copy.9
  35.3 9.4 %collective-permute-done.15 = bf16[8,256,128]{2,1,0:T(8,128)(2,1)} collective-permute-done((bf16[8,256,128]{2,1,0:T(8,128)(2,1)}, bf16[8,256,128]{2,1,0:T(8,128)(2,1)}, u32[]{:S(2)}, u32[]{:S(2)}) %collective-permute-start.15) | collective-permute-done | bytes 524320 | tf_op jit(solution)/shard_map/ppermute | solution.py:32
  44.7 2.3 %pad_maximum_fusion.3.near = bf16[16,256,128]{2,1,0:T(8,128)(2,1)} fusion(bf16[8,256,128]{2,1,0:T(8,128)(2,1)} %collective-permute-done.15, bf16[4,256,128]{2,1,0:T(8,128)(2,1)} %copy-done.12, bf16[4,256,128]{2,1,0:T(8,128)(2,1)} %copy-done.11), kind=kLoop, calls=%fused_computation.3 | loop fusion | flops 1048576 | bytes 2097152 | tf_op jit(solution)/shard_map/concatenate | solution.py:203
  46.9 1.0 copy-done.2
  47.9 1.7 %collective-permute-start.16 = (bf16[16,256,128]{2,1,0:T(8,128)(2,1)}, bf16[16,256,128]{2,1,0:T(8,128)(2,1)}, u32[]{:S(2)}, u32[]{:S(2)}) collective-permute-start(bf16[16,256,128]{2,1,0:T(8,128)(2,1)} %pad_maximum_fusion.3.near), channel_id=1, source_target_pairs={{0,1},{1,0},{2,3},{3,2},{4,5},{5,4},{6,7},{7,6},{8,9},{9,8},{10,11... | collective-permute-start | bytes 3145736 | tf_op jit(solution)/shard_map/ppermute | solution.py:32
  49.6 0.1 pad_add_fusion.meta
  49.7 1.2 pad_maximum_fusion.near
  50.9 0.1 collective-permute-start.8
  51.0 0.1 reshape.9.sent
  51.2 2.3 %pack.6 = bf16[16,256,128]{2,1,0:T(8,128)(2,1)} custom-call(s32[3]{0:T(128)S(1)} %pad_add_fusion.meta, s32[512]{0:T(512)S(1)} %reshape.9.sent, bf16[16,256,128]{2,1,0:T(8,128)(2,1)S(1)} %pad_maximum_fusion.2.near, bf16[16,256,128]{2,1,0:T(8,128)(2,1)} %collective-permute-done.7.far), custom_call_target="tpu_custom_call" | custom-call | bytes 2097152 | tf_op jit(solution)/shard_map/pack/pallas_call | solution.py:75
  53.4 1.2 copy-done.3
  54.7 1.6 %pack.7 = bf16[16,256,128]{2,1,0:T(8,128)(2,1)} custom-call(s32[3]{0:T(128)S(1)} %pad_add_fusion.meta, s32[512]{0:T(512)S(1)} %reshape.9.sent, bf16[16,256,128]{2,1,0:T(8,128)(2,1)S(1)} %pad_maximum_fusion.1.near, bf16[16,256,128]{2,1,0:T(8,128)(2,1)S(1)} %copy-done.3), custom_call_target="tpu_custom_call" | custom-call | bytes 2097152 | tf_op jit(solution)/shard_map/pack/pallas_call | solution.py:75
  56.3 2.6 %collective-permute-start.27 = (bf16[16,256,128]{2,1,0:T(8,128)(2,1)}, bf16[16,256,128]{2,1,0:T(8,128)(2,1)}, u32[]{:S(2)}, u32[]{:S(2)}) collective-permute-start(bf16[16,256,128]{2,1,0:T(8,128)(2,1)} %pack.7), channel_id=1, source_target_pairs={{0,3},{1,2},{2,1},{3,0},{4,7},{5,6},{6,5},{7,4},{8,11},{9,10},{10,... | collective-permute-start | bytes 3145736 | tf_op jit(solution)/shard_map/ppermute | solution.py:32
  58.9 3.5 %collective-permute-done.16.far = bf16[16,256,128]{2,1,0:T(8,128)(2,1)} collective-permute-done((bf16[16,256,128]{2,1,0:T(8,128)(2,1)}, bf16[16,256,128]{2,1,0:T(8,128)(2,1)}, u32[]{:S(2)}, u32[]{:S(2)}) %collective-permute-start.16) | collective-permute-done | bytes 1048608 | tf_op jit(solution)/shard_map/ppermute | solution.py:32
  62.4 2.6 %pack.5 = bf16[16,256,128]{2,1,0:T(8,128)(2,1)} custom-call(s32[3]{0:T(128)S(1)} %pad_add_fusion.meta, s32[512]{0:T(512)S(1)} %reshape.9.sent, bf16[16,256,128]{2,1,0:T(8,128)(2,1)} %pad_maximum_fusion.3.near, bf16[16,256,128]{2,1,0:T(8,128)(2,1)} %collective-permute-done.16.far), custom_call_target="tpu_custom_call" | custom-call | bytes 2097152 | tf_op jit(solution)/shard_map/pack/pallas_call | solution.py:75
  65.1 0.1 reshape.10.live
  65.1 1.1 collective-permute-done.8.far
  66.2 1.3 pack.4
  67.6 0.4 collective-permute-start.9
  68.0 5.7 %collective-permute-done.22.last = bf16[16,256,128]{2,1,0:T(8,128)(2,1)} collective-permute-done((bf16[16,256,128]{2,1,0:T(8,128)(2,1)}, bf16[16,256,128]{2,1,0:T(8,128)(2,1)}, u32[]{:S(2)}, u32[]{:S(2)}) %collective-permute-start.22) | collective-permute-done | bytes 1048608 | tf_op jit(solution)/shard_map/ppermute | solution.py:32
  73.6 5.8 %copy-done = bf16[1,4096,2048]{2,1,0:T(8,128)(2,1)S(1)} copy-done((bf16[1,4096,2048]{2,1,0:T(8,128)(2,1)S(1)}, bf16[1,4096,2048]{2,1,0:T(8,128)(2,1)}, u32[]{:S(2)}) %copy-start) | copy-done | bytes 16777240
  79.4 6.9 %ladder.6 = (bf16[2,256,256]{2,1,0:T(8,128)(2,1)S(1)}, bf16[2,256,256]{2,1,0:T(8,128)(2,1)S(1)}, bf16[2,256,256]{2,1,0:T(8,128)(2,1)S(1)}, bf16[2,256,256]{2,1,0:T(8,128)(2,1)S(1)}) custom-call(s32[3]{0:T(128)S(1)} %pad_add_fusion.meta, s32[512]{0:T(512)S(1)} %reshape.9.sent, s32[256]{0:T(256)S(1)} %reshape.10.live, ...), custom_call_target="tpu_custom_call" | custom-call | flops 4294967296 | bytes 2097152 | tf_op jit(solution)/shard_map/ladder/pallas_call | solution.py:116
  86.4 2.8 %collective-permute-start.23 = (bf16[2,256,256]{2,1,0:T(8,128)(2,1)S(1)}, bf16[2,256,256]{2,1,0:T(8,128)(2,1)S(1)}, u32[]{:S(2)}, u32[]{:S(2)}) collective-permute-start(bf16[2,256,256]{2,1,0:T(8,128)(2,1)S(1)} %get-tuple-element.41), channel_id=1, source_target_pairs={{0,64},{16,80},{32,96},{48,112},{64,0},{80,16},{96,32},{112,48},{1... | collective-permute-start | bytes 786440 | tf_op jit(solution)/shard_map/ppermute | solution.py:37
  89.2 0.3 collective-permute-start.24
  89.5 2.4 %collective-permute-start.25 = (bf16[2,256,256]{2,1,0:T(8,128)(2,1)S(1)}, bf16[2,256,256]{2,1,0:T(8,128)(2,1)S(1)}, u32[]{:S(2)}, u32[]{:S(2)}) collective-permute-start(bf16[2,256,256]{2,1,0:T(8,128)(2,1)S(1)} %get-tuple-element.43), channel_id=1, source_target_pairs={{0,96},{16,112},{32,0},{48,16},{64,32},{80,48},{96,64},{112,80},{1... | collective-permute-start | bytes 786440 | tf_op jit(solution)/shard_map/ppermute | solution.py:37
  91.9 6.7 %ladder.7 = (bf16[2,256,256]{2,1,0:T(8,128)(2,1)S(1)}, bf16[2,256,256]{2,1,0:T(8,128)(2,1)S(1)}, bf16[2,256,256]{2,1,0:T(8,128)(2,1)S(1)}, bf16[2,256,256]{2,1,0:T(8,128)(2,1)S(1)}) custom-call(s32[3]{0:T(128)S(1)} %pad_add_fusion.meta, s32[512]{0:T(512)S(1)} %reshape.9.sent, s32[256]{0:T(256)S(1)} %reshape.10.live, ...), custom_call_target="tpu_custom_call" | custom-call | flops 4294967296 | bytes 2097152 | tf_op jit(solution)/shard_map/ladder/pallas_call | solution.py:116
  98.6 0.1 collective-permute-start.28
  98.7 2.3 %collective-permute-done.24.m1 = bf16[2,256,256]{2,1,0:T(8,128)(2,1)S(1)} collective-permute-done((bf16[2,256,256]{2,1,0:T(8,128)(2,1)S(1)}, bf16[2,256,256]{2,1,0:T(8,128)(2,1)S(1)}, u32[]{:S(2)}, u32[]{:S(2)}) %collective-permute-start.24) | collective-permute-done | bytes 262176 | tf_op jit(solution)/shard_map/ppermute | solution.py:37
  101.1 2.7 %collective-permute-start.30 = (bf16[2,256,256]{2,1,0:T(8,128)(2,1)S(1)}, bf16[2,256,256]{2,1,0:T(8,128)(2,1)S(1)}, u32[]{:S(2)}, u32[]{:S(2)}) collective-permute-start(bf16[2,256,256]{2,1,0:T(8,128)(2,1)S(1)} %get-tuple-element.47), channel_id=1, source_target_pairs={{0,96},{16,112},{32,0},{48,16},{64,32},{80,48},{96,64},{112,80},{1... | collective-permute-start | bytes 786440 | tf_op jit(solution)/shard_map/ppermute | solution.py:37
  103.7 7.3 %ladder.5 = (bf16[2,256,256]{2,1,0:T(8,128)(2,1)S(1)}, bf16[2,256,256]{2,1,0:T(8,128)(2,1)S(1)}, bf16[2,256,256]{2,1,0:T(8,128)(2,1)S(1)}, bf16[2,256,256]{2,1,0:T(8,128)(2,1)S(1)}) custom-call(s32[3]{0:T(128)S(1)} %pad_add_fusion.meta, s32[512]{0:T(512)S(1)} %reshape.9.sent, s32[256]{0:T(256)S(1)} %reshape.10.live, ...), custom_call_target="tpu_custom_call" | custom-call | flops 4294967296 | bytes 2097152 | tf_op jit(solution)/shard_map/ladder/pallas_call | solution.py:116
  111.1 2.1 %collective-permute-start.18 = (bf16[2,256,256]{2,1,0:T(8,128)(2,1)S(1)}, bf16[2,256,256]{2,1,0:T(8,128)(2,1)S(1)}, u32[]{:S(2)}, u32[]{:S(2)}) collective-permute-start(bf16[2,256,256]{2,1,0:T(8,128)(2,1)S(1)} %get-tuple-element.37), channel_id=1, source_target_pairs={{0,64},{16,80},{32,96},{48,112},{64,0},{80,16},{96,32},{112,48},{1... | collective-permute-start | bytes 786440 | tf_op jit(solution)/shard_map/ppermute | solution.py:37
  113.2 2.9 %collective-permute-start.20 = (bf16[2,256,256]{2,1,0:T(8,128)(2,1)S(1)}, bf16[2,256,256]{2,1,0:T(8,128)(2,1)S(1)}, u32[]{:S(2)}, u32[]{:S(2)}) collective-permute-start(bf16[2,256,256]{2,1,0:T(8,128)(2,1)S(1)} %get-tuple-element.39), channel_id=1, source_target_pairs={{0,96},{16,112},{32,0},{48,16},{64,32},{80,48},{96,64},{112,80},{1... | collective-permute-start | bytes 786440 | tf_op jit(solution)/shard_map/ppermute | solution.py:37
  116.2 6.5 %ladder.4 = (bf16[2,256,256]{2,1,0:T(8,128)(2,1)S(1)}, bf16[2,256,256]{2,1,0:T(8,128)(2,1)S(1)}, bf16[2,256,256]{2,1,0:T(8,128)(2,1)S(1)}, bf16[2,256,256]{2,1,0:T(8,128)(2,1)S(1)}) custom-call(s32[3]{0:T(128)S(1)} %pad_add_fusion.meta, s32[512]{0:T(512)S(1)} %reshape.9.sent, s32[256]{0:T(256)S(1)} %reshape.10.live, ...), custom_call_target="tpu_custom_call" | custom-call | flops 4294967296 | bytes 2097152 | tf_op jit(solution)/shard_map/ladder/pallas_call | solution.py:116
  122.7 0.1 collective-permute-start.10
  122.8 0.6 collective-permute-start.11
  123.4 2.1 %collective-permute-start.12 = (bf16[2,256,256]{2,1,0:T(8,128)(2,1)S(1)}, bf16[2,256,256]{2,1,0:T(8,128)(2,1)S(1)}, u32[]{:S(2)}, u32[]{:S(2)}) collective-permute-start(bf16[2,256,256]{2,1,0:T(8,128)(2,1)S(1)} %get-tuple-element.32), channel_id=1, source_target_pairs={{0,96},{16,112},{32,0},{48,16},{64,32},{80,48},{96,64},{112,80},{1... | collective-permute-start | bytes 786440 | tf_op jit(solution)/shard_map/ppermute | solution.py:37
  125.9 4.2 %collective-permute-start.26 = (bf16[4,256,256]{2,1,0:T(8,128)(2,1)S(1)}, bf16[4,256,256]{2,1,0:T(8,128)(2,1)S(1)}, u32[]{:S(2)}, u32[]{:S(2)}) collective-permute-start(bf16[4,256,256]{2,1,0:T(8,128)(2,1)S(1)} %pad_maximum_fusion.10), channel_id=1, source_target_pairs={{0,16},{16,0},{32,48},{48,32},{64,80},{80,64},{96,112},{112,96},{1... | collective-permute-start | bytes 1572872 | tf_op jit(solution)/shard_map/ppermute | solution.py:41
  130.0 0.1 collective-permute-start.31
  130.3 5.6 %collective-permute-start.21 = (bf16[4,256,256]{2,1,0:T(8,128)(2,1)S(1)}, bf16[4,256,256]{2,1,0:T(8,128)(2,1)S(1)}, u32[]{:S(2)}, u32[]{:S(2)}) collective-permute-start(bf16[4,256,256]{2,1,0:T(8,128)(2,1)S(1)} %pad_maximum_fusion.9), channel_id=1, source_target_pairs={{0,16},{16,0},{32,48},{48,32},{64,80},{80,64},{96,112},{112,96},{1... | collective-permute-start | bytes 1572872 | tf_op jit(solution)/shard_map/ppermute | solution.py:41
  135.9 1.2 collective-permute-done.11.m1
  137.3 1.4 collective-permute-start.13
  138.6 2.0 %residual.4.refs_0_ = f32[8192,256]{1,0:T(8,128)} custom-call(s32[3]{0:T(128)S(1)} %pad_add_fusion.meta, bf16[8192,256]{1,0:T(8,128)(2,1)S(1)} %copy-done.1, bf16[2,256,256]{2,1,0:T(8,128)(2,1)S(1)} %collective-permute-done.28.m0, bf16[2,256,256]{2,1,0:T(8,128)(2,1)S(1)} %collective-permute-done.29.m1, bf16[2,256,256]{2,1,0:T(8,128)(2,1)S(1)} %collective-permute-done.30.m2, ...), custom_call_target="tpu_custom_call" | custom-call | flops 524288 | bytes 2097152 | tf_op jit(solution)/shard_map/residual/pallas_call | solution.py:160
  140.6 2.0 %residual.5.refs_0_ = f32[8192,256]{1,0:T(8,128)} custom-call(s32[3]{0:T(128)S(1)} %pad_add_fusion.meta, bf16[8192,256]{1,0:T(8,128)(2,1)S(1)} %copy-done.1, bf16[2,256,256]{2,1,0:T(8,128)(2,1)S(1)} %copy-done.6, bf16[2,256,256]{2,1,0:T(8,128)(2,1)S(1)} %copy-done.8, bf16[2,256,256]{2,1,0:T(8,128)(2,1)S(1)} %copy-done.10, ...), custom_call_target="tpu_custom_call", output_to_operand_aliasing={{}: (7, {})} | custom-call | flops 524288 | bytes 2097152 | tf_op jit(solution)/shard_map/residual/pallas_call | solution.py:160
  142.6 2.0 %residual.6.refs_0_ = f32[8192,256]{1,0:T(8,128)} custom-call(s32[3]{0:T(128)S(1)} %pad_add_fusion.meta, bf16[8192,256]{1,0:T(8,128)(2,1)S(1)} %copy-done.1, bf16[2,256,256]{2,1,0:T(8,128)(2,1)S(1)} %collective-permute-done.18.m0, bf16[2,256,256]{2,1,0:T(8,128)(2,1)S(1)} %collective-permute-done.19.m1, ...), custom_call_target="tpu_custom_call", output_to_operand_aliasing={{}: (7, {})} | custom-call | flops 524288 | bytes 2097152 | tf_op jit(solution)/shard_map/residual/pallas_call | solution.py:160
  144.6 2.0 %residual.7 = f32[8192,256]{1,0:T(8,128)} custom-call(s32[3]{0:T(128)S(1)} %pad_add_fusion.meta, bf16[8192,256]{1,0:T(8,128)(2,1)S(1)} %copy-done.1, bf16[2,256,256]{2,1,0:T(8,128)(2,1)S(1)} %collective-permute-done.10.m0, bf16[2,256,256]{2,1,0:T(8,128)(2,1)S(1)} %collective-permute-done.11.m1, ...), custom_call_target="tpu_custom_call", output_to_operand_aliasing={{}: (7, {})} | custom-call | flops 524288 | bytes 2097152 | tf_op jit(solution)/shard_map/residual/pallas_call | solution.py:160
  (89 shorter events, 0.7 us)
Async XLA Ops:
  2.2 31.2 %copy-start.11 = (bf16[4,256,128]{2,1,0:T(8,128)(2,1)}, bf16[4,256,128]{2,1,0:T(8,128)(2,1)S(1)}, u32[]{:S(2)}) copy-start(bf16[4,256,128]{2,1,0:T(8,128)(2,1)S(1)} %get-tuple-element.34) | copy-start | bytes 786436
  2.3 6.6 %collective-permute-start = (bf16[4,256,128]{2,1,0:T(8,128)(2,1)S(1)}, bf16[4,256,128]{2,1,0:T(8,128)(2,1)S(1)}, u32[]{:S(2)}, u32[]{:S(2)}) collective-permute-start(bf16[4,256,128]{2,1,0:T(8,128)(2,1)S(1)} %get-tuple-element.51), channel_id=1, source_target_pairs={{0,4},{1,5},{2,6},{3,7},{4,0},{5,1},{6,2},{7,3},{8,12},{9,13},{10,... | collective-permute-start | bytes 786440 | tf_op jit(solution)/shard_map/ppermute | solution.py:32
  4.8 7.8 %collective-permute-start.1 = (bf16[4,256,128]{2,1,0:T(8,128)(2,1)S(1)}, bf16[4,256,128]{2,1,0:T(8,128)(2,1)S(1)}, u32[]{:S(2)}, u32[]{:S(2)}) collective-permute-start(bf16[4,256,128]{2,1,0:T(8,128)(2,1)S(1)} %get-tuple-element.50), channel_id=1, source_target_pairs={{0,12},{1,13},{2,14},{3,15},{4,8},{5,9},{6,10},{7,11},{8,4},{9,5},... | collective-permute-start | bytes 786440 | tf_op jit(solution)/shard_map/ppermute | solution.py:32
  8.9 10.5 %collective-permute-start.3 = (bf16[8,256,128]{2,1,0:T(8,128)(2,1)S(1)}, bf16[8,256,128]{2,1,0:T(8,128)(2,1)S(1)}, u32[]{:S(2)}, u32[]{:S(2)}) collective-permute-start(bf16[8,256,128]{2,1,0:T(8,128)(2,1)S(1)} %pad_maximum_fusion.5), channel_id=1, source_target_pairs={{0,12},{1,13},{2,14},{3,15},{4,8},{5,9},{6,10},{7,11},{8,4},{9,5},... | collective-permute-start | bytes 1572872 | tf_op jit(solution)/shard_map/ppermute | solution.py:32
  12.6 8.4 %collective-permute-start.4 = (bf16[8,256,128]{2,1,0:T(8,128)(2,1)S(1)}, bf16[8,256,128]{2,1,0:T(8,128)(2,1)S(1)}, u32[]{:S(2)}, u32[]{:S(2)}) collective-permute-start(bf16[8,256,128]{2,1,0:T(8,128)(2,1)S(1)} %pad_maximum_fusion.6), channel_id=1, source_target_pairs={{0,4},{1,5},{2,6},{3,7},{4,0},{5,1},{6,2},{7,3},{8,12},{9,13},{10,... | collective-permute-start | bytes 1572872 | tf_op jit(solution)/shard_map/ppermute | solution.py:32
  12.7 12.5 %collective-permute-start.14 = (bf16[4,256,128]{2,1,0:T(8,128)(2,1)S(1)}, bf16[4,256,128]{2,1,0:T(8,128)(2,1)S(1)}, u32[]{:S(2)}, u32[]{:S(2)}) collective-permute-start(bf16[4,256,128]{2,1,0:T(8,128)(2,1)S(1)} %get-tuple-element.34), channel_id=1, source_target_pairs={{0,4},{1,5},{2,6},{3,7},{4,0},{5,1},{6,2},{7,3},{8,12},{9,13},{10,... | collective-permute-start | bytes 786440 | tf_op jit(solution)/shard_map/ppermute | solution.py:32
  21.1 43.9 %copy-start.14 = (s32[16,16]{1,0:T(8,128)S(1)}, s32[16,16]{1,0:T(8,128)}, u32[]{:S(2)}) copy-start(s32[16,16]{1,0:T(8,128)} %param.9) | copy-start | bytes 3076
  21.2 25.8 %collective-permute-start.7 = (bf16[16,256,128]{2,1,0:T(8,128)(2,1)S(1)}, bf16[16,256,128]{2,1,0:T(8,128)(2,1)}, u32[]{:S(2)}, u32[]{:S(2)}) collective-permute-start(bf16[16,256,128]{2,1,0:T(8,128)(2,1)S(1)} %pad_maximum_fusion.2.near), channel_id=1, source_target_pairs={{0,3},{1,2},{2,1},{3,0},{4,7},{5,6},{6,5},{7,4},{8,11},{9,10},{10,... | collective-permute-start | bytes 3145736 | tf_op jit(solution)/shard_map/ppermute | solution.py:32
  24.0 23.0 %collective-permute-start.6 = (bf16[16,256,128]{2,1,0:T(8,128)(2,1)S(1)}, bf16[16,256,128]{2,1,0:T(8,128)(2,1)S(1)}, u32[]{:S(2)}, u32[]{:S(2)}) collective-permute-start(bf16[16,256,128]{2,1,0:T(8,128)(2,1)S(1)} %pad_maximum_fusion.1.near), channel_id=1, source_target_pairs={{0,1},{1,0},{2,3},{3,2},{4,5},{5,4},{6,7},{7,6},{8,9},{9,8},{10,11... | collective-permute-start | bytes 3145736 | tf_op jit(solution)/shard_map/ppermute | solution.py:32
  24.0 9.5 %collective-permute-start.2 = (bf16[4,256,128]{2,1,0:T(8,128)(2,1)S(1)}, bf16[4,256,128]{2,1,0:T(8,128)(2,1)S(1)}, u32[]{:S(2)}, u32[]{:S(2)}) collective-permute-start(bf16[4,256,128]{2,1,0:T(8,128)(2,1)S(1)} %get-tuple-element.27), channel_id=1, source_target_pairs={{0,12},{1,13},{2,14},{3,15},{4,8},{5,9},{6,10},{7,11},{8,4},{9,5},... | collective-permute-start | bytes 786440 | tf_op jit(solution)/shard_map/ppermute | solution.py:32
  25.2 9.2 %copy-start.12 = (bf16[4,256,128]{2,1,0:T(8,128)(2,1)}, bf16[4,256,128]{2,1,0:T(8,128)(2,1)S(1)}, u32[]{:S(2)}) copy-start(bf16[4,256,128]{2,1,0:T(8,128)(2,1)S(1)} %collective-permute-done.14) | copy-start | bytes 786436
  26.1 18.6 %collective-permute-start.15 = (bf16[8,256,128]{2,1,0:T(8,128)(2,1)}, bf16[8,256,128]{2,1,0:T(8,128)(2,1)}, u32[]{:S(2)}, u32[]{:S(2)}) collective-permute-start(bf16[8,256,128]{2,1,0:T(8,128)(2,1)} %pad_maximum_fusion.8), channel_id=1, source_target_pairs={{0,12},{1,13},{2,14},{3,15},{4,8},{5,9},{6,10},{7,11},{8,4},{9,5},... | collective-permute-start | bytes 1572872 | tf_op jit(solution)/shard_map/ppermute | solution.py:32
  33.4 0.9 copy-start.13
  34.4 15.3 %collective-permute-start.5 = (bf16[8,256,128]{2,1,0:T(8,128)(2,1)}, bf16[8,256,128]{2,1,0:T(8,128)(2,1)}, u32[]{:S(2)}, u32[]{:S(2)}) collective-permute-start(bf16[8,256,128]{2,1,0:T(8,128)(2,1)} %pad_maximum_fusion.4), channel_id=1, source_target_pairs={{0,4},{1,5},{2,6},{3,7},{4,0},{5,1},{6,2},{7,3},{8,12},{9,13},{10,... | collective-permute-start | bytes 1572872 | tf_op jit(solution)/shard_map/ppermute | solution.py:32
  46.9 1.0 copy-start.2
  47.9 14.5 %collective-permute-start.16 = (bf16[16,256,128]{2,1,0:T(8,128)(2,1)}, bf16[16,256,128]{2,1,0:T(8,128)(2,1)}, u32[]{:S(2)}, u32[]{:S(2)}) collective-permute-start(bf16[16,256,128]{2,1,0:T(8,128)(2,1)} %pad_maximum_fusion.3.near), channel_id=1, source_target_pairs={{0,1},{1,0},{2,3},{3,2},{4,5},{5,4},{6,7},{7,6},{8,9},{9,8},{10,11... | collective-permute-start | bytes 3145736 | tf_op jit(solution)/shard_map/ppermute | solution.py:32
  50.9 15.3 %collective-permute-start.8 = (bf16[16,256,128]{2,1,0:T(8,128)(2,1)S(1)}, bf16[16,256,128]{2,1,0:T(8,128)(2,1)}, u32[]{:S(2)}, u32[]{:S(2)}) collective-permute-start(bf16[16,256,128]{2,1,0:T(8,128)(2,1)S(1)} %pad_maximum_fusion.near), channel_id=1, source_target_pairs={{0,3},{1,2},{2,1},{3,0},{4,7},{5,6},{6,5},{7,4},{8,11},{9,10},{10,... | collective-permute-start | bytes 3145736 | tf_op jit(solution)/shard_map/ppermute | solution.py:32
  53.4 20.2 %collective-permute-start.22 = (bf16[16,256,128]{2,1,0:T(8,128)(2,1)}, bf16[16,256,128]{2,1,0:T(8,128)(2,1)}, u32[]{:S(2)}, u32[]{:S(2)}) collective-permute-start(bf16[16,256,128]{2,1,0:T(8,128)(2,1)} %pack.6), channel_id=1, source_target_pairs={{0,1},{1,0},{2,3},{3,2},{4,5},{5,4},{6,7},{7,6},{8,9},{9,8},{10,11... | collective-permute-start | bytes 3145736 | tf_op jit(solution)/shard_map/ppermute | solution.py:32
  53.4 1.2 copy-start.3
  56.3 33.2 %collective-permute-start.27 = (bf16[16,256,128]{2,1,0:T(8,128)(2,1)}, bf16[16,256,128]{2,1,0:T(8,128)(2,1)}, u32[]{:S(2)}, u32[]{:S(2)}) collective-permute-start(bf16[16,256,128]{2,1,0:T(8,128)(2,1)} %pack.7), channel_id=1, source_target_pairs={{0,3},{1,2},{2,1},{3,0},{4,7},{5,6},{6,5},{7,4},{8,11},{9,10},{10,... | collective-permute-start | bytes 3145736 | tf_op jit(solution)/shard_map/ppermute | solution.py:32
  65.0 38.7 %collective-permute-start.17 = (bf16[16,256,128]{2,1,0:T(8,128)(2,1)}, bf16[16,256,128]{2,1,0:T(8,128)(2,1)}, u32[]{:S(2)}, u32[]{:S(2)}) collective-permute-start(bf16[16,256,128]{2,1,0:T(8,128)(2,1)} %pack.5), channel_id=1, source_target_pairs={{0,3},{1,2},{2,1},{3,0},{4,7},{5,6},{6,5},{7,4},{8,11},{9,10},{10,... | collective-permute-start | bytes 3145736 | tf_op jit(solution)/shard_map/ppermute | solution.py:32
  67.6 45.6 %collective-permute-start.9 = (bf16[16,256,128]{2,1,0:T(8,128)(2,1)S(1)}, bf16[16,256,128]{2,1,0:T(8,128)(2,1)S(1)}, u32[]{:S(2)}, u32[]{:S(2)}) collective-permute-start(bf16[16,256,128]{2,1,0:T(8,128)(2,1)S(1)} %pack.4), channel_id=1, source_target_pairs={{0,1},{1,0},{2,3},{3,2},{4,5},{5,4},{6,7},{7,6},{8,9},{9,8},{10,11... | collective-permute-start | bytes 3145736 | tf_op jit(solution)/shard_map/ppermute | solution.py:32
  73.6 5.8 %copy-start = (bf16[1,4096,2048]{2,1,0:T(8,128)(2,1)S(1)}, bf16[1,4096,2048]{2,1,0:T(8,128)(2,1)}, u32[]{:S(2)}) copy-start(bf16[1,4096,2048]{2,1,0:T(8,128)(2,1)} %param.7) | copy-start | bytes 50331652
  79.4 12.5 %copy-start.4 = (bf16[16,256,128]{2,1,0:T(8,128)(2,1)S(1)}, bf16[16,256,128]{2,1,0:T(8,128)(2,1)}, u32[]{:S(2)}) copy-start(bf16[16,256,128]{2,1,0:T(8,128)(2,1)} %copy-done.2) | copy-start | bytes 3145732
  86.4 12.2 %collective-permute-start.23 = (bf16[2,256,256]{2,1,0:T(8,128)(2,1)S(1)}, bf16[2,256,256]{2,1,0:T(8,128)(2,1)S(1)}, u32[]{:S(2)}, u32[]{:S(2)}) collective-permute-start(bf16[2,256,256]{2,1,0:T(8,128)(2,1)S(1)} %get-tuple-element.41), channel_id=1, source_target_pairs={{0,64},{16,80},{32,96},{48,112},{64,0},{80,16},{96,32},{112,48},{1... | collective-permute-start | bytes 786440 | tf_op jit(solution)/shard_map/ppermute | solution.py:37
  89.2 11.9 %collective-permute-start.24 = (bf16[2,256,256]{2,1,0:T(8,128)(2,1)S(1)}, bf16[2,256,256]{2,1,0:T(8,128)(2,1)S(1)}, u32[]{:S(2)}, u32[]{:S(2)}) collective-permute-start(bf16[2,256,256]{2,1,0:T(8,128)(2,1)S(1)} %get-tuple-element.42), channel_id=1, source_target_pairs={{0,32},{16,48},{32,64},{48,80},{64,96},{80,112},{96,0},{112,16},{1... | collective-permute-start | bytes 786440 | tf_op jit(solution)/shard_map/ppermute | solution.py:37
  89.5 11.5 %collective-permute-start.25 = (bf16[2,256,256]{2,1,0:T(8,128)(2,1)S(1)}, bf16[2,256,256]{2,1,0:T(8,128)(2,1)S(1)}, u32[]{:S(2)}, u32[]{:S(2)}) collective-permute-start(bf16[2,256,256]{2,1,0:T(8,128)(2,1)S(1)} %get-tuple-element.43), channel_id=1, source_target_pairs={{0,96},{16,112},{32,0},{48,16},{64,32},{80,48},{96,64},{112,80},{1... | collective-permute-start | bytes 786440 | tf_op jit(solution)/shard_map/ppermute | solution.py:37
  91.9 24.3 %slice-start = ((s8[16777216]{0:T(1024)(128)(4,1)}), s8[4194304]{0:T(1024)(128)(4,1)S(1)}, s32[]{:S(2)}) async-start(s8[16777216]{0:T(1024)(128)(4,1)} %bitcast.9), calls=%async_computation | async-start | bytes 8388608
  91.9 24.3 %slice-start.1 = ((s8[16777216]{0:T(1024)(128)(4,1)}), s8[4194304]{0:T(1024)(128)(4,1)S(1)}, s32[]{:S(2)}) async-start(s8[16777216]{0:T(1024)(128)(4,1)} %bitcast.9), calls=%async_computation.1 | async-start | bytes 8388608
  98.6 12.5 %copy-start.5 = (bf16[2,256,256]{2,1,0:T(8,128)(2,1)}, bf16[2,256,256]{2,1,0:T(8,128)(2,1)S(1)}, u32[]{:S(2)}) copy-start(bf16[2,256,256]{2,1,0:T(8,128)(2,1)S(1)} %collective-permute-done.23.m0) | copy-start | bytes 786436
  98.6 14.5 %collective-permute-start.28 = (bf16[2,256,256]{2,1,0:T(8,128)(2,1)S(1)}, bf16[2,256,256]{2,1,0:T(8,128)(2,1)S(1)}, u32[]{:S(2)}, u32[]{:S(2)}) collective-permute-start(bf16[2,256,256]{2,1,0:T(8,128)(2,1)S(1)} %get-tuple-element.45), channel_id=1, source_target_pairs={{0,64},{16,80},{32,96},{48,112},{64,0},{80,16},{96,32},{112,48},{1... | collective-permute-start | bytes 786440 | tf_op jit(solution)/shard_map/ppermute | solution.py:37
  101.0 10.0 %copy-start.7 = (bf16[2,256,256]{2,1,0:T(8,128)(2,1)}, bf16[2,256,256]{2,1,0:T(8,128)(2,1)S(1)}, u32[]{:S(2)}) copy-start(bf16[2,256,256]{2,1,0:T(8,128)(2,1)S(1)} %collective-permute-done.24.m1) | copy-start | bytes 786436
  101.0 15.1 %slice-start.2 = ((s8[16777216]{0:T(1024)(128)(4,1)}), s8[4194304]{0:T(1024)(128)(4,1)S(1)}, s32[]{:S(2)}) async-start(s8[16777216]{0:T(1024)(128)(4,1)} %bitcast.9), calls=%async_computation.2 | async-start | bytes 8388608
  101.0 21.7 %collective-permute-start.29 = (bf16[2,256,256]{2,1,0:T(8,128)(2,1)S(1)}, bf16[2,256,256]{2,1,0:T(8,128)(2,1)S(1)}, u32[]{:S(2)}, u32[]{:S(2)}) collective-permute-start(bf16[2,256,256]{2,1,0:T(8,128)(2,1)S(1)} %get-tuple-element.46), channel_id=1, source_target_pairs={{0,32},{16,48},{32,64},{48,80},{64,96},{80,112},{96,0},{112,16},{1... | collective-permute-start | bytes 786440 | tf_op jit(solution)/shard_map/ppermute | solution.py:37
  101.1 10.0 %copy-start.9 = (bf16[2,256,256]{2,1,0:T(8,128)(2,1)}, bf16[2,256,256]{2,1,0:T(8,128)(2,1)S(1)}, u32[]{:S(2)}) copy-start(bf16[2,256,256]{2,1,0:T(8,128)(2,1)S(1)} %collective-permute-done.25.m2) | copy-start | bytes 786436
  101.1 21.7 %collective-permute-start.30 = (bf16[2,256,256]{2,1,0:T(8,128)(2,1)S(1)}, bf16[2,256,256]{2,1,0:T(8,128)(2,1)S(1)}, u32[]{:S(2)}, u32[]{:S(2)}) collective-permute-start(bf16[2,256,256]{2,1,0:T(8,128)(2,1)S(1)} %get-tuple-element.47), channel_id=1, source_target_pairs={{0,96},{16,112},{32,0},{48,16},{64,32},{80,48},{96,64},{112,80},{1... | collective-permute-start | bytes 786440 | tf_op jit(solution)/shard_map/ppermute | solution.py:37
  103.7 12.4 %slice-start.3 = ((s8[16777216]{0:T(1024)(128)(4,1)}), s8[4194304]{0:T(1024)(128)(4,1)S(1)}, s32[]{:S(2)}) async-start(s8[16777216]{0:T(1024)(128)(4,1)} %bitcast.9), calls=%async_computation.3 | async-start | bytes 8388608
  111.1 12.4 %collective-permute-start.18 = (bf16[2,256,256]{2,1,0:T(8,128)(2,1)S(1)}, bf16[2,256,256]{2,1,0:T(8,128)(2,1)S(1)}, u32[]{:S(2)}, u32[]{:S(2)}) collective-permute-start(bf16[2,256,256]{2,1,0:T(8,128)(2,1)S(1)} %get-tuple-element.37), channel_id=1, source_target_pairs={{0,64},{16,80},{32,96},{48,112},{64,0},{80,16},{96,32},{112,48},{1... | collective-permute-start | bytes 786440 | tf_op jit(solution)/shard_map/ppermute | solution.py:37
  113.1 12.7 %collective-permute-start.19 = (bf16[2,256,256]{2,1,0:T(8,128)(2,1)S(1)}, bf16[2,256,256]{2,1,0:T(8,128)(2,1)S(1)}, u32[]{:S(2)}, u32[]{:S(2)}) collective-permute-start(bf16[2,256,256]{2,1,0:T(8,128)(2,1)S(1)} %get-tuple-element.38), channel_id=1, source_target_pairs={{0,32},{16,48},{32,64},{48,80},{64,96},{80,112},{96,0},{112,16},{1... | collective-permute-start | bytes 786440 | tf_op jit(solution)/shard_map/ppermute | solution.py:37
  113.2 12.4 %slice-start.4 = ((bf16[2,256,256]{2,1,0:T(8,128)(2,1)}), bf16[1,256,256]{2,1,0:T(8,128)(2,1)S(1)}, s32[]{:S(2)}) async-start(bf16[2,256,256]{2,1,0:T(8,128)(2,1)} %copy-done.5), calls=%async_computation.4 | async-start | bytes 262144 | tf_op jit(solution)/shard_map/slice | solution.py:213
  113.2 12.4 %slice-start.5 = ((bf16[2,256,256]{2,1,0:T(8,128)(2,1)}), bf16[1,256,256]{2,1,0:T(8,128)(2,1)S(1)}, s32[]{:S(2)}) async-start(bf16[2,256,256]{2,1,0:T(8,128)(2,1)} %copy-done.7), calls=%async_computation.5 | async-start | bytes 262144 | tf_op jit(solution)/shard_map/slice | solution.py:213
  113.2 12.4 %slice-start.6 = ((bf16[2,256,256]{2,1,0:T(8,128)(2,1)}), bf16[1,256,256]{2,1,0:T(8,128)(2,1)S(1)}, s32[]{:S(2)}) async-start(bf16[2,256,256]{2,1,0:T(8,128)(2,1)} %copy-done.9), calls=%async_computation.6 | async-start | bytes 262144 | tf_op jit(solution)/shard_map/slice | solution.py:213
  113.2 16.8 %collective-permute-start.20 = (bf16[2,256,256]{2,1,0:T(8,128)(2,1)S(1)}, bf16[2,256,256]{2,1,0:T(8,128)(2,1)S(1)}, u32[]{:S(2)}, u32[]{:S(2)}) collective-permute-start(bf16[2,256,256]{2,1,0:T(8,128)(2,1)S(1)} %get-tuple-element.39), channel_id=1, source_target_pairs={{0,96},{16,112},{32,0},{48,16},{64,32},{80,48},{96,64},{112,80},{1... | collective-permute-start | bytes 786440 | tf_op jit(solution)/shard_map/ppermute | solution.py:37
  122.7 16.0 %copy-start.1 = (bf16[8192,256]{1,0:T(8,128)(2,1)S(1)}, bf16[8192,256]{1,0:T(8,128)(2,1)}, u32[]{:S(2)}) copy-start(bf16[8192,256]{1,0:T(8,128)(2,1)} %prev.7) | copy-start | bytes 12582916
  122.7 7.5 %collective-permute-start.10 = (bf16[2,256,256]{2,1,0:T(8,128)(2,1)S(1)}, bf16[2,256,256]{2,1,0:T(8,128)(2,1)S(1)}, u32[]{:S(2)}, u32[]{:S(2)}) collective-permute-start(bf16[2,256,256]{2,1,0:T(8,128)(2,1)S(1)} %get-tuple-element.30), channel_id=1, source_target_pairs={{0,64},{16,80},{32,96},{48,112},{64,0},{80,16},{96,32},{112,48},{1... | collective-permute-start | bytes 786440 | tf_op jit(solution)/shard_map/ppermute | solution.py:37
  122.8 14.3 %collective-permute-start.11 = (bf16[2,256,256]{2,1,0:T(8,128)(2,1)S(1)}, bf16[2,256,256]{2,1,0:T(8,128)(2,1)S(1)}, u32[]{:S(2)}, u32[]{:S(2)}) collective-permute-start(bf16[2,256,256]{2,1,0:T(8,128)(2,1)S(1)} %get-tuple-element.31), channel_id=1, source_target_pairs={{0,32},{16,48},{32,64},{48,80},{64,96},{80,112},{96,0},{112,16},{1... | collective-permute-start | bytes 786440 | tf_op jit(solution)/shard_map/ppermute | solution.py:37
  123.4 13.7 %collective-permute-start.12 = (bf16[2,256,256]{2,1,0:T(8,128)(2,1)S(1)}, bf16[2,256,256]{2,1,0:T(8,128)(2,1)S(1)}, u32[]{:S(2)}, u32[]{:S(2)}) collective-permute-start(bf16[2,256,256]{2,1,0:T(8,128)(2,1)S(1)} %get-tuple-element.32), channel_id=1, source_target_pairs={{0,96},{16,112},{32,0},{48,16},{64,32},{80,48},{96,64},{112,80},{1... | collective-permute-start | bytes 786440 | tf_op jit(solution)/shard_map/ppermute | solution.py:37
  125.9 14.8 %collective-permute-start.26 = (bf16[4,256,256]{2,1,0:T(8,128)(2,1)S(1)}, bf16[4,256,256]{2,1,0:T(8,128)(2,1)S(1)}, u32[]{:S(2)}, u32[]{:S(2)}) collective-permute-start(bf16[4,256,256]{2,1,0:T(8,128)(2,1)S(1)} %pad_maximum_fusion.10), channel_id=1, source_target_pairs={{0,16},{16,0},{32,48},{48,32},{64,80},{80,64},{96,112},{112,96},{1... | collective-permute-start | bytes 1572872 | tf_op jit(solution)/shard_map/ppermute | solution.py:41
  130.0 8.6 %collective-permute-start.31 = (bf16[4,256,256]{2,1,0:T(8,128)(2,1)S(1)}, bf16[4,256,256]{2,1,0:T(8,128)(2,1)S(1)}, u32[]{:S(2)}, u32[]{:S(2)}) collective-permute-start(bf16[4,256,256]{2,1,0:T(8,128)(2,1)S(1)} %pad_maximum_fusion.11), channel_id=1, source_target_pairs={{0,16},{16,0},{32,48},{48,32},{64,80},{80,64},{96,112},{112,96},{1... | collective-permute-start | bytes 1572872 | tf_op jit(solution)/shard_map/ppermute | solution.py:41
  130.1 10.5 %copy-start.6 = (bf16[2,256,256]{2,1,0:T(8,128)(2,1)S(1)}, bf16[2,256,256]{2,1,0:T(8,128)(2,1)}, u32[]{:S(2)}) copy-start(bf16[2,256,256]{2,1,0:T(8,128)(2,1)} %copy-done.5) | copy-start | bytes 786436
  130.2 10.5 %copy-start.8 = (bf16[2,256,256]{2,1,0:T(8,128)(2,1)S(1)}, bf16[2,256,256]{2,1,0:T(8,128)(2,1)}, u32[]{:S(2)}) copy-start(bf16[2,256,256]{2,1,0:T(8,128)(2,1)} %copy-done.7) | copy-start | bytes 786436
  130.2 10.5 %copy-start.10 = (bf16[2,256,256]{2,1,0:T(8,128)(2,1)S(1)}, bf16[2,256,256]{2,1,0:T(8,128)(2,1)}, u32[]{:S(2)}) copy-start(bf16[2,256,256]{2,1,0:T(8,128)(2,1)} %copy-done.9) | copy-start | bytes 786436
  130.3 12.4 %collective-permute-start.21 = (bf16[4,256,256]{2,1,0:T(8,128)(2,1)S(1)}, bf16[4,256,256]{2,1,0:T(8,128)(2,1)S(1)}, u32[]{:S(2)}, u32[]{:S(2)}) collective-permute-start(bf16[4,256,256]{2,1,0:T(8,128)(2,1)S(1)} %pad_maximum_fusion.9), channel_id=1, source_target_pairs={{0,16},{16,0},{32,48},{48,32},{64,80},{80,64},{96,112},{112,96},{1... | collective-permute-start | bytes 1572872 | tf_op jit(solution)/shard_map/ppermute | solution.py:41
  137.3 7.3 %collective-permute-start.13 = (bf16[4,256,256]{2,1,0:T(8,128)(2,1)S(1)}, bf16[4,256,256]{2,1,0:T(8,128)(2,1)S(1)}, u32[]{:S(2)}, u32[]{:S(2)}) collective-permute-start(bf16[4,256,256]{2,1,0:T(8,128)(2,1)S(1)} %pad_maximum_fusion.7), channel_id=1, source_target_pairs={{0,16},{16,0},{32,48},{48,32},{64,80},{80,64},{96,112},{112,96},{1... | collective-permute-start | bytes 1572872 | tf_op jit(solution)/shard_map/ppermute | solution.py:41

commit v2 on v0

v2 whole, which is shorter than its diff:
```python
import functools

import jax
import jax.numpy as jnp
from jax import lax
from jax.experimental import pallas as pl
from jax.experimental.pallas import tpu as pltpu
from jax.sharding import PartitionSpec as P

TILE = 128
CAP = 2
OWN = 4
NV = 16
NX = 4
WAVES = (256, 384, 384)
STEPS = (0, 1, 3, 2)
X1, X2, OPPOSITE, HERE = (1, 3), (3, 1), (2, 2), (0, 0)
VMEM = pl.BlockSpec(memory_space=pltpu.VMEM)
SMEM = pl.BlockSpec(memory_space=pltpu.SMEM)
ANY = pl.BlockSpec(memory_space=pl.ANY)
SHORT = pl.CostEstimate(flops=0, bytes_accessed=1024, transcendentals=0)


def moved(vir, along_y, d):
    return jnp.where(along_y, (vir + 4 * d) & 15, (vir & 12) | ((vir + d) & 3))


def send(array, phase, d):
    def target(o, v):
        y, z = divmod(v, 4)
        return (y + d) % 4 * 4 + z if o % 2 == phase else y * 4 + (z + d) % 4

    pairs = [(o * NV + v, o * NV + target(o, v)) for o in range(2 * NX) for v in range(NV)]
    return lax.ppermute(array, ("occ", "vir"), pairs)


def flip_x(array, masks):
    return lax.ppermute(array, "occ", [(o, o ^ 2 * masks[o % 2]) for o in range(2 * NX)])


def swap(array):
    return lax.ppermute(array, "occ", [(o, o ^ 1) for o in range(2 * NX)])


def far_memory(array):
    return pltpu.with_memory_space_constraint(array, pltpu.HBM)


def by_core(core, masks):
    return masks[0] if masks[0] == masks[1] else jnp.where(core == 0, masks[0], masks[1])


def call(kernel, name, args, outs, scratch=(), weights=None, gates=(), limit=10 << 20, flops=0):
    specs = [SMEM if jnp.issubdtype(a.dtype, jnp.integer) else VMEM for a in args]
    if weights is not None:
        args, specs = [*args, far_memory(weights)], [*specs, ANY]
    n = len(args)
    specs += [ANY] * len(gates)

    def body(*refs):
        kernel(*refs[:n], *refs[n + len(gates) :])

    return pl.pallas_call(
        body,
        out_shape=[jax.ShapeDtypeStruct(shape, jnp.bfloat16) for shape in outs],
        in_specs=specs,
        out_specs=[VMEM] * len(outs),
        scratch_shapes=list(scratch),
        cost_estimate=pl.CostEstimate(flops=flops, bytes_accessed=1024, transcendentals=0),
        compiler_params=pltpu.CompilerParams(vmem_limit_bytes=limit),
        name=name,
    )(*args, *gates)


def choose(pieces):
    def kernel(*refs):
        for i, ((_, k), ref) in enumerate(zip(pieces, refs)):
            refs[-1][i] = ref[k]

    outs = [(len(pieces), *pieces[0][0].shape[1:])]
    return call(kernel, "choose", [p for p, _ in pieces], outs)[0]


def pack(meta, sent, held, at, rows, gates=()):
    def kernel(meta, sent, *refs):
        me, core = meta[0], meta[1]
        for d, out in zip(STEPS[1:], refs[4:]):
            target = moved(me, core == 1, d)
            for j, (ref, step) in enumerate(zip(refs, STEPS)):
                sender = moved(me, core == 0, 4 - step)
                for k in range(CAP):
                    t = sent[(sender * NV + target) * CAP + k]
                    q = j * CAP + k
                    tile = ref[pl.ds(at, rows), pl.ds(pl.multiple_of(t * TILE, TILE), TILE)]
                    out[q // OWN, :, pl.ds(q % OWN * TILE, TILE)] = tile

    width = held[0].shape[1]
    return call(kernel, "pack", [meta, sent, *held], [(2, rows, width)] * 3, gates=gates, limit=16 << 20)


def fetch(meta, weights, held, sems, chips):
    width = held.shape[2]
    copies = []
    for j, masks in enumerate(chips):
        at = pl.multiple_of((meta[2] ^ by_core(meta[1], masks)) * width, width)
        copy = pltpu.make_async_copy(weights.at[:, pl.ds(at, width)], held.at[j], sems.at[j])
        copy.start()
        copies.append(copy)
    return copies


def dots(meta, lhs, held, copies, outs):
    half = held.shape[2] // 2
    core = meta[1]
    for j, (copy, out) in enumerate(zip(copies, outs)):
        copy.wait()
        product = jnp.dot(
            lhs[...], held[j], preferred_element_type=jnp.float32
        ).astype(jnp.bfloat16)
        out[core] = product[:, :half]
        out[1 - core] = product[:, half:]


def room(weights, chips):
    depth, width = weights.shape
    return [
        pltpu.VMEM((len(chips), depth, width // NX), jnp.bfloat16),
        pltpu.SemaphoreType.DMA((len(chips),)),
    ]


def receive(meta, sent, live, lhs, held, packed, start):
    me, core = meta[0], meta[1]
    for i, d in enumerate(STEPS):
        for j, step in enumerate(STEPS):
            sender = moved(moved(me, core == 0, 4 - step), core == 1, 4 - d)
            for k in range(CAP):
                if i == 0:
                    t = sent[(sender * NV + me) * CAP + k]
                    tile = held[j][
                        pl.ds(start, lhs.shape[0]), pl.ds(pl.multiple_of(t * TILE, TILE), TILE)
                    ]
                else:
                    q = j * CAP + k
                    tile = packed[i - 1][q // OWN, :, pl.ds(q % OWN * TILE, TILE)]
                at = pl.multiple_of((sender * CAP + k) * TILE, TILE)
                keep = k < live[sender * NV + me]
                lhs[:, pl.ds(at, TILE)] = jnp.where(keep, tile, jnp.zeros_like(tile))


def ladder_far(meta, sent, live, held, packed, start, weights, gates=()):
    chips = (OPPOSITE, X1, X2)

    def kernel(meta, sent, live, *refs):
        weights, lhs, out0, out1, out2, buffer, sems = refs[7:]
        copies = fetch(meta, weights, buffer, sems, chips)
        receive(meta, sent, live, lhs, refs[:4], refs[4:7], start)
        dots(meta, lhs, buffer, copies, (out0, out1, out2))

    rows, (depth, width) = packed[0].shape[1], weights.shape
    outs = [(rows, depth)] + [(2, rows, width // (2 * NX))] * 3
    args = [meta, sent, live, *held, *packed]
    return call(kernel, "ladder_far", args, outs, room(weights, chips), weights, gates, 34 << 20)


def ladder_here(meta, lhs, weights, gates=()):
    def kernel(meta, lhs, weights, out, buffer, sems):
        dots(meta, lhs, buffer, fetch(meta, weights, buffer, sems, (HERE,)), (out,))

    (rows, depth), width = lhs.shape, weights.shape[1]
    outs = [(2, rows, width // (2 * NX))]
    flops = rows * depth * width // 2
    return call(
        kernel, "ladder_here", [meta, lhs], outs, room(weights, (HERE,)), weights, gates, 16 << 20, flops
    )[0]


def add(meta, prev, pieces, swapped, total, base, n_rows):
    def kernel(meta, prev, p0, p1, p2, p3, swapped, *refs):
        out, sums, sems = refs[-3:]
        core, rows = meta[1], sums.shape[1]
        copies = []
        for j, (masks, ref) in enumerate(zip((HERE, X1, X2, OPPOSITE), (p0, p1, p2, p3))):
            for b in range(2):
                chip = meta[2] ^ by_core(core ^ b, masks)
                at = pl.ds(pl.multiple_of((chip * 2 + (core ^ b)) * n_rows + base, 32), rows)
                block = swapped[j] if b else ref[pieces[j][1]]
                n = j * 2 + b
                sums[n] = prev[at].astype(jnp.float32) + block.astype(jnp.float32)
                copy = pltpu.make_async_copy(sums.at[n], out.at[at], sems.at[n])
                copy.start()
                copies.append(copy)
        for copy in copies:
            copy.wait()

    rows, width = swapped.shape[1:]
    args = [meta, prev, *(p for p, _ in pieces), swapped]
    specs = [SMEM] + [VMEM] * 6
    aliases = {}
    if total is not None:
        aliases = {len(args): 0}
        args.append(total)
        specs.append(ANY)
    return pl.pallas_call(
        kernel,
        out_shape=jax.ShapeDtypeStruct(prev.shape, jnp.float32),
        in_specs=specs,
        out_specs=ANY,
        scratch_shapes=[
            pltpu.VMEM((8, rows, width), jnp.float32),
            pltpu.SemaphoreType.DMA((8,)),
        ],
        input_output_aliases=aliases,
        cost_estimate=SHORT,
        compiler_params=pltpu.CompilerParams(vmem_limit_bytes=18 << 20),
        name="residual",
    )(*args)


def local(right_prev, amplitudes, integrals, send_tiles, pair_count):
    n_rows = amplitudes.shape[0]
    occ, vir = lax.axis_index("occ"), lax.axis_index("vir")
    meta = jnp.stack([vir, occ % 2, occ // 2]).astype(jnp.int32)
    sent, live = send_tiles.reshape(-1), pair_count.reshape(-1)
    weights = integrals[0]

    held = [amplitudes] + [send(amplitudes, 0, d) for d in STEPS[1:]]
    starts = [sum(WAVES[:i]) for i in range(len(WAVES))]
    waves, gates = [], ()
    for start, rows in zip(starts, WAVES):
        packed = pack(meta, sent, held, start, rows, gates)
        waves.append([send(v, 1, d) for v, d in zip(packed, STEPS[1:])])
        gates = packed[:1]

    moved_blocks, results = (), []
    for got, start in zip(waves, starts):
        lhs, *sends = ladder_far(meta, sent, live, held, got, start, weights, gates)
        blocks = [flip_x(v, m) for v, m in zip(sends, (OPPOSITE, X1, X2))]
        here = ladder_here(meta, lhs, weights, moved_blocks)
        moved_blocks, gates = blocks, (here,)
        results.append([(here, 0), (blocks[1], 0), (blocks[2], 0), (blocks[0], 0)])

    total = None
    for pieces, start in zip(results, starts):
        swapped = swap(choose([(p, i + 1) for p, i in pieces]))
        total = add(meta, right_prev, pieces, swapped, total, start, n_rows)
    return total


def solution(mesh):
    in_specs = (P(None, ("vir", "occ")), P("occ", "vir"), P("vir", None, None), P(), P())
    out_specs = P(None, ("vir", "occ"))
    return jax.shard_map(local, mesh=mesh, in_specs=in_specs, out_specs=out_specs, check_vma=False)
```

time: 244 us -> 142 us (0.58)
  waiting for transfers between devices: 113 us -> 37.2 us
  blocking collectives: 54.3 us -> 0 us
  Pallas kernels: 0 us -> 52.9 us
  starting transfers between devices: 0.01 us -> 42.1 us
  matrix products: 22.8 us -> 0 us
  local copies, waits for them, and re-layouts: 27.8 us -> 8.8 us
  between operations: 13.5 us -> 0.37 us
  other arithmetic: 12.2 us -> 0.08 us
    all_gather x1 -> x0, waiting for transfers between devices: 113 us -> none  [local(): gathered = lax.all_gather(amp_tiles, 'vir', axis=1, tiled=True)]
    all_to_all x1 -> x0, blocking collectives: 54.3 us -> none  [local(): lax.all_to_all(ladder, 'occ', split_axis=1, concat_axis=0, tiled=True)]
    pallas_call x0 -> x15, Pallas kernels: none -> 52.9 us  [the longest x12 46.3 us: call(): pl.pallas_call(body, out_shape=[jax.ShapeDtypeStruct(shape, jnp.bfloat16)...]
    ppermute x0 -> x24, starting transfers between devices: none -> 42.1 us  [the longest x12 20.5 us: send(): return lax.ppermute(array, ('occ', 'vir'), pairs)]
    ppermute x0 -> x24, waiting for transfers between devices: none -> 37.2 us  [the longest x12 27.9 us: send(): return lax.ppermute(array, ('occ', 'vir'), pairs)]
    dot_general x1 -> x0, matrix products: 22.8 us -> none  [local(): jnp.dot(received, integrals[0], preferred_element_type=jnp.float32)]
    select_n x1 -> x0, local copies, waits for them, and re-layouts: 12 us -> none  [local(): jnp.where(live_slots[None, :, None], picked, jnp.zeros_like(picked))]
    gather x1 -> x0, local copies, waits for them, and re-layouts: 11 us -> none  [local(): picked = jnp.take(gathered, columns, axis=1)]
  transfers between devices with their start and end apart: 1 -> 24, of which waited for: 1 -> 7; matrix products, arithmetic and copies ran while one was open for 1% -> 1% of each run, Pallas kernels for 0% -> 34%
where the time goes in v2:
time: 142 us; the launch traced here: 141 us
  Pallas kernels  52.9 us (37%)
  starting transfers between devices  42.1 us (30%)
  waiting for transfers between devices  37.2 us (26%)
  local copies, waits for them, and re-layouts  8.8 us (6%)
    pallas_call x12, Pallas kernels, call(): pl.pallas_call(body, out_shape=[jax.ShapeDtypeStruct(shape, jnp.bfloat16)...  46.3 us
    ppermute x12, waiting for transfers between devices, send(): return lax.ppermute(array, ('occ', 'vir'), pairs)  27.9 us
    ppermute x12, starting transfers between devices, send(): return lax.ppermute(array, ('occ', 'vir'), pairs)  20.5 us
    ppermute x9, starting transfers between devices, flip_x(): lax.ppermute(array, 'occ', [(o, o ^ 2 * masks[o % 2]) for o in range(2 *...  13.3 us
    unnamed x21, local copies, waits for them, and re-layouts  8.58 us
    ppermute x3, starting transfers between devices, swap(): return lax.ppermute(array, 'occ', [(o, o ^ 1) for o in range(2 * NX)])  8.39 us
    ppermute x9, waiting for transfers between devices, flip_x(): lax.ppermute(array, 'occ', [(o, o ^ 2 * masks[o % 2]) for o in range(2 *...  6.71 us
    pallas_call x3, Pallas kernels, add(): pl.pallas_call(kernel, out_shape=jax.ShapeDtypeStruct(prev.shape, jnp.flo...  6.56 us
  transfers between devices with their start and end apart: 24, of which 7 were waited for; matrix products, arithmetic and copies ran while one was open for 1% of the time, Pallas kernels for 34%

profile of v2, /device:TPU:1, one launch (start us, length us, event | category | flops | bytes accessed | tf_op | source)
XLA Modules:
  0.0 141.4 jit_solution(2725204822283762102)
XLA Ops:
  0.0 4.4 %collective-permute-start.2 = (bf16[1024,512]{1,0:T(8,128)(2,1)}, bf16[1024,512]{1,0:T(8,128)(2,1)S(1)}, u32[]{:S(2)}, u32[]{:S(2)}) collective-permute-start(bf16[1024,512]{1,0:T(8,128)(2,1)} %refs_3_.5), channel_id=1, source_target_pairs={{0,8},{1,9},{2,10},{3,11},{4,12},{5,13},{6,14},{7,15},{8,0},{9,1},... | collective-permute-start | bytes 3145736 | tf_op jit(solution)/shard_map/ppermute | solution.py:34
  4.4 0.4 collective-permute-start.1
  4.9 1.0 collective-permute-start
  5.9 0.9 copy.8
  6.8 0.1 reshape.6.refs_1_
  6.9 0.1 pad_add_fusion.refs_0_.meta
  7.0 10.2 %collective-permute-done.2.refs_5_.refs_6_ = bf16[1024,512]{1,0:T(8,128)(2,1)S(1)} collective-permute-done((bf16[1024,512]{1,0:T(8,128)(2,1)}, bf16[1024,512]{1,0:T(8,128)(2,1)S(1)}, u32[]{:S(2)}, u32[]{:S(2)}) %collective-permute-start.2) | collective-permute-done | bytes 1048608 | tf_op jit(solution)/shard_map/ppermute | solution.py:34
  17.2 12.0 %collective-permute-done.1.refs_4_.refs_5_ = bf16[1024,512]{1,0:T(8,128)(2,1)S(1)} collective-permute-done((bf16[1024,512]{1,0:T(8,128)(2,1)}, bf16[1024,512]{1,0:T(8,128)(2,1)S(1)}, u32[]{:S(2)}, u32[]{:S(2)}) %collective-permute-start.1) | collective-permute-done | bytes 1048608 | tf_op jit(solution)/shard_map/ppermute | solution.py:34
  29.1 0.0 collective-permute-done.refs_3_.refs_4_
  29.1 1.0 copy-done.3
  30.1 1.2 copy-done.1
  31.3 1.2 copy-done.4
  32.6 1.8 %pack.3 = (bf16[2,256,512]{2,1,0:T(8,128)(2,1)}, bf16[2,256,512]{2,1,0:T(8,128)(2,1)S(1)}, bf16[2,256,512]{2,1,0:T(8,128)(2,1)}) custom-call(s32[3]{0:T(128)S(1)} %pad_add_fusion.refs_0_.meta, s32[512]{0:T(512)S(1)} %reshape.6.refs_1_, bf16[1024,512]{1,0:T(8,128)(2,1)S(1)} %copy-done.1, bf16[1024,512]{1,0:T(8,128)(2,1)S(1)} %copy-done.4, ...), custom_call_target="tpu_custom_call" | custom-call | bytes 1024 | tf_op jit(solution)/shard_map/pack/pallas_call | solution.py:63
  34.4 2.5 %collective-permute-start.10 = (bf16[2,256,512]{2,1,0:T(8,128)(2,1)S(1)}, bf16[2,256,512]{2,1,0:T(8,128)(2,1)S(1)}, u32[]{:S(2)}, u32[]{:S(2)}) collective-permute-start(bf16[2,256,512]{2,1,0:T(8,128)(2,1)S(1)} %get-tuple-element.33), channel_id=1, source_target_pairs={{0,3},{1,0},{2,1},{3,2},{4,7},{5,4},{6,5},{7,6},{8,11},{9,8},{10,9... | collective-permute-start | bytes 1572872 | tf_op jit(solution)/shard_map/ppermute | solution.py:34
  36.9 0.5 collective-permute-start.11
  37.4 0.5 collective-permute-start.9
  37.9 2.4 %pack.4 = (bf16[2,384,512]{2,1,0:T(8,128)(2,1)}, bf16[2,384,512]{2,1,0:T(8,128)(2,1)}, bf16[2,384,512]{2,1,0:T(8,128)(2,1)}) custom-call(s32[3]{0:T(128)S(1)} %pad_add_fusion.refs_0_.meta, s32[512]{0:T(512)S(1)} %reshape.6.refs_1_, bf16[1024,512]{1,0:T(8,128)(2,1)S(1)} %copy-done.1, bf16[1024,512]{1,0:T(8,128)(2,1)S(1)} %copy-done.4, ...), custom_call_target="tpu_custom_call" | custom-call | bytes 1024 | tf_op jit(solution)/shard_map/pack/pallas_call | solution.py:63
  40.3 2.1 %collective-permute-start.7 = (bf16[2,384,512]{2,1,0:T(8,128)(2,1)}, bf16[2,384,512]{2,1,0:T(8,128)(2,1)}, u32[]{:S(2)}, u32[]{:S(2)}) collective-permute-start(bf16[2,384,512]{2,1,0:T(8,128)(2,1)} %get-tuple-element.31), channel_id=1, source_target_pairs={{0,3},{1,0},{2,1},{3,2},{4,7},{5,4},{6,5},{7,6},{8,11},{9,8},{10,9... | collective-permute-start | bytes 2359304 | tf_op jit(solution)/shard_map/ppermute | solution.py:34
  42.5 1.3 collective-permute-start.8
  43.7 4.9 %collective-permute-done.10.refs_8_ = bf16[2,256,512]{2,1,0:T(8,128)(2,1)S(1)} collective-permute-done((bf16[2,256,512]{2,1,0:T(8,128)(2,1)S(1)}, bf16[2,256,512]{2,1,0:T(8,128)(2,1)S(1)}, u32[]{:S(2)}, u32[]{:S(2)}) %collective-permute-start.10) | collective-permute-done | bytes 524320 | tf_op jit(solution)/shard_map/ppermute | solution.py:34
  48.6 0.8 copy-done.7
  49.4 0.0 collective-permute-start.6
  49.4 0.1 reshape.7.refs_2_
  49.5 1.2 copy-done.5
  50.7 1.0 pack.5
  51.7 0.9 collective-permute-done.9.refs_7_
  52.6 1.2 copy-done.6
  53.9 1.0 copy-done.8
  54.9 7.9 %ladder_far.3 = (bf16[256,4096]{1,0:T(8,128)(2,1)S(1)}, bf16[2,256,256]{2,1,0:T(8,128)(2,1)S(1)}, bf16[2,256,256]{2,1,0:T(8,128)(2,1)S(1)}, bf16[2,256,256]{2,1,0:T(8,128)(2,1)S(1)}) custom-call(s32[3]{0:T(128)S(1)} %pad_add_fusion.refs_0_.meta, s32[512]{0:T(512)S(1)} %reshape.6.refs_1_, s32[256]{0:T(256)S(1)} %reshape.7.refs_2_, ...), custom_call_target="tpu_custom_call" | custom-call | bytes 1024 | tf_op jit(solution)/shard_map/ladder_far/pallas_call | solution.py:63
  62.8 2.8 %collective-permute-start.12 = (bf16[2,256,256]{2,1,0:T(8,128)(2,1)S(1)}, bf16[2,256,256]{2,1,0:T(8,128)(2,1)S(1)}, u32[]{:S(2)}, u32[]{:S(2)}) collective-permute-start(bf16[2,256,256]{2,1,0:T(8,128)(2,1)S(1)} %get-tuple-element.37), channel_id=1, source_target_pairs={{0,64},{16,80},{32,96},{48,112},{64,0},{80,16},{96,32},{112,48},{1... | collective-permute-start | bytes 786440 | tf_op jit(solution)/shard_map/ppermute | solution.py:38
  65.6 2.6 %collective-permute-start.4 = (bf16[2,384,512]{2,1,0:T(8,128)(2,1)S(1)}, bf16[2,384,512]{2,1,0:T(8,128)(2,1)S(1)}, u32[]{:S(2)}, u32[]{:S(2)}) collective-permute-start(bf16[2,384,512]{2,1,0:T(8,128)(2,1)S(1)} %get-tuple-element.29), channel_id=1, source_target_pairs={{0,3},{1,0},{2,1},{3,2},{4,7},{5,4},{6,5},{7,6},{8,11},{9,8},{10,9... | collective-permute-start | bytes 2359304 | tf_op jit(solution)/shard_map/ppermute | solution.py:34
  68.3 1.3 collective-permute-done.12.refs_3_.p3
  69.6 5.0 %collective-permute-start.5 = (bf16[2,384,512]{2,1,0:T(8,128)(2,1)S(1)}, bf16[2,384,512]{2,1,0:T(8,128)(2,1)S(1)}, u32[]{:S(2)}, u32[]{:S(2)}) collective-permute-start(bf16[2,384,512]{2,1,0:T(8,128)(2,1)S(1)} %get-tuple-element.30), channel_id=1, source_target_pairs={{0,2},{1,3},{2,0},{3,1},{4,6},{5,7},{6,4},{7,5},{8,10},{9,11},{10,... | collective-permute-start | bytes 2359304 | tf_op jit(solution)/shard_map/ppermute | solution.py:34
  74.6 0.0 collective-permute-done.7.refs_8_
  74.6 2.6 %collective-permute-start.13 = (bf16[2,256,256]{2,1,0:T(8,128)(2,1)S(1)}, bf16[2,256,256]{2,1,0:T(8,128)(2,1)S(1)}, u32[]{:S(2)}, u32[]{:S(2)}) collective-permute-start(bf16[2,256,256]{2,1,0:T(8,128)(2,1)S(1)} %get-tuple-element.38), channel_id=1, source_target_pairs={{0,32},{16,112},{32,0},{48,80},{64,96},{80,48},{96,64},{112,16},{1... | collective-permute-start | bytes 786440 | tf_op jit(solution)/shard_map/ppermute | solution.py:38
  77.2 0.0 collective-permute-done.6.refs_7_
  77.2 0.0 collective-permute-start.14
  77.2 4.0 %ladder_here.3.refs_11_.refs_0_.p0 = bf16[2,256,256]{2,1,0:T(8,128)(2,1)S(1)} custom-call(s32[3]{0:T(128)S(1)} %pad_add_fusion.refs_0_.meta, bf16[256,4096]{1,0:T(8,128)(2,1)S(1)} %get-tuple-element.35.refs_1_, bf16[4096,2048]{1,0:T(8,128)(2,1)} %bitcast.5), custom_call_target="tpu_custom_call" | custom-call | flops 1073741824 | bytes 1024 | tf_op jit(solution)/shard_map/ladder_here/pallas_call | solution.py:63
  81.3 10.3 %ladder_far.4 = (bf16[384,4096]{1,0:T(8,128)(2,1)S(1)}, bf16[2,384,256]{2,1,0:T(8,128)(2,1)S(1)}, bf16[2,384,256]{2,1,0:T(8,128)(2,1)S(1)}, bf16[2,384,256]{2,1,0:T(8,128)(2,1)S(1)}) custom-call(s32[3]{0:T(128)S(1)} %pad_add_fusion.refs_0_.meta, s32[512]{0:T(512)S(1)} %reshape.6.refs_1_, s32[256]{0:T(256)S(1)} %reshape.7.refs_2_, ...), custom_call_target="tpu_custom_call" | custom-call | bytes 1024 | tf_op jit(solution)/shard_map/ladder_far/pallas_call | solution.py:63
  91.5 1.5 %collective-permute-start.15 = (bf16[2,384,256]{2,1,0:T(8,128)(2,1)S(1)}, bf16[2,384,256]{2,1,0:T(8,128)(2,1)S(1)}, u32[]{:S(2)}, u32[]{:S(2)}) collective-permute-start(bf16[2,384,256]{2,1,0:T(8,128)(2,1)S(1)} %get-tuple-element.41), channel_id=1, source_target_pairs={{0,64},{16,80},{32,96},{48,112},{64,0},{80,16},{96,32},{112,48},{1... | collective-permute-start | bytes 1179656 | tf_op jit(solution)/shard_map/ppermute | solution.py:38
  93.1 0.0 collective-permute-done.14.refs_5_.refs_2_.p2
  93.1 2.4 %collective-permute-start.16 = (bf16[2,384,256]{2,1,0:T(8,128)(2,1)S(1)}, bf16[2,384,256]{2,1,0:T(8,128)(2,1)S(1)}, u32[]{:S(2)}, u32[]{:S(2)}) collective-permute-start(bf16[2,384,256]{2,1,0:T(8,128)(2,1)S(1)} %get-tuple-element.42), channel_id=1, source_target_pairs={{0,32},{16,112},{32,0},{48,80},{64,96},{80,48},{96,64},{112,16},{1... | collective-permute-start | bytes 1179656 | tf_op jit(solution)/shard_map/ppermute | solution.py:38
  95.5 0.0 collective-permute-done.4.refs_8_
  95.5 0.0 collective-permute-start.17
  95.5 4.6 %ladder_here.4.refs_11_.refs_0_.p0 = bf16[2,384,256]{2,1,0:T(8,128)(2,1)S(1)} custom-call(s32[3]{0:T(128)S(1)} %pad_add_fusion.refs_0_.meta, bf16[384,4096]{1,0:T(8,128)(2,1)S(1)} %get-tuple-element.36.refs_1_, bf16[4096,2048]{1,0:T(8,128)(2,1)} %bitcast.7, bf16[2,256,256]{2,1,0:T(8,128)(2,1)S(1)} %collective-permute-done.12.refs_3_.p3, ...), custom_call_target="tpu_custom_call" | custom-call | flops 1610612736 | bytes 1024 | tf_op jit(solution)/shard_map/ladder_here/pallas_call | solution.py:63
  100.1 0.0 collective-permute-done.5.refs_9_
  100.1 0.0 collective-permute-done.3.refs_7_
  100.1 9.2 %ladder_far.5 = (bf16[384,4096]{1,0:T(8,128)(2,1)S(1)}, bf16[2,384,256]{2,1,0:T(8,128)(2,1)S(1)}, bf16[2,384,256]{2,1,0:T(8,128)(2,1)S(1)}, bf16[2,384,256]{2,1,0:T(8,128)(2,1)S(1)}) custom-call(s32[3]{0:T(128)S(1)} %pad_add_fusion.refs_0_.meta, s32[512]{0:T(512)S(1)} %reshape.6.refs_1_, s32[256]{0:T(256)S(1)} %reshape.7.refs_2_, ...), custom_call_target="tpu_custom_call" | custom-call | bytes 1024 | tf_op jit(solution)/shard_map/ladder_far/pallas_call | solution.py:63
  109.4 0.4 collective-permute-start.18
  109.7 1.3 collective-permute-start.19
  111.0 2.3 %collective-permute-start.20 = (bf16[2,384,256]{2,1,0:T(8,128)(2,1)S(1)}, bf16[2,384,256]{2,1,0:T(8,128)(2,1)S(1)}, u32[]{:S(2)}, u32[]{:S(2)}) collective-permute-start(bf16[2,384,256]{2,1,0:T(8,128)(2,1)S(1)} %get-tuple-element.46), channel_id=1, source_target_pairs={{0,64},{16,80},{32,96},{48,112},{64,0},{80,16},{96,32},{112,48},{1... | collective-permute-start | bytes 1179656 | tf_op jit(solution)/shard_map/ppermute | solution.py:38
  113.3 0.0 collective-permute-done.16.refs_4_.refs_1_.p1
  113.3 0.1 choose.4
  113.4 4.7 %collective-permute-start.22 = (bf16[4,384,256]{2,1,0:T(8,128)(2,1)S(1)}, bf16[4,384,256]{2,1,0:T(8,128)(2,1)S(1)}, u32[]{:S(2)}, u32[]{:S(2)}) collective-permute-start(bf16[4,384,256]{2,1,0:T(8,128)(2,1)S(1)} %choose.4), channel_id=1, source_target_pairs={{0,16},{16,0},{32,48},{48,32},{64,80},{80,64},{96,112},{112,96},{1... | collective-permute-start | bytes 2359304 | tf_op jit(solution)/shard_map/ppermute | solution.py:42
  118.1 4.9 %ladder_here.5.refs_0_.p0 = bf16[2,384,256]{2,1,0:T(8,128)(2,1)S(1)} custom-call(s32[3]{0:T(128)S(1)} %pad_add_fusion.refs_0_.meta, bf16[384,4096]{1,0:T(8,128)(2,1)S(1)} %get-tuple-element.40.refs_1_, bf16[4096,2048]{1,0:T(8,128)(2,1)} %bitcast.9, bf16[2,384,256]{2,1,0:T(8,128)(2,1)S(1)} %collective-permute-done.15.refs_3_.p3, ...), custom_call_target="tpu_custom_call" | custom-call | flops 1610612736 | bytes 1024 | tf_op jit(solution)/shard_map/ladder_here/pallas_call | solution.py:63
  122.9 0.0 collective-permute-done.19.refs_2_.p2
  123.0 5.4 %collective-permute-done.20.refs_3_.p3 = bf16[2,384,256]{2,1,0:T(8,128)(2,1)S(1)} collective-permute-done((bf16[2,384,256]{2,1,0:T(8,128)(2,1)S(1)}, bf16[2,384,256]{2,1,0:T(8,128)(2,1)S(1)}, u32[]{:S(2)}, u32[]{:S(2)}) %collective-permute-start.20) | collective-permute-done | bytes 393248 | tf_op jit(solution)/shard_map/ppermute | solution.py:38
  128.3 0.1 choose.3
  128.4 3.6 %collective-permute-start.21 = (bf16[4,384,256]{2,1,0:T(8,128)(2,1)S(1)}, bf16[4,384,256]{2,1,0:T(8,128)(2,1)S(1)}, u32[]{:S(2)}, u32[]{:S(2)}) collective-permute-start(bf16[4,384,256]{2,1,0:T(8,128)(2,1)S(1)} %choose.3), channel_id=1, source_target_pairs={{0,16},{16,0},{32,48},{48,32},{64,80},{80,64},{96,112},{112,96},{1... | collective-permute-start | bytes 2359304 | tf_op jit(solution)/shard_map/ppermute | solution.py:42
  132.0 0.1 collective-permute-start.23
  132.1 2.5 %collective-permute-done.23.swapped = bf16[4,256,256]{2,1,0:T(8,128)(2,1)S(1)} collective-permute-done((bf16[4,256,256]{2,1,0:T(8,128)(2,1)S(1)}, bf16[4,256,256]{2,1,0:T(8,128)(2,1)S(1)}, u32[]{:S(2)}, u32[]{:S(2)}) %collective-permute-start.23) | collective-permute-done | bytes 524320 | tf_op jit(solution)/shard_map/ppermute | solution.py:42
  134.6 1.9 %residual.3.refs_0_ = f32[8192,256]{1,0:T(8,128)} custom-call(s32[3]{0:T(128)S(1)} %pad_add_fusion.refs_0_.meta, bf16[8192,256]{1,0:T(8,128)(2,1)S(1)} %copy-done, bf16[2,256,256]{2,1,0:T(8,128)(2,1)S(1)} %ladder_here.3.refs_11_.refs_0_.p0, bf16[2,256,256]{2,1,0:T(8,128)(2,1)S(1)} %collective-permute-done.13.refs_4_.refs_1_.p1, ...), custom_call_target="tpu_custom_call" | custom-call | bytes 1024 | tf_op jit(solution)/shard_map/residual/pallas_call | solution.py:204
  136.6 2.3 %residual.4.refs_0_ = f32[8192,256]{1,0:T(8,128)} custom-call(s32[3]{0:T(128)S(1)} %pad_add_fusion.refs_0_.meta, bf16[8192,256]{1,0:T(8,128)(2,1)S(1)} %copy-done, bf16[2,384,256]{2,1,0:T(8,128)(2,1)S(1)} %ladder_here.4.refs_11_.refs_0_.p0, bf16[2,384,256]{2,1,0:T(8,128)(2,1)S(1)} %collective-permute-done.16.refs_4_.refs_1_.p1, ...), custom_call_target="tpu_custom_call", output_to_operand_aliasing={{}: (7, {})} | custom-call | bytes 1024 | tf_op jit(solution)/shard_map/residual/pallas_call | solution.py:204
  138.9 2.3 %residual.5 = f32[8192,256]{1,0:T(8,128)} custom-call(s32[3]{0:T(128)S(1)} %pad_add_fusion.refs_0_.meta, bf16[8192,256]{1,0:T(8,128)(2,1)S(1)} %copy-done, bf16[2,384,256]{2,1,0:T(8,128)(2,1)S(1)} %ladder_here.5.refs_0_.p0, bf16[2,384,256]{2,1,0:T(8,128)(2,1)S(1)} %collective-permute-done.18.refs_1_.p1, ...), custom_call_target="tpu_custom_call", output_to_operand_aliasing={{}: (7, {})} | custom-call | bytes 1024 | tf_op jit(solution)/shard_map/residual/pallas_call | solution.py:204
  (23 shorter events, 0.1 us)
Async XLA Ops:
  0.0 49.4 %copy-start.9 = (s32[16,16]{1,0:T(8,128)S(1)}, s32[16,16]{1,0:T(8,128)}, u32[]{:S(2)}) copy-start(s32[16,16]{1,0:T(8,128)} %param.9) | copy-start | bytes 3076
  0.0 17.2 %collective-permute-start.2 = (bf16[1024,512]{1,0:T(8,128)(2,1)}, bf16[1024,512]{1,0:T(8,128)(2,1)S(1)}, u32[]{:S(2)}, u32[]{:S(2)}) collective-permute-start(bf16[1024,512]{1,0:T(8,128)(2,1)} %refs_3_.5), channel_id=1, source_target_pairs={{0,8},{1,9},{2,10},{3,11},{4,12},{5,13},{6,14},{7,15},{8,0},{9,1},... | collective-permute-start | bytes 3145736 | tf_op jit(solution)/shard_map/ppermute | solution.py:34
  4.4 24.7 %collective-permute-start.1 = (bf16[1024,512]{1,0:T(8,128)(2,1)}, bf16[1024,512]{1,0:T(8,128)(2,1)S(1)}, u32[]{:S(2)}, u32[]{:S(2)}) collective-permute-start(bf16[1024,512]{1,0:T(8,128)(2,1)} %refs_3_.5), channel_id=1, source_target_pairs={{0,12},{1,13},{2,14},{3,15},{4,0},{5,1},{6,2},{7,3},{8,4},{9,5},{1... | collective-permute-start | bytes 3145736 | tf_op jit(solution)/shard_map/ppermute | solution.py:34
  4.9 24.3 %collective-permute-start = (bf16[1024,512]{1,0:T(8,128)(2,1)}, bf16[1024,512]{1,0:T(8,128)(2,1)S(1)}, u32[]{:S(2)}, u32[]{:S(2)}) collective-permute-start(bf16[1024,512]{1,0:T(8,128)(2,1)} %refs_3_.5), channel_id=1, source_target_pairs={{0,4},{1,5},{2,6},{3,7},{4,8},{5,9},{6,10},{7,11},{8,12},{9,13},{1... | collective-permute-start | bytes 3145736 | tf_op jit(solution)/shard_map/ppermute | solution.py:34
  29.1 1.0 copy-start.3
  30.1 1.2 copy-start.1
  31.3 1.2 copy-start.4
  32.6 16.9 %copy-start.2 = (bf16[1024,512]{1,0:T(8,128)(2,1)S(1)}, bf16[1024,512]{1,0:T(8,128)(2,1)}, u32[]{:S(2)}) copy-start(bf16[1024,512]{1,0:T(8,128)(2,1)} %refs_3_.5) | copy-start | bytes 3145732
  34.4 14.2 %collective-permute-start.10 = (bf16[2,256,512]{2,1,0:T(8,128)(2,1)S(1)}, bf16[2,256,512]{2,1,0:T(8,128)(2,1)S(1)}, u32[]{:S(2)}, u32[]{:S(2)}) collective-permute-start(bf16[2,256,512]{2,1,0:T(8,128)(2,1)S(1)} %get-tuple-element.33), channel_id=1, source_target_pairs={{0,3},{1,0},{2,1},{3,2},{4,7},{5,4},{6,5},{7,6},{8,11},{9,8},{10,9... | collective-permute-start | bytes 1572872 | tf_op jit(solution)/shard_map/ppermute | solution.py:34
  36.9 14.9 %collective-permute-start.11 = (bf16[2,256,512]{2,1,0:T(8,128)(2,1)}, bf16[2,256,512]{2,1,0:T(8,128)(2,1)}, u32[]{:S(2)}, u32[]{:S(2)}) collective-permute-start(bf16[2,256,512]{2,1,0:T(8,128)(2,1)} %get-tuple-element.34), channel_id=1, source_target_pairs={{0,2},{1,3},{2,0},{3,1},{4,6},{5,7},{6,4},{7,5},{8,10},{9,11},{10,... | collective-permute-start | bytes 1572872 | tf_op jit(solution)/shard_map/ppermute | solution.py:34
  37.4 15.3 %collective-permute-start.9 = (bf16[2,256,512]{2,1,0:T(8,128)(2,1)}, bf16[2,256,512]{2,1,0:T(8,128)(2,1)}, u32[]{:S(2)}, u32[]{:S(2)}) collective-permute-start(bf16[2,256,512]{2,1,0:T(8,128)(2,1)} %get-tuple-element.26.refs_6_), channel_id=1, source_target_pairs={{0,1},{1,2},{2,3},{3,0},{4,5},{5,6},{6,7},{7,4},{8,9},{9,10},{10,1... | collective-permute-start | bytes 1572872 | tf_op jit(solution)/shard_map/ppermute | solution.py:34
  40.3 34.3 %collective-permute-start.7 = (bf16[2,384,512]{2,1,0:T(8,128)(2,1)}, bf16[2,384,512]{2,1,0:T(8,128)(2,1)}, u32[]{:S(2)}, u32[]{:S(2)}) collective-permute-start(bf16[2,384,512]{2,1,0:T(8,128)(2,1)} %get-tuple-element.31), channel_id=1, source_target_pairs={{0,3},{1,0},{2,1},{3,2},{4,7},{5,4},{6,5},{7,6},{8,11},{9,8},{10,9... | collective-permute-start | bytes 2359304 | tf_op jit(solution)/shard_map/ppermute | solution.py:34
  42.5 32.2 %collective-permute-start.8 = (bf16[2,384,512]{2,1,0:T(8,128)(2,1)}, bf16[2,384,512]{2,1,0:T(8,128)(2,1)}, u32[]{:S(2)}, u32[]{:S(2)}) collective-permute-start(bf16[2,384,512]{2,1,0:T(8,128)(2,1)} %get-tuple-element.32), channel_id=1, source_target_pairs={{0,2},{1,3},{2,0},{3,1},{4,6},{5,7},{6,4},{7,5},{8,10},{9,11},{10,... | collective-permute-start | bytes 2359304 | tf_op jit(solution)/shard_map/ppermute | solution.py:34
  48.6 0.8 copy-start.7
  49.4 27.8 %collective-permute-start.6 = (bf16[2,384,512]{2,1,0:T(8,128)(2,1)}, bf16[2,384,512]{2,1,0:T(8,128)(2,1)}, u32[]{:S(2)}, u32[]{:S(2)}) collective-permute-start(bf16[2,384,512]{2,1,0:T(8,128)(2,1)} %get-tuple-element.27.refs_6_), channel_id=1, source_target_pairs={{0,1},{1,2},{2,3},{3,0},{4,5},{5,6},{6,7},{7,4},{8,9},{9,10},{10,1... | collective-permute-start | bytes 2359304 | tf_op jit(solution)/shard_map/ppermute | solution.py:34
  49.5 1.2 copy-start.5
  52.6 1.2 copy-start.6
  53.9 1.0 copy-start.8
  62.8 6.8 %collective-permute-start.12 = (bf16[2,256,256]{2,1,0:T(8,128)(2,1)S(1)}, bf16[2,256,256]{2,1,0:T(8,128)(2,1)S(1)}, u32[]{:S(2)}, u32[]{:S(2)}) collective-permute-start(bf16[2,256,256]{2,1,0:T(8,128)(2,1)S(1)} %get-tuple-element.37), channel_id=1, source_target_pairs={{0,64},{16,80},{32,96},{48,112},{64,0},{80,16},{96,32},{112,48},{1... | collective-permute-start | bytes 786440 | tf_op jit(solution)/shard_map/ppermute | solution.py:38
  65.6 29.9 %collective-permute-start.4 = (bf16[2,384,512]{2,1,0:T(8,128)(2,1)S(1)}, bf16[2,384,512]{2,1,0:T(8,128)(2,1)S(1)}, u32[]{:S(2)}, u32[]{:S(2)}) collective-permute-start(bf16[2,384,512]{2,1,0:T(8,128)(2,1)S(1)} %get-tuple-element.29), channel_id=1, source_target_pairs={{0,3},{1,0},{2,1},{3,2},{4,7},{5,4},{6,5},{7,6},{8,11},{9,8},{10,9... | collective-permute-start | bytes 2359304 | tf_op jit(solution)/shard_map/ppermute | solution.py:34
  69.6 30.5 %collective-permute-start.5 = (bf16[2,384,512]{2,1,0:T(8,128)(2,1)S(1)}, bf16[2,384,512]{2,1,0:T(8,128)(2,1)S(1)}, u32[]{:S(2)}, u32[]{:S(2)}) collective-permute-start(bf16[2,384,512]{2,1,0:T(8,128)(2,1)S(1)} %get-tuple-element.30), channel_id=1, source_target_pairs={{0,2},{1,3},{2,0},{3,1},{4,6},{5,7},{6,4},{7,5},{8,10},{9,11},{10,... | collective-permute-start | bytes 2359304 | tf_op jit(solution)/shard_map/ppermute | solution.py:34
  74.6 25.5 %collective-permute-start.3 = (bf16[2,384,512]{2,1,0:T(8,128)(2,1)S(1)}, bf16[2,384,512]{2,1,0:T(8,128)(2,1)S(1)}, u32[]{:S(2)}, u32[]{:S(2)}) collective-permute-start(bf16[2,384,512]{2,1,0:T(8,128)(2,1)S(1)} %get-tuple-element.28.refs_11_), channel_id=1, source_target_pairs={{0,1},{1,2},{2,3},{3,0},{4,5},{5,6},{6,7},{7,4},{8,9},{9,10},{10,1... | collective-permute-start | bytes 2359304 | tf_op jit(solution)/shard_map/ppermute | solution.py:34
  74.6 16.9 %collective-permute-start.13 = (bf16[2,256,256]{2,1,0:T(8,128)(2,1)S(1)}, bf16[2,256,256]{2,1,0:T(8,128)(2,1)S(1)}, u32[]{:S(2)}, u32[]{:S(2)}) collective-permute-start(bf16[2,256,256]{2,1,0:T(8,128)(2,1)S(1)} %get-tuple-element.38), channel_id=1, source_target_pairs={{0,32},{16,112},{32,0},{48,80},{64,96},{80,48},{96,64},{112,16},{1... | collective-permute-start | bytes 786440 | tf_op jit(solution)/shard_map/ppermute | solution.py:38
  77.2 15.9 %collective-permute-start.14 = (bf16[2,256,256]{2,1,0:T(8,128)(2,1)S(1)}, bf16[2,256,256]{2,1,0:T(8,128)(2,1)S(1)}, u32[]{:S(2)}, u32[]{:S(2)}) collective-permute-start(bf16[2,256,256]{2,1,0:T(8,128)(2,1)S(1)} %get-tuple-element.39), channel_id=1, source_target_pairs={{0,96},{16,48},{32,64},{48,16},{64,32},{80,112},{96,0},{112,80},{1... | collective-permute-start | bytes 786440 | tf_op jit(solution)/shard_map/ppermute | solution.py:38
  91.5 19.5 %collective-permute-start.15 = (bf16[2,384,256]{2,1,0:T(8,128)(2,1)S(1)}, bf16[2,384,256]{2,1,0:T(8,128)(2,1)S(1)}, u32[]{:S(2)}, u32[]{:S(2)}) collective-permute-start(bf16[2,384,256]{2,1,0:T(8,128)(2,1)S(1)} %get-tuple-element.41), channel_id=1, source_target_pairs={{0,64},{16,80},{32,96},{48,112},{64,0},{80,16},{96,32},{112,48},{1... | collective-permute-start | bytes 1179656 | tf_op jit(solution)/shard_map/ppermute | solution.py:38
  93.1 20.2 %collective-permute-start.16 = (bf16[2,384,256]{2,1,0:T(8,128)(2,1)S(1)}, bf16[2,384,256]{2,1,0:T(8,128)(2,1)S(1)}, u32[]{:S(2)}, u32[]{:S(2)}) collective-permute-start(bf16[2,384,256]{2,1,0:T(8,128)(2,1)S(1)} %get-tuple-element.42), channel_id=1, source_target_pairs={{0,32},{16,112},{32,0},{48,80},{64,96},{80,48},{96,64},{112,16},{1... | collective-permute-start | bytes 1179656 | tf_op jit(solution)/shard_map/ppermute | solution.py:38
  95.5 17.8 %collective-permute-start.17 = (bf16[2,384,256]{2,1,0:T(8,128)(2,1)S(1)}, bf16[2,384,256]{2,1,0:T(8,128)(2,1)S(1)}, u32[]{:S(2)}, u32[]{:S(2)}) collective-permute-start(bf16[2,384,256]{2,1,0:T(8,128)(2,1)S(1)} %get-tuple-element.43), channel_id=1, source_target_pairs={{0,96},{16,48},{32,64},{48,16},{64,32},{80,112},{96,0},{112,80},{1... | collective-permute-start | bytes 1179656 | tf_op jit(solution)/shard_map/ppermute | solution.py:38
  109.4 13.6 %collective-permute-start.18 = (bf16[2,384,256]{2,1,0:T(8,128)(2,1)S(1)}, bf16[2,384,256]{2,1,0:T(8,128)(2,1)S(1)}, u32[]{:S(2)}, u32[]{:S(2)}) collective-permute-start(bf16[2,384,256]{2,1,0:T(8,128)(2,1)S(1)} %get-tuple-element.44), channel_id=1, source_target_pairs={{0,32},{16,112},{32,0},{48,80},{64,96},{80,48},{96,64},{112,16},{1... | collective-permute-start | bytes 1179656 | tf_op jit(solution)/shard_map/ppermute | solution.py:38
  109.7 13.2 %collective-permute-start.19 = (bf16[2,384,256]{2,1,0:T(8,128)(2,1)S(1)}, bf16[2,384,256]{2,1,0:T(8,128)(2,1)S(1)}, u32[]{:S(2)}, u32[]{:S(2)}) collective-permute-start(bf16[2,384,256]{2,1,0:T(8,128)(2,1)S(1)} %get-tuple-element.45), channel_id=1, source_target_pairs={{0,96},{16,48},{32,64},{48,16},{64,32},{80,112},{96,0},{112,80},{1... | collective-permute-start | bytes 1179656 | tf_op jit(solution)/shard_map/ppermute | solution.py:38
  111.0 17.3 %collective-permute-start.20 = (bf16[2,384,256]{2,1,0:T(8,128)(2,1)S(1)}, bf16[2,384,256]{2,1,0:T(8,128)(2,1)S(1)}, u32[]{:S(2)}, u32[]{:S(2)}) collective-permute-start(bf16[2,384,256]{2,1,0:T(8,128)(2,1)S(1)} %get-tuple-element.46), channel_id=1, source_target_pairs={{0,64},{16,80},{32,96},{48,112},{64,0},{80,16},{96,32},{112,48},{1... | collective-permute-start | bytes 1179656 | tf_op jit(solution)/shard_map/ppermute | solution.py:38
  113.4 23.2 %collective-permute-start.22 = (bf16[4,384,256]{2,1,0:T(8,128)(2,1)S(1)}, bf16[4,384,256]{2,1,0:T(8,128)(2,1)S(1)}, u32[]{:S(2)}, u32[]{:S(2)}) collective-permute-start(bf16[4,384,256]{2,1,0:T(8,128)(2,1)S(1)} %choose.4), channel_id=1, source_target_pairs={{0,16},{16,0},{32,48},{48,32},{64,80},{80,64},{96,112},{112,96},{1... | collective-permute-start | bytes 2359304 | tf_op jit(solution)/shard_map/ppermute | solution.py:42
  118.1 16.6 %copy-start = (bf16[8192,256]{1,0:T(8,128)(2,1)S(1)}, bf16[8192,256]{1,0:T(8,128)(2,1)}, u32[]{:S(2)}) copy-start(bf16[8192,256]{1,0:T(8,128)(2,1)} %prev.5) | copy-start | bytes 12582916
  128.4 10.5 %collective-permute-start.21 = (bf16[4,384,256]{2,1,0:T(8,128)(2,1)S(1)}, bf16[4,384,256]{2,1,0:T(8,128)(2,1)S(1)}, u32[]{:S(2)}, u32[]{:S(2)}) collective-permute-start(bf16[4,384,256]{2,1,0:T(8,128)(2,1)S(1)} %choose.3), channel_id=1, source_target_pairs={{0,16},{16,0},{32,48},{48,32},{64,80},{80,64},{96,112},{112,96},{1... | collective-permute-start | bytes 2359304 | tf_op jit(solution)/shard_map/ppermute | solution.py:42
  132.0 2.6 %collective-permute-start.23 = (bf16[4,256,256]{2,1,0:T(8,128)(2,1)S(1)}, bf16[4,256,256]{2,1,0:T(8,128)(2,1)S(1)}, u32[]{:S(2)}, u32[]{:S(2)}) collective-permute-start(bf16[4,256,256]{2,1,0:T(8,128)(2,1)S(1)} %choose.5), channel_id=1, source_target_pairs={{0,16},{16,0},{32,48},{48,32},{64,80},{80,64},{96,112},{112,96},{1... | collective-permute-start | bytes 1572872 | tf_op jit(solution)/shard_map/ppermute | solution.py:42

commit v3 on v2

--- a/solution.py
+++ b/solution.py
@@ -12,7 +12,7 @@
 OWN = 4
 NV = 16
 NX = 4
-WAVES = (256, 384, 384)
+GROUPS = ((256,), (384, 384))
 STEPS = (0, 1, 3, 2)
 X1, X2, OPPOSITE, HERE = (1, 3), (3, 1), (2, 2), (0, 0)
 VMEM = pl.BlockSpec(memory_space=pltpu.VMEM)
@@ -70,6 +70,25 @@
         compiler_params=pltpu.CompilerParams(vmem_limit_bytes=limit),
         name=name,
     )(*args, *gates)
+
+
+def cut(amplitudes, at, rows, gates=()):
+    def kernel(source, *refs):
+        out, sem = refs[-2:]
+        copy = pltpu.make_async_copy(source.at[pl.ds(at, rows)], out, sem)
+        copy.start()
+        copy.wait()
+
+    return pl.pallas_call(
+        kernel,
+        out_shape=jax.ShapeDtypeStruct((rows, amplitudes.shape[1]), amplitudes.dtype),
+        in_specs=[ANY] * (1 + len(gates)),
+        out_specs=VMEM,
+        scratch_shapes=[pltpu.SemaphoreType.DMA],
+        cost_estimate=SHORT,
+        compiler_params=pltpu.CompilerParams(vmem_limit_bytes=4 << 20),
+        name="cut",
+    )(far_memory(amplitudes), *gates)
 
 
 def choose(pieces):
@@ -224,24 +243,27 @@
     sent, live = send_tiles.reshape(-1), pair_count.reshape(-1)
     weights = integrals[0]
 
-    held = [amplitudes] + [send(amplitudes, 0, d) for d in STEPS[1:]]
-    starts = [sum(WAVES[:i]) for i in range(len(WAVES))]
-    waves, gates = [], ()
-    for start, rows in zip(starts, WAVES):
-        packed = pack(meta, sent, held, start, rows, gates)
-        waves.append([send(v, 1, d) for v, d in zip(packed, STEPS[1:])])
-        gates = packed[:1]
-
-    moved_blocks, results = (), []
-    for got, start in zip(waves, starts):
-        lhs, *sends = ladder_far(meta, sent, live, held, got, start, weights, gates)
-        blocks = [flip_x(v, m) for v, m in zip(sends, (OPPOSITE, X1, X2))]
-        here = ladder_here(meta, lhs, weights, moved_blocks)
-        moved_blocks, gates = blocks, (here,)
-        results.append([(here, 0), (blocks[1], 0), (blocks[2], 0), (blocks[0], 0)])
+    waves, hops, gates, cut_gate, base = [], (), (), (), 0
+    for group in GROUPS:
+        own = cut(amplitudes, base, sum(group), cut_gate)
+        held = [own] + [send(own, 0, d) for d in STEPS[1:]]
+        start, received = 0, []
+        for rows in group:
+            packed = pack(meta, sent, held, start, rows, gates)
+            received.append([send(v, 1, d) for v, d in zip(packed, STEPS[1:])])
+            start, gates = start + rows, packed[:1]
+        start, cut_gate = 0, received[0]
+        for rows, got in zip(group, received):
+            lhs, *sends = ladder_far(meta, sent, live, held, got, start, weights, gates)
+            blocks = [flip_x(v, m) for v, m in zip(sends, (OPPOSITE, X1, X2))]
+            here = ladder_here(meta, lhs, weights, hops)
+            hops, gates = blocks, (here,)
+            waves.append(([(p, 0) for p in (here, blocks[1], blocks[2], blocks[0])], base + start))
+            start += rows
+        base += start
 
     total = None
-    for pieces, start in zip(results, starts):
+    for pieces, start in waves:
         swapped = swap(choose([(p, i + 1) for p, i in pieces]))
         total = add(meta, right_prev, pieces, swapped, total, start, n_rows)
     return total

time: 142 us -> 141 us (level)
  waiting for transfers between devices: 37.2 us -> 29.4 us
  starting transfers between devices: 42.1 us -> 48.8 us
  Pallas kernels: 52.9 us -> 50.9 us
  local copies, waits for them, and re-layouts: 8.8 us -> 10.4 us
    ppermute x9, waiting for transfers between devices: 6.71 us -> 0.56 us  [flip_x(): lax.ppermute(array, 'occ', [(o, o ^ 2 * masks[o % 2]) for o in range(2 *...]
    ppermute x3, starting transfers between devices: 8.39 us -> 14.4 us  [swap(): return lax.ppermute(array, 'occ', [(o, o ^ 1) for o in range(2 * NX)])]
    pallas_call x12, Pallas kernels: 46.3 us -> 42.3 us  [call(): pl.pallas_call(body, out_shape=[jax.ShapeDtypeStruct(shape, jnp.bfloat16)...]
    pallas_call x0 -> x2, Pallas kernels: none -> 2.1 us  [cut(): pl.pallas_call(kernel, out_shape=jax.ShapeDtypeStruct((rows, amplitudes.s...]
    ppermute x12 -> x15, waiting for transfers between devices: 27.9 us -> 26.4 us  [send(): return lax.ppermute(array, ('occ', 'vir'), pairs)]
    unnamed x21 -> x31, local copies, waits for them, and re-layouts: 8.58 us -> 9.52 us
    ppermute x12 -> x15, starting transfers between devices: 20.5 us -> 21.3 us  [send(): return lax.ppermute(array, ('occ', 'vir'), pairs)]
  transfers between devices with their start and end apart: 24 -> 27, of which waited for: 7 -> 8; matrix products, arithmetic and copies ran while one was open for 1% -> 1% of each run, Pallas kernels for 34% -> 32%
where the time goes in v3:
time: 141 us; the launch traced here: 140 us
  Pallas kernels  50.9 us (36%)
  starting transfers between devices  48.8 us (35%)
  waiting for transfers between devices  29.4 us (21%)
  local copies, waits for them, and re-layouts  10.4 us (7%)
    pallas_call x12, Pallas kernels, call(): pl.pallas_call(body, out_shape=[jax.ShapeDtypeStruct(shape, jnp.bfloat16)...  42.3 us
    ppermute x15, waiting for transfers between devices, send(): return lax.ppermute(array, ('occ', 'vir'), pairs)  26.4 us
    ppermute x15, starting transfers between devices, send(): return lax.ppermute(array, ('occ', 'vir'), pairs)  21.3 us
    ppermute x3, starting transfers between devices, swap(): return lax.ppermute(array, 'occ', [(o, o ^ 1) for o in range(2 * NX)])  14.4 us
    ppermute x9, starting transfers between devices, flip_x(): lax.ppermute(array, 'occ', [(o, o ^ 2 * masks[o % 2]) for o in range(2 *...  13.1 us
    unnamed x31, local copies, waits for them, and re-layouts  9.52 us
    pallas_call x3, Pallas kernels, add(): pl.pallas_call(kernel, out_shape=jax.ShapeDtypeStruct(prev.shape, jnp.flo...  6.56 us
  transfers between devices with their start and end apart: 27, of which 8 were waited for; matrix products, arithmetic and copies ran while one was open for 1% of the time, Pallas kernels for 32%

profile of v3, /device:TPU:1, one launch (start us, length us, event | category | flops | bytes accessed | tf_op | source)
XLA Modules:
  0.0 140.1 jit_solution(5778022848934457030)
XLA Ops:
  0.0 1.0 cut.2.refs_2_.refs_3_
  1.0 4.5 %collective-permute-start.2 = (bf16[256,512]{1,0:T(8,128)(2,1)S(1)}, bf16[256,512]{1,0:T(8,128)(2,1)S(1)}, u32[]{:S(2)}, u32[]{:S(2)}) collective-permute-start(bf16[256,512]{1,0:T(8,128)(2,1)S(1)} %cut.2.refs_2_.refs_3_), channel_id=1, source_target_pairs={{0,8},{1,9},{2,10},{3,11},{4,12},{5,13},{6,14},{7,15},{8,0},{9,1},... | collective-permute-start | bytes 786440 | tf_op jit(solution)/shard_map/ppermute | solution.py:34
  5.5 0.4 collective-permute-start.1
  5.9 1.0 collective-permute-start
  6.9 0.9 copy.8
  7.8 0.1 reshape.6.refs_1_
  8.0 0.1 pad_add_fusion.refs_0_.meta
  8.1 1.5 %collective-permute-done.2.refs_5_.refs_6_ = bf16[256,512]{1,0:T(8,128)(2,1)S(1)} collective-permute-done((bf16[256,512]{1,0:T(8,128)(2,1)S(1)}, bf16[256,512]{1,0:T(8,128)(2,1)S(1)}, u32[]{:S(2)}, u32[]{:S(2)}) %collective-permute-start.2) | collective-permute-done | bytes 262176 | tf_op jit(solution)/shard_map/ppermute | solution.py:34
  9.5 3.6 %collective-permute-done.1.refs_4_.refs_5_ = bf16[256,512]{1,0:T(8,128)(2,1)S(1)} collective-permute-done((bf16[256,512]{1,0:T(8,128)(2,1)S(1)}, bf16[256,512]{1,0:T(8,128)(2,1)S(1)}, u32[]{:S(2)}, u32[]{:S(2)}) %collective-permute-start.1) | collective-permute-done | bytes 262176 | tf_op jit(solution)/shard_map/ppermute | solution.py:34
  13.1 0.0 collective-permute-done.refs_3_.refs_4_
  13.1 0.9 pack.3
  14.0 2.5 %collective-permute-start.4 = (bf16[2,256,512]{2,1,0:T(8,128)(2,1)S(1)}, bf16[2,256,512]{2,1,0:T(8,128)(2,1)S(1)}, u32[]{:S(2)}, u32[]{:S(2)}) collective-permute-start(bf16[2,256,512]{2,1,0:T(8,128)(2,1)S(1)} %get-tuple-element.27), channel_id=1, source_target_pairs={{0,3},{1,0},{2,1},{3,2},{4,7},{5,4},{6,5},{7,6},{8,11},{9,8},{10,9... | collective-permute-start | bytes 1572872 | tf_op jit(solution)/shard_map/ppermute | solution.py:34
  16.5 0.5 collective-permute-start.5
  17.0 0.6 collective-permute-start.3
  17.6 10.7 %collective-permute-done.4.refs_1_.refs_8_ = bf16[2,256,512]{2,1,0:T(8,128)(2,1)S(1)} collective-permute-done((bf16[2,256,512]{2,1,0:T(8,128)(2,1)S(1)}, bf16[2,256,512]{2,1,0:T(8,128)(2,1)S(1)}, u32[]{:S(2)}, u32[]{:S(2)}) %collective-permute-start.4) | collective-permute-done | bytes 524320 | tf_op jit(solution)/shard_map/ppermute | solution.py:34
  28.3 3.7 %collective-permute-done.3.refs_0_.refs_7_ = bf16[2,256,512]{2,1,0:T(8,128)(2,1)S(1)} collective-permute-done((bf16[2,256,512]{2,1,0:T(8,128)(2,1)S(1)}, bf16[2,256,512]{2,1,0:T(8,128)(2,1)S(1)}, u32[]{:S(2)}, u32[]{:S(2)}) %collective-permute-start.3) | collective-permute-done | bytes 524320 | tf_op jit(solution)/shard_map/ppermute | solution.py:34
  32.0 1.1 cut.3.refs_2_.refs_3_
  33.2 0.8 copy-done.1
  34.0 0.8 copy-done.5
  34.8 2.2 %collective-permute-start.8 = (bf16[768,512]{1,0:T(8,128)(2,1)S(1)}, bf16[768,512]{1,0:T(8,128)(2,1)S(1)}, u32[]{:S(2)}, u32[]{:S(2)}) collective-permute-start(bf16[768,512]{1,0:T(8,128)(2,1)S(1)} %cut.3.refs_2_.refs_3_), channel_id=1, source_target_pairs={{0,8},{1,9},{2,10},{3,11},{4,12},{5,13},{6,14},{7,15},{8,0},{9,1},... | collective-permute-start | bytes 2359304 | tf_op jit(solution)/shard_map/ppermute | solution.py:34
  36.9 1.0 collective-permute-start.7
  37.9 0.5 collective-permute-start.6
  38.4 0.8 reshape.7.refs_2_
  39.2 1.0 copy-done.2
  40.2 1.0 copy-done.4
  41.2 1.0 copy-done.6
  42.3 0.9 copy-done.8
  43.2 0.9 copy-done.10
  44.2 0.9 copy-done.12
  45.1 1.0 copy-done.14
  46.2 7.3 %ladder_far.3 = (bf16[256,4096]{1,0:T(8,128)(2,1)S(1)}, bf16[2,256,256]{2,1,0:T(8,128)(2,1)S(1)}, bf16[2,256,256]{2,1,0:T(8,128)(2,1)S(1)}, bf16[2,256,256]{2,1,0:T(8,128)(2,1)S(1)}) custom-call(s32[3]{0:T(128)S(1)} %pad_add_fusion.refs_0_.meta, s32[512]{0:T(512)S(1)} %reshape.6.refs_1_, s32[256]{0:T(256)S(1)} %reshape.7.refs_2_, ...), custom_call_target="tpu_custom_call" | custom-call | bytes 1024 | tf_op jit(solution)/shard_map/ladder_far/pallas_call | solution.py:63
  53.4 4.0 %ladder_here.3.refs_6_.refs_0_.p0 = bf16[2,256,256]{2,1,0:T(8,128)(2,1)S(1)} custom-call(s32[3]{0:T(128)S(1)} %pad_add_fusion.refs_0_.meta, bf16[256,4096]{1,0:T(8,128)(2,1)S(1)} %get-tuple-element.29.refs_1_, bf16[4096,2048]{1,0:T(8,128)(2,1)} %bitcast.5), custom_call_target="tpu_custom_call" | custom-call | flops 1073741824 | bytes 1024 | tf_op jit(solution)/shard_map/ladder_here/pallas_call | solution.py:63
  57.5 1.0 pack.4
  58.5 0.7 collective-permute-start.13
  59.2 0.4 collective-permute-start.14
  59.6 0.5 collective-permute-start.12
  60.1 2.7 %collective-permute-start.15 = (bf16[2,256,256]{2,1,0:T(8,128)(2,1)S(1)}, bf16[2,256,256]{2,1,0:T(8,128)(2,1)S(1)}, u32[]{:S(2)}, u32[]{:S(2)}) collective-permute-start(bf16[2,256,256]{2,1,0:T(8,128)(2,1)S(1)} %get-tuple-element.37), channel_id=1, source_target_pairs={{0,64},{16,80},{32,96},{48,112},{64,0},{80,16},{96,32},{112,48},{1... | collective-permute-start | bytes 786440 | tf_op jit(solution)/shard_map/ppermute | solution.py:38
  62.9 1.0 pack.5
  63.9 2.4 %collective-permute-start.10 = (bf16[2,384,512]{2,1,0:T(8,128)(2,1)S(1)}, bf16[2,384,512]{2,1,0:T(8,128)(2,1)S(1)}, u32[]{:S(2)}, u32[]{:S(2)}) collective-permute-start(bf16[2,384,512]{2,1,0:T(8,128)(2,1)S(1)} %get-tuple-element.32), channel_id=1, source_target_pairs={{0,3},{1,0},{2,1},{3,2},{4,7},{5,4},{6,5},{7,6},{8,11},{9,8},{10,9... | collective-permute-start | bytes 2359304 | tf_op jit(solution)/shard_map/ppermute | solution.py:34
  66.3 0.5 collective-permute-done.15.refs_3_.p3
  66.9 4.1 %collective-permute-start.11 = (bf16[2,384,512]{2,1,0:T(8,128)(2,1)S(1)}, bf16[2,384,512]{2,1,0:T(8,128)(2,1)S(1)}, u32[]{:S(2)}, u32[]{:S(2)}) collective-permute-start(bf16[2,384,512]{2,1,0:T(8,128)(2,1)S(1)} %get-tuple-element.33), channel_id=1, source_target_pairs={{0,2},{1,3},{2,0},{3,1},{4,6},{5,7},{6,4},{7,5},{8,10},{9,11},{10,... | collective-permute-start | bytes 2359304 | tf_op jit(solution)/shard_map/ppermute | solution.py:34
  70.9 1.0 collective-permute-done.14.refs_9_
  71.9 2.5 %collective-permute-start.16 = (bf16[2,256,256]{2,1,0:T(8,128)(2,1)S(1)}, bf16[2,256,256]{2,1,0:T(8,128)(2,1)S(1)}, u32[]{:S(2)}, u32[]{:S(2)}) collective-permute-start(bf16[2,256,256]{2,1,0:T(8,128)(2,1)S(1)} %get-tuple-element.38), channel_id=1, source_target_pairs={{0,32},{16,112},{32,0},{48,80},{64,96},{80,48},{96,64},{112,16},{1... | collective-permute-start | bytes 786440 | tf_op jit(solution)/shard_map/ppermute | solution.py:38
  74.4 5.9 %collective-permute-done.12.refs_7_ = bf16[2,384,512]{2,1,0:T(8,128)(2,1)S(1)} collective-permute-done((bf16[2,384,512]{2,1,0:T(8,128)(2,1)S(1)}, bf16[2,384,512]{2,1,0:T(8,128)(2,1)S(1)}, u32[]{:S(2)}, u32[]{:S(2)}) %collective-permute-start.12) | collective-permute-done | bytes 786464 | tf_op jit(solution)/shard_map/ppermute | solution.py:34
  80.3 1.2 collective-permute-start.17
  81.5 9.2 %ladder_far.4 = (bf16[384,4096]{1,0:T(8,128)(2,1)S(1)}, bf16[2,384,256]{2,1,0:T(8,128)(2,1)S(1)}, bf16[2,384,256]{2,1,0:T(8,128)(2,1)S(1)}, bf16[2,384,256]{2,1,0:T(8,128)(2,1)S(1)}) custom-call(s32[3]{0:T(128)S(1)} %pad_add_fusion.refs_0_.meta, s32[512]{0:T(512)S(1)} %reshape.6.refs_1_, s32[256]{0:T(256)S(1)} %reshape.7.refs_2_, ...), custom_call_target="tpu_custom_call" | custom-call | bytes 1024 | tf_op jit(solution)/shard_map/ladder_far/pallas_call | solution.py:63
  90.8 2.5 %collective-permute-start.18 = (bf16[2,384,256]{2,1,0:T(8,128)(2,1)S(1)}, bf16[2,384,256]{2,1,0:T(8,128)(2,1)S(1)}, u32[]{:S(2)}, u32[]{:S(2)}) collective-permute-start(bf16[2,384,256]{2,1,0:T(8,128)(2,1)S(1)} %get-tuple-element.41), channel_id=1, source_target_pairs={{0,64},{16,80},{32,96},{48,112},{64,0},{80,16},{96,32},{112,48},{1... | collective-permute-start | bytes 1179656 | tf_op jit(solution)/shard_map/ppermute | solution.py:38
  93.3 0.2 collective-permute-start.19
  93.5 0.0 collective-permute-start.20
  93.5 4.6 %ladder_here.4.refs_11_.refs_0_.p0 = bf16[2,384,256]{2,1,0:T(8,128)(2,1)S(1)} custom-call(s32[3]{0:T(128)S(1)} %pad_add_fusion.refs_0_.meta, bf16[384,4096]{1,0:T(8,128)(2,1)S(1)} %get-tuple-element.36.refs_1_, bf16[4096,2048]{1,0:T(8,128)(2,1)} %bitcast.7, bf16[2,256,256]{2,1,0:T(8,128)(2,1)S(1)} %collective-permute-done.15.refs_3_.p3, ...), custom_call_target="tpu_custom_call" | custom-call | flops 1610612736 | bytes 1024 | tf_op jit(solution)/shard_map/ladder_here/pallas_call | solution.py:63
  98.1 9.2 %ladder_far.5 = (bf16[384,4096]{1,0:T(8,128)(2,1)S(1)}, bf16[2,384,256]{2,1,0:T(8,128)(2,1)S(1)}, bf16[2,384,256]{2,1,0:T(8,128)(2,1)S(1)}, bf16[2,384,256]{2,1,0:T(8,128)(2,1)S(1)}) custom-call(s32[3]{0:T(128)S(1)} %pad_add_fusion.refs_0_.meta, s32[512]{0:T(512)S(1)} %reshape.6.refs_1_, s32[256]{0:T(256)S(1)} %reshape.7.refs_2_, ...), custom_call_target="tpu_custom_call" | custom-call | bytes 1024 | tf_op jit(solution)/shard_map/ladder_far/pallas_call | solution.py:63
  107.4 2.6 %collective-permute-start.21 = (bf16[2,384,256]{2,1,0:T(8,128)(2,1)S(1)}, bf16[2,384,256]{2,1,0:T(8,128)(2,1)S(1)}, u32[]{:S(2)}, u32[]{:S(2)}) collective-permute-start(bf16[2,384,256]{2,1,0:T(8,128)(2,1)S(1)} %get-tuple-element.44), channel_id=1, source_target_pairs={{0,32},{16,112},{32,0},{48,80},{64,96},{80,48},{96,64},{112,16},{1... | collective-permute-start | bytes 1179656 | tf_op jit(solution)/shard_map/ppermute | solution.py:38
  109.9 0.9 collective-permute-start.22
  110.8 0.5 collective-permute-start.23
  111.3 0.1 choose.4
  111.4 8.3 %collective-permute-start.25 = (bf16[4,384,256]{2,1,0:T(8,128)(2,1)S(1)}, bf16[4,384,256]{2,1,0:T(8,128)(2,1)S(1)}, u32[]{:S(2)}, u32[]{:S(2)}) collective-permute-start(bf16[4,384,256]{2,1,0:T(8,128)(2,1)S(1)} %choose.4), channel_id=1, source_target_pairs={{0,16},{16,0},{32,48},{48,32},{64,80},{80,64},{96,112},{112,96},{1... | collective-permute-start | bytes 2359304 | tf_op jit(solution)/shard_map/ppermute | solution.py:42
  119.7 4.9 %ladder_here.5.refs_0_.p0 = bf16[2,384,256]{2,1,0:T(8,128)(2,1)S(1)} custom-call(s32[3]{0:T(128)S(1)} %pad_add_fusion.refs_0_.meta, bf16[384,4096]{1,0:T(8,128)(2,1)S(1)} %get-tuple-element.40.refs_1_, bf16[4096,2048]{1,0:T(8,128)(2,1)} %bitcast.9, bf16[2,384,256]{2,1,0:T(8,128)(2,1)S(1)} %collective-permute-done.18.refs_3_.p3, ...), custom_call_target="tpu_custom_call" | custom-call | flops 1610612736 | bytes 1024 | tf_op jit(solution)/shard_map/ladder_here/pallas_call | solution.py:63
  124.6 0.1 choose.3
  124.6 6.0 %collective-permute-start.24 = (bf16[4,384,256]{2,1,0:T(8,128)(2,1)S(1)}, bf16[4,384,256]{2,1,0:T(8,128)(2,1)S(1)}, u32[]{:S(2)}, u32[]{:S(2)}) collective-permute-start(bf16[4,384,256]{2,1,0:T(8,128)(2,1)S(1)} %choose.3), channel_id=1, source_target_pairs={{0,16},{16,0},{32,48},{48,32},{64,80},{80,64},{96,112},{112,96},{1... | collective-permute-start | bytes 2359304 | tf_op jit(solution)/shard_map/ppermute | solution.py:42
  130.7 0.1 collective-permute-start.26
  130.8 2.5 %collective-permute-done.26.swapped = bf16[4,256,256]{2,1,0:T(8,128)(2,1)S(1)} collective-permute-done((bf16[4,256,256]{2,1,0:T(8,128)(2,1)S(1)}, bf16[4,256,256]{2,1,0:T(8,128)(2,1)S(1)}, u32[]{:S(2)}, u32[]{:S(2)}) %collective-permute-start.26) | collective-permute-done | bytes 524320 | tf_op jit(solution)/shard_map/ppermute | solution.py:42
  133.3 1.9 %residual.3.refs_0_ = f32[8192,256]{1,0:T(8,128)} custom-call(s32[3]{0:T(128)S(1)} %pad_add_fusion.refs_0_.meta, bf16[8192,256]{1,0:T(8,128)(2,1)S(1)} %copy-done, bf16[2,256,256]{2,1,0:T(8,128)(2,1)S(1)} %ladder_here.3.refs_6_.refs_0_.p0, bf16[2,256,256]{2,1,0:T(8,128)(2,1)S(1)} %collective-permute-done.16.refs_4_.refs_1_.p1, ...), custom_call_target="tpu_custom_call" | custom-call | bytes 1024 | tf_op jit(solution)/shard_map/residual/pallas_call | solution.py:223
  135.3 2.3 %residual.4.refs_0_ = f32[8192,256]{1,0:T(8,128)} custom-call(s32[3]{0:T(128)S(1)} %pad_add_fusion.refs_0_.meta, bf16[8192,256]{1,0:T(8,128)(2,1)S(1)} %copy-done, bf16[2,384,256]{2,1,0:T(8,128)(2,1)S(1)} %ladder_here.4.refs_11_.refs_0_.p0, bf16[2,384,256]{2,1,0:T(8,128)(2,1)S(1)} %collective-permute-done.19.refs_4_.refs_1_.p1, ...), custom_call_target="tpu_custom_call", output_to_operand_aliasing={{}: (7, {})} | custom-call | bytes 1024 | tf_op jit(solution)/shard_map/residual/pallas_call | solution.py:223
  137.6 2.3 %residual.5 = f32[8192,256]{1,0:T(8,128)} custom-call(s32[3]{0:T(128)S(1)} %pad_add_fusion.refs_0_.meta, bf16[8192,256]{1,0:T(8,128)(2,1)S(1)} %copy-done, bf16[2,384,256]{2,1,0:T(8,128)(2,1)S(1)} %ladder_here.5.refs_0_.p0, bf16[2,384,256]{2,1,0:T(8,128)(2,1)S(1)} %collective-permute-done.21.refs_1_.p1, ...), custom_call_target="tpu_custom_call", output_to_operand_aliasing={{}: (7, {})} | custom-call | bytes 1024 | tf_op jit(solution)/shard_map/residual/pallas_call | solution.py:223
  (41 shorter events, 0.1 us)
Async XLA Ops:
  1.0 8.6 %collective-permute-start.2 = (bf16[256,512]{1,0:T(8,128)(2,1)S(1)}, bf16[256,512]{1,0:T(8,128)(2,1)S(1)}, u32[]{:S(2)}, u32[]{:S(2)}) collective-permute-start(bf16[256,512]{1,0:T(8,128)(2,1)S(1)} %cut.2.refs_2_.refs_3_), channel_id=1, source_target_pairs={{0,8},{1,9},{2,10},{3,11},{4,12},{5,13},{6,14},{7,15},{8,0},{9,1},... | collective-permute-start | bytes 786440 | tf_op jit(solution)/shard_map/ppermute | solution.py:34
  5.5 7.6 %collective-permute-start.1 = (bf16[256,512]{1,0:T(8,128)(2,1)S(1)}, bf16[256,512]{1,0:T(8,128)(2,1)S(1)}, u32[]{:S(2)}, u32[]{:S(2)}) collective-permute-start(bf16[256,512]{1,0:T(8,128)(2,1)S(1)} %cut.2.refs_2_.refs_3_), channel_id=1, source_target_pairs={{0,12},{1,13},{2,14},{3,15},{4,0},{5,1},{6,2},{7,3},{8,4},{9,5},{1... | collective-permute-start | bytes 786440 | tf_op jit(solution)/shard_map/ppermute | solution.py:34
  5.9 7.2 %collective-permute-start = (bf16[256,512]{1,0:T(8,128)(2,1)S(1)}, bf16[256,512]{1,0:T(8,128)(2,1)S(1)}, u32[]{:S(2)}, u32[]{:S(2)}) collective-permute-start(bf16[256,512]{1,0:T(8,128)(2,1)S(1)} %cut.2.refs_2_.refs_3_), channel_id=1, source_target_pairs={{0,4},{1,5},{2,6},{3,7},{4,8},{5,9},{6,10},{7,11},{8,12},{9,13},{1... | collective-permute-start | bytes 786440 | tf_op jit(solution)/shard_map/ppermute | solution.py:34
  9.5 18.8 %copy-start.7 = (bf16[256,512]{1,0:T(8,128)(2,1)}, bf16[256,512]{1,0:T(8,128)(2,1)S(1)}, u32[]{:S(2)}) copy-start(bf16[256,512]{1,0:T(8,128)(2,1)S(1)} %collective-permute-done.2.refs_5_.refs_6_) | copy-start | bytes 786436
  13.1 15.2 %copy-start.9 = (bf16[256,512]{1,0:T(8,128)(2,1)}, bf16[256,512]{1,0:T(8,128)(2,1)S(1)}, u32[]{:S(2)}) copy-start(bf16[256,512]{1,0:T(8,128)(2,1)S(1)} %collective-permute-done.1.refs_4_.refs_5_) | copy-start | bytes 786436
  13.1 15.2 %copy-start.11 = (bf16[256,512]{1,0:T(8,128)(2,1)}, bf16[256,512]{1,0:T(8,128)(2,1)S(1)}, u32[]{:S(2)}) copy-start(bf16[256,512]{1,0:T(8,128)(2,1)S(1)} %collective-permute-done.refs_3_.refs_4_) | copy-start | bytes 786436
  14.0 23.9 %copy-start.13 = (bf16[2,256,512]{2,1,0:T(8,128)(2,1)}, bf16[2,256,512]{2,1,0:T(8,128)(2,1)S(1)}, u32[]{:S(2)}) copy-start(bf16[2,256,512]{2,1,0:T(8,128)(2,1)S(1)} %get-tuple-element.26.refs_11_) | copy-start | bytes 1572868
  14.0 14.3 %collective-permute-start.4 = (bf16[2,256,512]{2,1,0:T(8,128)(2,1)S(1)}, bf16[2,256,512]{2,1,0:T(8,128)(2,1)S(1)}, u32[]{:S(2)}, u32[]{:S(2)}) collective-permute-start(bf16[2,256,512]{2,1,0:T(8,128)(2,1)S(1)} %get-tuple-element.27), channel_id=1, source_target_pairs={{0,3},{1,0},{2,1},{3,2},{4,7},{5,4},{6,5},{7,6},{8,11},{9,8},{10,9... | collective-permute-start | bytes 1572872 | tf_op jit(solution)/shard_map/ppermute | solution.py:34
  16.5 11.7 %collective-permute-start.5 = (bf16[2,256,512]{2,1,0:T(8,128)(2,1)S(1)}, bf16[2,256,512]{2,1,0:T(8,128)(2,1)S(1)}, u32[]{:S(2)}, u32[]{:S(2)}) collective-permute-start(bf16[2,256,512]{2,1,0:T(8,128)(2,1)S(1)} %get-tuple-element.28), channel_id=1, source_target_pairs={{0,2},{1,3},{2,0},{3,1},{4,6},{5,7},{6,4},{7,5},{8,10},{9,11},{10,... | collective-permute-start | bytes 1572872 | tf_op jit(solution)/shard_map/ppermute | solution.py:34
  17.0 15.0 %collective-permute-start.3 = (bf16[2,256,512]{2,1,0:T(8,128)(2,1)S(1)}, bf16[2,256,512]{2,1,0:T(8,128)(2,1)S(1)}, u32[]{:S(2)}, u32[]{:S(2)}) collective-permute-start(bf16[2,256,512]{2,1,0:T(8,128)(2,1)S(1)} %get-tuple-element.26.refs_11_), channel_id=1, source_target_pairs={{0,1},{1,2},{2,3},{3,0},{4,5},{5,6},{6,7},{7,4},{8,9},{9,10},{10,1... | collective-permute-start | bytes 1572872 | tf_op jit(solution)/shard_map/ppermute | solution.py:34
  28.3 8.6 %copy-start.3 = (bf16[2,256,512]{2,1,0:T(8,128)(2,1)}, bf16[2,256,512]{2,1,0:T(8,128)(2,1)S(1)}, u32[]{:S(2)}) copy-start(bf16[2,256,512]{2,1,0:T(8,128)(2,1)S(1)} %collective-permute-done.5.refs_2_.refs_9_) | copy-start | bytes 1572868
  33.1 0.8 copy-start.1
  34.0 0.8 copy-start.5
  34.8 22.7 %collective-permute-start.8 = (bf16[768,512]{1,0:T(8,128)(2,1)S(1)}, bf16[768,512]{1,0:T(8,128)(2,1)S(1)}, u32[]{:S(2)}, u32[]{:S(2)}) collective-permute-start(bf16[768,512]{1,0:T(8,128)(2,1)S(1)} %cut.3.refs_2_.refs_3_), channel_id=1, source_target_pairs={{0,8},{1,9},{2,10},{3,11},{4,12},{5,13},{6,14},{7,15},{8,0},{9,1},... | collective-permute-start | bytes 2359304 | tf_op jit(solution)/shard_map/ppermute | solution.py:34
  36.9 20.6 %collective-permute-start.7 = (bf16[768,512]{1,0:T(8,128)(2,1)S(1)}, bf16[768,512]{1,0:T(8,128)(2,1)S(1)}, u32[]{:S(2)}, u32[]{:S(2)}) collective-permute-start(bf16[768,512]{1,0:T(8,128)(2,1)S(1)} %cut.3.refs_2_.refs_3_), channel_id=1, source_target_pairs={{0,12},{1,13},{2,14},{3,15},{4,0},{5,1},{6,2},{7,3},{8,4},{9,5},{1... | collective-permute-start | bytes 2359304 | tf_op jit(solution)/shard_map/ppermute | solution.py:34
  37.9 19.6 %collective-permute-start.6 = (bf16[768,512]{1,0:T(8,128)(2,1)S(1)}, bf16[768,512]{1,0:T(8,128)(2,1)S(1)}, u32[]{:S(2)}, u32[]{:S(2)}) collective-permute-start(bf16[768,512]{1,0:T(8,128)(2,1)S(1)} %cut.3.refs_2_.refs_3_), channel_id=1, source_target_pairs={{0,4},{1,5},{2,6},{3,7},{4,8},{5,9},{6,10},{7,11},{8,12},{9,13},{1... | collective-permute-start | bytes 2359304 | tf_op jit(solution)/shard_map/ppermute | solution.py:34
  39.2 1.0 copy-start.2
  40.2 1.0 copy-start.4
  41.2 1.0 copy-start.6
  42.3 0.9 copy-start.8
  43.2 0.9 copy-start.10
  44.2 0.9 copy-start.12
  45.1 1.0 copy-start.14
  58.5 12.4 %collective-permute-start.13 = (bf16[2,384,512]{2,1,0:T(8,128)(2,1)S(1)}, bf16[2,384,512]{2,1,0:T(8,128)(2,1)S(1)}, u32[]{:S(2)}, u32[]{:S(2)}) collective-permute-start(bf16[2,384,512]{2,1,0:T(8,128)(2,1)S(1)} %get-tuple-element.34), channel_id=1, source_target_pairs={{0,3},{1,0},{2,1},{3,2},{4,7},{5,4},{6,5},{7,6},{8,11},{9,8},{10,9... | collective-permute-start | bytes 2359304 | tf_op jit(solution)/shard_map/ppermute | solution.py:34
  59.2 12.7 %collective-permute-start.14 = (bf16[2,384,512]{2,1,0:T(8,128)(2,1)S(1)}, bf16[2,384,512]{2,1,0:T(8,128)(2,1)S(1)}, u32[]{:S(2)}, u32[]{:S(2)}) collective-permute-start(bf16[2,384,512]{2,1,0:T(8,128)(2,1)S(1)} %get-tuple-element.35), channel_id=1, source_target_pairs={{0,2},{1,3},{2,0},{3,1},{4,6},{5,7},{6,4},{7,5},{8,10},{9,11},{10,... | collective-permute-start | bytes 2359304 | tf_op jit(solution)/shard_map/ppermute | solution.py:34
  59.6 20.7 %collective-permute-start.12 = (bf16[2,384,512]{2,1,0:T(8,128)(2,1)S(1)}, bf16[2,384,512]{2,1,0:T(8,128)(2,1)S(1)}, u32[]{:S(2)}, u32[]{:S(2)}) collective-permute-start(bf16[2,384,512]{2,1,0:T(8,128)(2,1)S(1)} %get-tuple-element.30.refs_6_), channel_id=1, source_target_pairs={{0,1},{1,2},{2,3},{3,0},{4,5},{5,6},{6,7},{7,4},{8,9},{9,10},{10,1... | collective-permute-start | bytes 2359304 | tf_op jit(solution)/shard_map/ppermute | solution.py:34
  60.1 6.7 %collective-permute-start.15 = (bf16[2,256,256]{2,1,0:T(8,128)(2,1)S(1)}, bf16[2,256,256]{2,1,0:T(8,128)(2,1)S(1)}, u32[]{:S(2)}, u32[]{:S(2)}) collective-permute-start(bf16[2,256,256]{2,1,0:T(8,128)(2,1)S(1)} %get-tuple-element.37), channel_id=1, source_target_pairs={{0,64},{16,80},{32,96},{48,112},{64,0},{80,16},{96,32},{112,48},{1... | collective-permute-start | bytes 786440 | tf_op jit(solution)/shard_map/ppermute | solution.py:38
  63.9 29.6 %collective-permute-start.10 = (bf16[2,384,512]{2,1,0:T(8,128)(2,1)S(1)}, bf16[2,384,512]{2,1,0:T(8,128)(2,1)S(1)}, u32[]{:S(2)}, u32[]{:S(2)}) collective-permute-start(bf16[2,384,512]{2,1,0:T(8,128)(2,1)S(1)} %get-tuple-element.32), channel_id=1, source_target_pairs={{0,3},{1,0},{2,1},{3,2},{4,7},{5,4},{6,5},{7,6},{8,11},{9,8},{10,9... | collective-permute-start | bytes 2359304 | tf_op jit(solution)/shard_map/ppermute | solution.py:34
  66.9 31.3 %collective-permute-start.11 = (bf16[2,384,512]{2,1,0:T(8,128)(2,1)S(1)}, bf16[2,384,512]{2,1,0:T(8,128)(2,1)S(1)}, u32[]{:S(2)}, u32[]{:S(2)}) collective-permute-start(bf16[2,384,512]{2,1,0:T(8,128)(2,1)S(1)} %get-tuple-element.33), channel_id=1, source_target_pairs={{0,2},{1,3},{2,0},{3,1},{4,6},{5,7},{6,4},{7,5},{8,10},{9,11},{10,... | collective-permute-start | bytes 2359304 | tf_op jit(solution)/shard_map/ppermute | solution.py:34
  70.9 27.2 %collective-permute-start.9 = (bf16[2,384,512]{2,1,0:T(8,128)(2,1)S(1)}, bf16[2,384,512]{2,1,0:T(8,128)(2,1)S(1)}, u32[]{:S(2)}, u32[]{:S(2)}) collective-permute-start(bf16[2,384,512]{2,1,0:T(8,128)(2,1)S(1)} %get-tuple-element.31.refs_11_), channel_id=1, source_target_pairs={{0,1},{1,2},{2,3},{3,0},{4,5},{5,6},{6,7},{7,4},{8,9},{9,10},{10,1... | collective-permute-start | bytes 2359304 | tf_op jit(solution)/shard_map/ppermute | solution.py:34
  71.9 18.8 %collective-permute-start.16 = (bf16[2,256,256]{2,1,0:T(8,128)(2,1)S(1)}, bf16[2,256,256]{2,1,0:T(8,128)(2,1)S(1)}, u32[]{:S(2)}, u32[]{:S(2)}) collective-permute-start(bf16[2,256,256]{2,1,0:T(8,128)(2,1)S(1)} %get-tuple-element.38), channel_id=1, source_target_pairs={{0,32},{16,112},{32,0},{48,80},{64,96},{80,48},{96,64},{112,16},{1... | collective-permute-start | bytes 786440 | tf_op jit(solution)/shard_map/ppermute | solution.py:38
  80.3 13.0 %collective-permute-start.17 = (bf16[2,256,256]{2,1,0:T(8,128)(2,1)S(1)}, bf16[2,256,256]{2,1,0:T(8,128)(2,1)S(1)}, u32[]{:S(2)}, u32[]{:S(2)}) collective-permute-start(bf16[2,256,256]{2,1,0:T(8,128)(2,1)S(1)} %get-tuple-element.39), channel_id=1, source_target_pairs={{0,96},{16,48},{32,64},{48,16},{64,32},{80,112},{96,0},{112,80},{1... | collective-permute-start | bytes 786440 | tf_op jit(solution)/shard_map/ppermute | solution.py:38
  90.8 20.0 %collective-permute-start.18 = (bf16[2,384,256]{2,1,0:T(8,128)(2,1)S(1)}, bf16[2,384,256]{2,1,0:T(8,128)(2,1)S(1)}, u32[]{:S(2)}, u32[]{:S(2)}) collective-permute-start(bf16[2,384,256]{2,1,0:T(8,128)(2,1)S(1)} %get-tuple-element.41), channel_id=1, source_target_pairs={{0,64},{16,80},{32,96},{48,112},{64,0},{80,16},{96,32},{112,48},{1... | collective-permute-start | bytes 1179656 | tf_op jit(solution)/shard_map/ppermute | solution.py:38
  93.3 18.0 %collective-permute-start.19 = (bf16[2,384,256]{2,1,0:T(8,128)(2,1)S(1)}, bf16[2,384,256]{2,1,0:T(8,128)(2,1)S(1)}, u32[]{:S(2)}, u32[]{:S(2)}) collective-permute-start(bf16[2,384,256]{2,1,0:T(8,128)(2,1)S(1)} %get-tuple-element.42), channel_id=1, source_target_pairs={{0,32},{16,112},{32,0},{48,80},{64,96},{80,48},{96,64},{112,16},{1... | collective-permute-start | bytes 1179656 | tf_op jit(solution)/shard_map/ppermute | solution.py:38
  93.5 17.8 %collective-permute-start.20 = (bf16[2,384,256]{2,1,0:T(8,128)(2,1)S(1)}, bf16[2,384,256]{2,1,0:T(8,128)(2,1)S(1)}, u32[]{:S(2)}, u32[]{:S(2)}) collective-permute-start(bf16[2,384,256]{2,1,0:T(8,128)(2,1)S(1)} %get-tuple-element.43), channel_id=1, source_target_pairs={{0,96},{16,48},{32,64},{48,16},{64,32},{80,112},{96,0},{112,80},{1... | collective-permute-start | bytes 1179656 | tf_op jit(solution)/shard_map/ppermute | solution.py:38
  107.4 17.2 %collective-permute-start.21 = (bf16[2,384,256]{2,1,0:T(8,128)(2,1)S(1)}, bf16[2,384,256]{2,1,0:T(8,128)(2,1)S(1)}, u32[]{:S(2)}, u32[]{:S(2)}) collective-permute-start(bf16[2,384,256]{2,1,0:T(8,128)(2,1)S(1)} %get-tuple-element.44), channel_id=1, source_target_pairs={{0,32},{16,112},{32,0},{48,80},{64,96},{80,48},{96,64},{112,16},{1... | collective-permute-start | bytes 1179656 | tf_op jit(solution)/shard_map/ppermute | solution.py:38
  109.9 14.6 %collective-permute-start.22 = (bf16[2,384,256]{2,1,0:T(8,128)(2,1)S(1)}, bf16[2,384,256]{2,1,0:T(8,128)(2,1)S(1)}, u32[]{:S(2)}, u32[]{:S(2)}) collective-permute-start(bf16[2,384,256]{2,1,0:T(8,128)(2,1)S(1)} %get-tuple-element.45), channel_id=1, source_target_pairs={{0,96},{16,48},{32,64},{48,16},{64,32},{80,112},{96,0},{112,80},{1... | collective-permute-start | bytes 1179656 | tf_op jit(solution)/shard_map/ppermute | solution.py:38
  110.8 13.8 %collective-permute-start.23 = (bf16[2,384,256]{2,1,0:T(8,128)(2,1)S(1)}, bf16[2,384,256]{2,1,0:T(8,128)(2,1)S(1)}, u32[]{:S(2)}, u32[]{:S(2)}) collective-permute-start(bf16[2,384,256]{2,1,0:T(8,128)(2,1)S(1)} %get-tuple-element.46), channel_id=1, source_target_pairs={{0,64},{16,80},{32,96},{48,112},{64,0},{80,16},{96,32},{112,48},{1... | collective-permute-start | bytes 1179656 | tf_op jit(solution)/shard_map/ppermute | solution.py:38
  111.4 23.9 %collective-permute-start.25 = (bf16[4,384,256]{2,1,0:T(8,128)(2,1)S(1)}, bf16[4,384,256]{2,1,0:T(8,128)(2,1)S(1)}, u32[]{:S(2)}, u32[]{:S(2)}) collective-permute-start(bf16[4,384,256]{2,1,0:T(8,128)(2,1)S(1)} %choose.4), channel_id=1, source_target_pairs={{0,16},{16,0},{32,48},{48,32},{64,80},{80,64},{96,112},{112,96},{1... | collective-permute-start | bytes 2359304 | tf_op jit(solution)/shard_map/ppermute | solution.py:42
  119.7 13.7 %copy-start = (bf16[8192,256]{1,0:T(8,128)(2,1)S(1)}, bf16[8192,256]{1,0:T(8,128)(2,1)}, u32[]{:S(2)}) copy-start(bf16[8192,256]{1,0:T(8,128)(2,1)} %prev.5) | copy-start | bytes 12582916
  124.6 13.0 %collective-permute-start.24 = (bf16[4,384,256]{2,1,0:T(8,128)(2,1)S(1)}, bf16[4,384,256]{2,1,0:T(8,128)(2,1)S(1)}, u32[]{:S(2)}, u32[]{:S(2)}) collective-permute-start(bf16[4,384,256]{2,1,0:T(8,128)(2,1)S(1)} %choose.3), channel_id=1, source_target_pairs={{0,16},{16,0},{32,48},{48,32},{64,80},{80,64},{96,112},{112,96},{1... | collective-permute-start | bytes 2359304 | tf_op jit(solution)/shard_map/ppermute | solution.py:42
  130.7 2.6 %collective-permute-start.26 = (bf16[4,256,256]{2,1,0:T(8,128)(2,1)S(1)}, bf16[4,256,256]{2,1,0:T(8,128)(2,1)S(1)}, u32[]{:S(2)}, u32[]{:S(2)}) collective-permute-start(bf16[4,256,256]{2,1,0:T(8,128)(2,1)S(1)} %choose.5), channel_id=1, source_target_pairs={{0,16},{16,0},{32,48},{48,32},{64,80},{80,64},{96,112},{112,96},{1... | collective-permute-start | bytes 1572872 | tf_op jit(solution)/shard_map/ppermute | solution.py:42

commit v4 on v3

--- a/solution.py
+++ b/solution.py
@@ -263,7 +263,7 @@
         base += start
 
     total = None
-    for pieces, start in waves:
+    for pieces, start in (waves[1], waves[0], *waves[2:]):
         swapped = swap(choose([(p, i + 1) for p, i in pieces]))
         total = add(meta, right_prev, pieces, swapped, total, start, n_rows)
     return total

time: 141 us -> 138 us (0.979)
  waiting for transfers between devices: 29.4 us -> 27.1 us
    ppermute x3, waiting for transfers between devices: 2.53 us -> 0.2 us  [swap(): return lax.ppermute(array, 'occ', [(o, o ^ 1) for o in range(2 * NX)])]
where the time goes in v4:
time: 138 us
  Pallas kernels  50.9 us (37%)
  starting transfers between devices  48.8 us (35%)
  waiting for transfers between devices  27.1 us (20%)
  local copies, waits for them, and re-layouts  10.4 us (8%)
    pallas_call x12, Pallas kernels, call(): pl.pallas_call(body, out_shape=[jax.ShapeDtypeStruct(shape, jnp.bfloat16)...  42.3 us
    ppermute x15, waiting for transfers between devices, send(): return lax.ppermute(array, ('occ', 'vir'), pairs)  26.4 us
    ppermute x15, starting transfers between devices, send(): return lax.ppermute(array, ('occ', 'vir'), pairs)  21.2 us
    ppermute x3, starting transfers between devices, swap(): return lax.ppermute(array, 'occ', [(o, o ^ 1) for o in range(2 * NX)])  14.4 us
    ppermute x9, starting transfers between devices, flip_x(): lax.ppermute(array, 'occ', [(o, o ^ 2 * masks[o % 2]) for o in range(2 *...  13.1 us
    unnamed x31, local copies, waits for them, and re-layouts  9.52 us
    pallas_call x3, Pallas kernels, add(): pl.pallas_call(kernel, out_shape=jax.ShapeDtypeStruct(prev.shape, jnp.flo...  6.56 us
  transfers between devices with their start and end apart: 27, of which 8 were waited for; matrix products, arithmetic and copies ran while one was open for 1% of the time, Pallas kernels for 32%

profile of v4, /device:TPU:1, one launch (start us, length us, event | category | flops | bytes accessed | tf_op | source)
XLA Modules:
  0.0 137.8 jit_solution(10603399675568141765)
XLA Ops:
  0.0 1.0 cut.2.refs_2_.refs_3_
  1.0 4.5 %collective-permute-start.2 = (bf16[256,512]{1,0:T(8,128)(2,1)S(1)}, bf16[256,512]{1,0:T(8,128)(2,1)S(1)}, u32[]{:S(2)}, u32[]{:S(2)}) collective-permute-start(bf16[256,512]{1,0:T(8,128)(2,1)S(1)} %cut.2.refs_2_.refs_3_), channel_id=1, source_target_pairs={{0,8},{1,9},{2,10},{3,11},{4,12},{5,13},{6,14},{7,15},{8,0},{9,1},... | collective-permute-start | bytes 786440 | tf_op jit(solution)/shard_map/ppermute | solution.py:34
  5.5 0.4 collective-permute-start.1
  5.9 1.0 collective-permute-start
  6.9 0.9 copy.8
  7.8 0.1 reshape.6.refs_1_
  8.0 0.1 pad_add_fusion.refs_0_.meta
  8.1 1.5 %collective-permute-done.2.refs_5_.refs_6_ = bf16[256,512]{1,0:T(8,128)(2,1)S(1)} collective-permute-done((bf16[256,512]{1,0:T(8,128)(2,1)S(1)}, bf16[256,512]{1,0:T(8,128)(2,1)S(1)}, u32[]{:S(2)}, u32[]{:S(2)}) %collective-permute-start.2) | collective-permute-done | bytes 262176 | tf_op jit(solution)/shard_map/ppermute | solution.py:34
  9.5 3.6 %collective-permute-done.1.refs_4_.refs_5_ = bf16[256,512]{1,0:T(8,128)(2,1)S(1)} collective-permute-done((bf16[256,512]{1,0:T(8,128)(2,1)S(1)}, bf16[256,512]{1,0:T(8,128)(2,1)S(1)}, u32[]{:S(2)}, u32[]{:S(2)}) %collective-permute-start.1) | collective-permute-done | bytes 262176 | tf_op jit(solution)/shard_map/ppermute | solution.py:34
  13.1 0.0 collective-permute-done.refs_3_.refs_4_
  13.1 0.9 pack.3
  14.0 2.5 %collective-permute-start.4 = (bf16[2,256,512]{2,1,0:T(8,128)(2,1)S(1)}, bf16[2,256,512]{2,1,0:T(8,128)(2,1)S(1)}, u32[]{:S(2)}, u32[]{:S(2)}) collective-permute-start(bf16[2,256,512]{2,1,0:T(8,128)(2,1)S(1)} %get-tuple-element.27), channel_id=1, source_target_pairs={{0,3},{1,0},{2,1},{3,2},{4,7},{5,4},{6,5},{7,6},{8,11},{9,8},{10,9... | collective-permute-start | bytes 1572872 | tf_op jit(solution)/shard_map/ppermute | solution.py:34
  16.5 0.5 collective-permute-start.5
  17.0 0.6 collective-permute-start.3
  17.6 10.7 %collective-permute-done.4.refs_1_.refs_8_ = bf16[2,256,512]{2,1,0:T(8,128)(2,1)S(1)} collective-permute-done((bf16[2,256,512]{2,1,0:T(8,128)(2,1)S(1)}, bf16[2,256,512]{2,1,0:T(8,128)(2,1)S(1)}, u32[]{:S(2)}, u32[]{:S(2)}) %collective-permute-start.4) | collective-permute-done | bytes 524320 | tf_op jit(solution)/shard_map/ppermute | solution.py:34
  28.3 3.7 %collective-permute-done.3.refs_0_.refs_7_ = bf16[2,256,512]{2,1,0:T(8,128)(2,1)S(1)} collective-permute-done((bf16[2,256,512]{2,1,0:T(8,128)(2,1)S(1)}, bf16[2,256,512]{2,1,0:T(8,128)(2,1)S(1)}, u32[]{:S(2)}, u32[]{:S(2)}) %collective-permute-start.3) | collective-permute-done | bytes 524320 | tf_op jit(solution)/shard_map/ppermute | solution.py:34
  32.0 1.1 cut.3.refs_2_.refs_3_
  33.2 0.8 copy-done.1
  34.0 0.8 copy-done.5
  34.8 2.2 %collective-permute-start.8 = (bf16[768,512]{1,0:T(8,128)(2,1)S(1)}, bf16[768,512]{1,0:T(8,128)(2,1)S(1)}, u32[]{:S(2)}, u32[]{:S(2)}) collective-permute-start(bf16[768,512]{1,0:T(8,128)(2,1)S(1)} %cut.3.refs_2_.refs_3_), channel_id=1, source_target_pairs={{0,8},{1,9},{2,10},{3,11},{4,12},{5,13},{6,14},{7,15},{8,0},{9,1},... | collective-permute-start | bytes 2359304 | tf_op jit(solution)/shard_map/ppermute | solution.py:34
  36.9 1.0 collective-permute-start.7
  37.9 0.5 collective-permute-start.6
  38.4 0.8 reshape.7.refs_2_
  39.2 1.0 copy-done.2
  40.2 1.0 copy-done.4
  41.2 1.0 copy-done.6
  42.3 0.9 copy-done.8
  43.2 0.9 copy-done.10
  44.2 0.9 copy-done.12
  45.1 1.0 copy-done.14
  46.2 7.3 %ladder_far.3 = (bf16[256,4096]{1,0:T(8,128)(2,1)S(1)}, bf16[2,256,256]{2,1,0:T(8,128)(2,1)S(1)}, bf16[2,256,256]{2,1,0:T(8,128)(2,1)S(1)}, bf16[2,256,256]{2,1,0:T(8,128)(2,1)S(1)}) custom-call(s32[3]{0:T(128)S(1)} %pad_add_fusion.refs_0_.meta, s32[512]{0:T(512)S(1)} %reshape.6.refs_1_, s32[256]{0:T(256)S(1)} %reshape.7.refs_2_, ...), custom_call_target="tpu_custom_call" | custom-call | bytes 1024 | tf_op jit(solution)/shard_map/ladder_far/pallas_call | solution.py:63
  53.4 4.0 %ladder_here.3.refs_6_.refs_0_.p0 = bf16[2,256,256]{2,1,0:T(8,128)(2,1)S(1)} custom-call(s32[3]{0:T(128)S(1)} %pad_add_fusion.refs_0_.meta, bf16[256,4096]{1,0:T(8,128)(2,1)S(1)} %get-tuple-element.29.refs_1_, bf16[4096,2048]{1,0:T(8,128)(2,1)} %bitcast.5), custom_call_target="tpu_custom_call" | custom-call | flops 1073741824 | bytes 1024 | tf_op jit(solution)/shard_map/ladder_here/pallas_call | solution.py:63
  57.5 0.0 collective-permute-done.8.refs_5_.refs_6_
  57.5 1.0 pack.4
  58.5 0.7 collective-permute-start.13
  59.2 0.3 collective-permute-start.14
  59.6 0.5 collective-permute-start.12
  60.1 2.8 %collective-permute-start.15 = (bf16[2,256,256]{2,1,0:T(8,128)(2,1)S(1)}, bf16[2,256,256]{2,1,0:T(8,128)(2,1)S(1)}, u32[]{:S(2)}, u32[]{:S(2)}) collective-permute-start(bf16[2,256,256]{2,1,0:T(8,128)(2,1)S(1)} %get-tuple-element.37), channel_id=1, source_target_pairs={{0,64},{16,80},{32,96},{48,112},{64,0},{80,16},{96,32},{112,48},{1... | collective-permute-start | bytes 786440 | tf_op jit(solution)/shard_map/ppermute | solution.py:38
  62.9 1.0 pack.5
  63.9 2.4 %collective-permute-start.10 = (bf16[2,384,512]{2,1,0:T(8,128)(2,1)S(1)}, bf16[2,384,512]{2,1,0:T(8,128)(2,1)S(1)}, u32[]{:S(2)}, u32[]{:S(2)}) collective-permute-start(bf16[2,384,512]{2,1,0:T(8,128)(2,1)S(1)} %get-tuple-element.32), channel_id=1, source_target_pairs={{0,3},{1,0},{2,1},{3,2},{4,7},{5,4},{6,5},{7,6},{8,11},{9,8},{10,9... | collective-permute-start | bytes 2359304 | tf_op jit(solution)/shard_map/ppermute | solution.py:34
  66.3 0.5 collective-permute-done.15.refs_3_.p3
  66.8 4.1 %collective-permute-start.11 = (bf16[2,384,512]{2,1,0:T(8,128)(2,1)S(1)}, bf16[2,384,512]{2,1,0:T(8,128)(2,1)S(1)}, u32[]{:S(2)}, u32[]{:S(2)}) collective-permute-start(bf16[2,384,512]{2,1,0:T(8,128)(2,1)S(1)} %get-tuple-element.33), channel_id=1, source_target_pairs={{0,2},{1,3},{2,0},{3,1},{4,6},{5,7},{6,4},{7,5},{8,10},{9,11},{10,... | collective-permute-start | bytes 2359304 | tf_op jit(solution)/shard_map/ppermute | solution.py:34
  70.9 1.0 collective-permute-done.14.refs_9_
  71.9 2.5 %collective-permute-start.16 = (bf16[2,256,256]{2,1,0:T(8,128)(2,1)S(1)}, bf16[2,256,256]{2,1,0:T(8,128)(2,1)S(1)}, u32[]{:S(2)}, u32[]{:S(2)}) collective-permute-start(bf16[2,256,256]{2,1,0:T(8,128)(2,1)S(1)} %get-tuple-element.38), channel_id=1, source_target_pairs={{0,32},{16,112},{32,0},{48,80},{64,96},{80,48},{96,64},{112,16},{1... | collective-permute-start | bytes 786440 | tf_op jit(solution)/shard_map/ppermute | solution.py:38
  74.4 5.9 %collective-permute-done.12.refs_7_ = bf16[2,384,512]{2,1,0:T(8,128)(2,1)S(1)} collective-permute-done((bf16[2,384,512]{2,1,0:T(8,128)(2,1)S(1)}, bf16[2,384,512]{2,1,0:T(8,128)(2,1)S(1)}, u32[]{:S(2)}, u32[]{:S(2)}) %collective-permute-start.12) | collective-permute-done | bytes 786464 | tf_op jit(solution)/shard_map/ppermute | solution.py:34
  80.3 1.2 collective-permute-start.17
  81.5 9.2 %ladder_far.4 = (bf16[384,4096]{1,0:T(8,128)(2,1)S(1)}, bf16[2,384,256]{2,1,0:T(8,128)(2,1)S(1)}, bf16[2,384,256]{2,1,0:T(8,128)(2,1)S(1)}, bf16[2,384,256]{2,1,0:T(8,128)(2,1)S(1)}) custom-call(s32[3]{0:T(128)S(1)} %pad_add_fusion.refs_0_.meta, s32[512]{0:T(512)S(1)} %reshape.6.refs_1_, s32[256]{0:T(256)S(1)} %reshape.7.refs_2_, ...), custom_call_target="tpu_custom_call" | custom-call | bytes 1024 | tf_op jit(solution)/shard_map/ladder_far/pallas_call | solution.py:63
  90.8 2.5 %collective-permute-start.18 = (bf16[2,384,256]{2,1,0:T(8,128)(2,1)S(1)}, bf16[2,384,256]{2,1,0:T(8,128)(2,1)S(1)}, u32[]{:S(2)}, u32[]{:S(2)}) collective-permute-start(bf16[2,384,256]{2,1,0:T(8,128)(2,1)S(1)} %get-tuple-element.41), channel_id=1, source_target_pairs={{0,64},{16,80},{32,96},{48,112},{64,0},{80,16},{96,32},{112,48},{1... | collective-permute-start | bytes 1179656 | tf_op jit(solution)/shard_map/ppermute | solution.py:38
  93.3 0.2 collective-permute-start.19
  93.5 4.6 %ladder_here.4.refs_11_.refs_0_.p0 = bf16[2,384,256]{2,1,0:T(8,128)(2,1)S(1)} custom-call(s32[3]{0:T(128)S(1)} %pad_add_fusion.refs_0_.meta, bf16[384,4096]{1,0:T(8,128)(2,1)S(1)} %get-tuple-element.36.refs_1_, bf16[4096,2048]{1,0:T(8,128)(2,1)} %bitcast.7, bf16[2,256,256]{2,1,0:T(8,128)(2,1)S(1)} %collective-permute-done.15.refs_3_.p3, ...), custom_call_target="tpu_custom_call" | custom-call | flops 1610612736 | bytes 1024 | tf_op jit(solution)/shard_map/ladder_here/pallas_call | solution.py:63
  98.1 9.2 %ladder_far.5 = (bf16[384,4096]{1,0:T(8,128)(2,1)S(1)}, bf16[2,384,256]{2,1,0:T(8,128)(2,1)S(1)}, bf16[2,384,256]{2,1,0:T(8,128)(2,1)S(1)}, bf16[2,384,256]{2,1,0:T(8,128)(2,1)S(1)}) custom-call(s32[3]{0:T(128)S(1)} %pad_add_fusion.refs_0_.meta, s32[512]{0:T(512)S(1)} %reshape.6.refs_1_, s32[256]{0:T(256)S(1)} %reshape.7.refs_2_, ...), custom_call_target="tpu_custom_call" | custom-call | bytes 1024 | tf_op jit(solution)/shard_map/ladder_far/pallas_call | solution.py:63
  107.4 2.6 %collective-permute-start.21 = (bf16[2,384,256]{2,1,0:T(8,128)(2,1)S(1)}, bf16[2,384,256]{2,1,0:T(8,128)(2,1)S(1)}, u32[]{:S(2)}, u32[]{:S(2)}) collective-permute-start(bf16[2,384,256]{2,1,0:T(8,128)(2,1)S(1)} %get-tuple-element.44), channel_id=1, source_target_pairs={{0,32},{16,112},{32,0},{48,80},{64,96},{80,48},{96,64},{112,16},{1... | collective-permute-start | bytes 1179656 | tf_op jit(solution)/shard_map/ppermute | solution.py:38
  109.9 0.9 collective-permute-start.22
  110.8 0.5 collective-permute-start.23
  111.3 0.1 choose.5
  111.4 8.3 %collective-permute-start.26 = (bf16[4,384,256]{2,1,0:T(8,128)(2,1)S(1)}, bf16[4,384,256]{2,1,0:T(8,128)(2,1)S(1)}, u32[]{:S(2)}, u32[]{:S(2)}) collective-permute-start(bf16[4,384,256]{2,1,0:T(8,128)(2,1)S(1)} %choose.5), channel_id=1, source_target_pairs={{0,16},{16,0},{32,48},{48,32},{64,80},{80,64},{96,112},{112,96},{1... | collective-permute-start | bytes 2359304 | tf_op jit(solution)/shard_map/ppermute | solution.py:42
  119.7 4.9 %ladder_here.5.refs_0_.p0 = bf16[2,384,256]{2,1,0:T(8,128)(2,1)S(1)} custom-call(s32[3]{0:T(128)S(1)} %pad_add_fusion.refs_0_.meta, bf16[384,4096]{1,0:T(8,128)(2,1)S(1)} %get-tuple-element.40.refs_1_, bf16[4096,2048]{1,0:T(8,128)(2,1)} %bitcast.9, bf16[2,384,256]{2,1,0:T(8,128)(2,1)S(1)} %collective-permute-done.18.refs_3_.p3, ...), custom_call_target="tpu_custom_call" | custom-call | flops 1610612736 | bytes 1024 | tf_op jit(solution)/shard_map/ladder_here/pallas_call | solution.py:63
  124.6 0.1 choose.3
  124.6 6.0 %collective-permute-start.24 = (bf16[4,384,256]{2,1,0:T(8,128)(2,1)S(1)}, bf16[4,384,256]{2,1,0:T(8,128)(2,1)S(1)}, u32[]{:S(2)}, u32[]{:S(2)}) collective-permute-start(bf16[4,384,256]{2,1,0:T(8,128)(2,1)S(1)} %choose.3), channel_id=1, source_target_pairs={{0,16},{16,0},{32,48},{48,32},{64,80},{80,64},{96,112},{112,96},{1... | collective-permute-start | bytes 2359304 | tf_op jit(solution)/shard_map/ppermute | solution.py:42
  130.7 0.1 collective-permute-start.25
  130.8 2.3 %residual.3.refs_0_ = f32[8192,256]{1,0:T(8,128)} custom-call(s32[3]{0:T(128)S(1)} %pad_add_fusion.refs_0_.meta, bf16[8192,256]{1,0:T(8,128)(2,1)S(1)} %copy-done, bf16[2,384,256]{2,1,0:T(8,128)(2,1)S(1)} %ladder_here.4.refs_11_.refs_0_.p0, bf16[2,384,256]{2,1,0:T(8,128)(2,1)S(1)} %collective-permute-done.19.refs_4_.refs_1_.p1, ...), custom_call_target="tpu_custom_call" | custom-call | bytes 1024 | tf_op jit(solution)/shard_map/residual/pallas_call | solution.py:223
  133.1 0.2 collective-permute-done.25.swapped
  133.3 1.9 %residual.4.refs_0_ = f32[8192,256]{1,0:T(8,128)} custom-call(s32[3]{0:T(128)S(1)} %pad_add_fusion.refs_0_.meta, bf16[8192,256]{1,0:T(8,128)(2,1)S(1)} %copy-done, bf16[2,256,256]{2,1,0:T(8,128)(2,1)S(1)} %ladder_here.3.refs_6_.refs_0_.p0, bf16[2,256,256]{2,1,0:T(8,128)(2,1)S(1)} %collective-permute-done.16.refs_4_.refs_1_.p1, ...), custom_call_target="tpu_custom_call", output_to_operand_aliasing={{}: (7, {})} | custom-call | bytes 1024 | tf_op jit(solution)/shard_map/residual/pallas_call | solution.py:223
  135.3 2.3 %residual.5 = f32[8192,256]{1,0:T(8,128)} custom-call(s32[3]{0:T(128)S(1)} %pad_add_fusion.refs_0_.meta, bf16[8192,256]{1,0:T(8,128)(2,1)S(1)} %copy-done, bf16[2,384,256]{2,1,0:T(8,128)(2,1)S(1)} %ladder_here.5.refs_0_.p0, bf16[2,384,256]{2,1,0:T(8,128)(2,1)S(1)} %collective-permute-done.21.refs_1_.p1, ...), custom_call_target="tpu_custom_call", output_to_operand_aliasing={{}: (7, {})} | custom-call | bytes 1024 | tf_op jit(solution)/shard_map/residual/pallas_call | solution.py:223
  (41 shorter events, 0.1 us)
Async XLA Ops:
  1.0 8.6 %collective-permute-start.2 = (bf16[256,512]{1,0:T(8,128)(2,1)S(1)}, bf16[256,512]{1,0:T(8,128)(2,1)S(1)}, u32[]{:S(2)}, u32[]{:S(2)}) collective-permute-start(bf16[256,512]{1,0:T(8,128)(2,1)S(1)} %cut.2.refs_2_.refs_3_), channel_id=1, source_target_pairs={{0,8},{1,9},{2,10},{3,11},{4,12},{5,13},{6,14},{7,15},{8,0},{9,1},... | collective-permute-start | bytes 786440 | tf_op jit(solution)/shard_map/ppermute | solution.py:34
  5.5 7.6 %collective-permute-start.1 = (bf16[256,512]{1,0:T(8,128)(2,1)S(1)}, bf16[256,512]{1,0:T(8,128)(2,1)S(1)}, u32[]{:S(2)}, u32[]{:S(2)}) collective-permute-start(bf16[256,512]{1,0:T(8,128)(2,1)S(1)} %cut.2.refs_2_.refs_3_), channel_id=1, source_target_pairs={{0,12},{1,13},{2,14},{3,15},{4,0},{5,1},{6,2},{7,3},{8,4},{9,5},{1... | collective-permute-start | bytes 786440 | tf_op jit(solution)/shard_map/ppermute | solution.py:34
  5.9 7.2 %collective-permute-start = (bf16[256,512]{1,0:T(8,128)(2,1)S(1)}, bf16[256,512]{1,0:T(8,128)(2,1)S(1)}, u32[]{:S(2)}, u32[]{:S(2)}) collective-permute-start(bf16[256,512]{1,0:T(8,128)(2,1)S(1)} %cut.2.refs_2_.refs_3_), channel_id=1, source_target_pairs={{0,4},{1,5},{2,6},{3,7},{4,8},{5,9},{6,10},{7,11},{8,12},{9,13},{1... | collective-permute-start | bytes 786440 | tf_op jit(solution)/shard_map/ppermute | solution.py:34
  9.5 18.8 %copy-start.7 = (bf16[256,512]{1,0:T(8,128)(2,1)}, bf16[256,512]{1,0:T(8,128)(2,1)S(1)}, u32[]{:S(2)}) copy-start(bf16[256,512]{1,0:T(8,128)(2,1)S(1)} %collective-permute-done.2.refs_5_.refs_6_) | copy-start | bytes 786436
  13.1 15.2 %copy-start.9 = (bf16[256,512]{1,0:T(8,128)(2,1)}, bf16[256,512]{1,0:T(8,128)(2,1)S(1)}, u32[]{:S(2)}) copy-start(bf16[256,512]{1,0:T(8,128)(2,1)S(1)} %collective-permute-done.1.refs_4_.refs_5_) | copy-start | bytes 786436
  13.1 15.2 %copy-start.11 = (bf16[256,512]{1,0:T(8,128)(2,1)}, bf16[256,512]{1,0:T(8,128)(2,1)S(1)}, u32[]{:S(2)}) copy-start(bf16[256,512]{1,0:T(8,128)(2,1)S(1)} %collective-permute-done.refs_3_.refs_4_) | copy-start | bytes 786436
  14.0 23.9 %copy-start.13 = (bf16[2,256,512]{2,1,0:T(8,128)(2,1)}, bf16[2,256,512]{2,1,0:T(8,128)(2,1)S(1)}, u32[]{:S(2)}) copy-start(bf16[2,256,512]{2,1,0:T(8,128)(2,1)S(1)} %get-tuple-element.26.refs_11_) | copy-start | bytes 1572868
  14.0 14.3 %collective-permute-start.4 = (bf16[2,256,512]{2,1,0:T(8,128)(2,1)S(1)}, bf16[2,256,512]{2,1,0:T(8,128)(2,1)S(1)}, u32[]{:S(2)}, u32[]{:S(2)}) collective-permute-start(bf16[2,256,512]{2,1,0:T(8,128)(2,1)S(1)} %get-tuple-element.27), channel_id=1, source_target_pairs={{0,3},{1,0},{2,1},{3,2},{4,7},{5,4},{6,5},{7,6},{8,11},{9,8},{10,9... | collective-permute-start | bytes 1572872 | tf_op jit(solution)/shard_map/ppermute | solution.py:34
  16.5 11.7 %collective-permute-start.5 = (bf16[2,256,512]{2,1,0:T(8,128)(2,1)S(1)}, bf16[2,256,512]{2,1,0:T(8,128)(2,1)S(1)}, u32[]{:S(2)}, u32[]{:S(2)}) collective-permute-start(bf16[2,256,512]{2,1,0:T(8,128)(2,1)S(1)} %get-tuple-element.28), channel_id=1, source_target_pairs={{0,2},{1,3},{2,0},{3,1},{4,6},{5,7},{6,4},{7,5},{8,10},{9,11},{10,... | collective-permute-start | bytes 1572872 | tf_op jit(solution)/shard_map/ppermute | solution.py:34
  17.0 15.0 %collective-permute-start.3 = (bf16[2,256,512]{2,1,0:T(8,128)(2,1)S(1)}, bf16[2,256,512]{2,1,0:T(8,128)(2,1)S(1)}, u32[]{:S(2)}, u32[]{:S(2)}) collective-permute-start(bf16[2,256,512]{2,1,0:T(8,128)(2,1)S(1)} %get-tuple-element.26.refs_11_), channel_id=1, source_target_pairs={{0,1},{1,2},{2,3},{3,0},{4,5},{5,6},{6,7},{7,4},{8,9},{9,10},{10,1... | collective-permute-start | bytes 1572872 | tf_op jit(solution)/shard_map/ppermute | solution.py:34
  28.3 8.6 %copy-start.3 = (bf16[2,256,512]{2,1,0:T(8,128)(2,1)}, bf16[2,256,512]{2,1,0:T(8,128)(2,1)S(1)}, u32[]{:S(2)}) copy-start(bf16[2,256,512]{2,1,0:T(8,128)(2,1)S(1)} %collective-permute-done.5.refs_2_.refs_9_) | copy-start | bytes 1572868
  33.1 0.8 copy-start.1
  34.0 0.8 copy-start.5
  34.8 22.7 %collective-permute-start.8 = (bf16[768,512]{1,0:T(8,128)(2,1)S(1)}, bf16[768,512]{1,0:T(8,128)(2,1)S(1)}, u32[]{:S(2)}, u32[]{:S(2)}) collective-permute-start(bf16[768,512]{1,0:T(8,128)(2,1)S(1)} %cut.3.refs_2_.refs_3_), channel_id=1, source_target_pairs={{0,8},{1,9},{2,10},{3,11},{4,12},{5,13},{6,14},{7,15},{8,0},{9,1},... | collective-permute-start | bytes 2359304 | tf_op jit(solution)/shard_map/ppermute | solution.py:34
  36.9 20.6 %collective-permute-start.7 = (bf16[768,512]{1,0:T(8,128)(2,1)S(1)}, bf16[768,512]{1,0:T(8,128)(2,1)S(1)}, u32[]{:S(2)}, u32[]{:S(2)}) collective-permute-start(bf16[768,512]{1,0:T(8,128)(2,1)S(1)} %cut.3.refs_2_.refs_3_), channel_id=1, source_target_pairs={{0,12},{1,13},{2,14},{3,15},{4,0},{5,1},{6,2},{7,3},{8,4},{9,5},{1... | collective-permute-start | bytes 2359304 | tf_op jit(solution)/shard_map/ppermute | solution.py:34
  37.9 19.6 %collective-permute-start.6 = (bf16[768,512]{1,0:T(8,128)(2,1)S(1)}, bf16[768,512]{1,0:T(8,128)(2,1)S(1)}, u32[]{:S(2)}, u32[]{:S(2)}) collective-permute-start(bf16[768,512]{1,0:T(8,128)(2,1)S(1)} %cut.3.refs_2_.refs_3_), channel_id=1, source_target_pairs={{0,4},{1,5},{2,6},{3,7},{4,8},{5,9},{6,10},{7,11},{8,12},{9,13},{1... | collective-permute-start | bytes 2359304 | tf_op jit(solution)/shard_map/ppermute | solution.py:34
  39.2 1.0 copy-start.2
  40.2 1.0 copy-start.4
  41.2 1.0 copy-start.6
  42.3 0.9 copy-start.8
  43.2 0.9 copy-start.10
  44.2 0.9 copy-start.12
  45.1 1.0 copy-start.14
  58.5 12.4 %collective-permute-start.13 = (bf16[2,384,512]{2,1,0:T(8,128)(2,1)S(1)}, bf16[2,384,512]{2,1,0:T(8,128)(2,1)S(1)}, u32[]{:S(2)}, u32[]{:S(2)}) collective-permute-start(bf16[2,384,512]{2,1,0:T(8,128)(2,1)S(1)} %get-tuple-element.34), channel_id=1, source_target_pairs={{0,3},{1,0},{2,1},{3,2},{4,7},{5,4},{6,5},{7,6},{8,11},{9,8},{10,9... | collective-permute-start | bytes 2359304 | tf_op jit(solution)/shard_map/ppermute | solution.py:34
  59.2 12.7 %collective-permute-start.14 = (bf16[2,384,512]{2,1,0:T(8,128)(2,1)S(1)}, bf16[2,384,512]{2,1,0:T(8,128)(2,1)S(1)}, u32[]{:S(2)}, u32[]{:S(2)}) collective-permute-start(bf16[2,384,512]{2,1,0:T(8,128)(2,1)S(1)} %get-tuple-element.35), channel_id=1, source_target_pairs={{0,2},{1,3},{2,0},{3,1},{4,6},{5,7},{6,4},{7,5},{8,10},{9,11},{10,... | collective-permute-start | bytes 2359304 | tf_op jit(solution)/shard_map/ppermute | solution.py:34
  59.6 20.7 %collective-permute-start.12 = (bf16[2,384,512]{2,1,0:T(8,128)(2,1)S(1)}, bf16[2,384,512]{2,1,0:T(8,128)(2,1)S(1)}, u32[]{:S(2)}, u32[]{:S(2)}) collective-permute-start(bf16[2,384,512]{2,1,0:T(8,128)(2,1)S(1)} %get-tuple-element.30.refs_6_), channel_id=1, source_target_pairs={{0,1},{1,2},{2,3},{3,0},{4,5},{5,6},{6,7},{7,4},{8,9},{9,10},{10,1... | collective-permute-start | bytes 2359304 | tf_op jit(solution)/shard_map/ppermute | solution.py:34
  60.1 6.7 %collective-permute-start.15 = (bf16[2,256,256]{2,1,0:T(8,128)(2,1)S(1)}, bf16[2,256,256]{2,1,0:T(8,128)(2,1)S(1)}, u32[]{:S(2)}, u32[]{:S(2)}) collective-permute-start(bf16[2,256,256]{2,1,0:T(8,128)(2,1)S(1)} %get-tuple-element.37), channel_id=1, source_target_pairs={{0,64},{16,80},{32,96},{48,112},{64,0},{80,16},{96,32},{112,48},{1... | collective-permute-start | bytes 786440 | tf_op jit(solution)/shard_map/ppermute | solution.py:38
  63.9 29.6 %collective-permute-start.10 = (bf16[2,384,512]{2,1,0:T(8,128)(2,1)S(1)}, bf16[2,384,512]{2,1,0:T(8,128)(2,1)S(1)}, u32[]{:S(2)}, u32[]{:S(2)}) collective-permute-start(bf16[2,384,512]{2,1,0:T(8,128)(2,1)S(1)} %get-tuple-element.32), channel_id=1, source_target_pairs={{0,3},{1,0},{2,1},{3,2},{4,7},{5,4},{6,5},{7,6},{8,11},{9,8},{10,9... | collective-permute-start | bytes 2359304 | tf_op jit(solution)/shard_map/ppermute | solution.py:34
  66.8 31.3 %collective-permute-start.11 = (bf16[2,384,512]{2,1,0:T(8,128)(2,1)S(1)}, bf16[2,384,512]{2,1,0:T(8,128)(2,1)S(1)}, u32[]{:S(2)}, u32[]{:S(2)}) collective-permute-start(bf16[2,384,512]{2,1,0:T(8,128)(2,1)S(1)} %get-tuple-element.33), channel_id=1, source_target_pairs={{0,2},{1,3},{2,0},{3,1},{4,6},{5,7},{6,4},{7,5},{8,10},{9,11},{10,... | collective-permute-start | bytes 2359304 | tf_op jit(solution)/shard_map/ppermute | solution.py:34
  70.9 27.2 %collective-permute-start.9 = (bf16[2,384,512]{2,1,0:T(8,128)(2,1)S(1)}, bf16[2,384,512]{2,1,0:T(8,128)(2,1)S(1)}, u32[]{:S(2)}, u32[]{:S(2)}) collective-permute-start(bf16[2,384,512]{2,1,0:T(8,128)(2,1)S(1)} %get-tuple-element.31.refs_11_), channel_id=1, source_target_pairs={{0,1},{1,2},{2,3},{3,0},{4,5},{5,6},{6,7},{7,4},{8,9},{9,10},{10,1... | collective-permute-start | bytes 2359304 | tf_op jit(solution)/shard_map/ppermute | solution.py:34
  71.9 18.8 %collective-permute-start.16 = (bf16[2,256,256]{2,1,0:T(8,128)(2,1)S(1)}, bf16[2,256,256]{2,1,0:T(8,128)(2,1)S(1)}, u32[]{:S(2)}, u32[]{:S(2)}) collective-permute-start(bf16[2,256,256]{2,1,0:T(8,128)(2,1)S(1)} %get-tuple-element.38), channel_id=1, source_target_pairs={{0,32},{16,112},{32,0},{48,80},{64,96},{80,48},{96,64},{112,16},{1... | collective-permute-start | bytes 786440 | tf_op jit(solution)/shard_map/ppermute | solution.py:38
  80.3 13.0 %collective-permute-start.17 = (bf16[2,256,256]{2,1,0:T(8,128)(2,1)S(1)}, bf16[2,256,256]{2,1,0:T(8,128)(2,1)S(1)}, u32[]{:S(2)}, u32[]{:S(2)}) collective-permute-start(bf16[2,256,256]{2,1,0:T(8,128)(2,1)S(1)} %get-tuple-element.39), channel_id=1, source_target_pairs={{0,96},{16,48},{32,64},{48,16},{64,32},{80,112},{96,0},{112,80},{1... | collective-permute-start | bytes 786440 | tf_op jit(solution)/shard_map/ppermute | solution.py:38
  90.8 20.0 %collective-permute-start.18 = (bf16[2,384,256]{2,1,0:T(8,128)(2,1)S(1)}, bf16[2,384,256]{2,1,0:T(8,128)(2,1)S(1)}, u32[]{:S(2)}, u32[]{:S(2)}) collective-permute-start(bf16[2,384,256]{2,1,0:T(8,128)(2,1)S(1)} %get-tuple-element.41), channel_id=1, source_target_pairs={{0,64},{16,80},{32,96},{48,112},{64,0},{80,16},{96,32},{112,48},{1... | collective-permute-start | bytes 1179656 | tf_op jit(solution)/shard_map/ppermute | solution.py:38
  93.3 18.0 %collective-permute-start.19 = (bf16[2,384,256]{2,1,0:T(8,128)(2,1)S(1)}, bf16[2,384,256]{2,1,0:T(8,128)(2,1)S(1)}, u32[]{:S(2)}, u32[]{:S(2)}) collective-permute-start(bf16[2,384,256]{2,1,0:T(8,128)(2,1)S(1)} %get-tuple-element.42), channel_id=1, source_target_pairs={{0,32},{16,112},{32,0},{48,80},{64,96},{80,48},{96,64},{112,16},{1... | collective-permute-start | bytes 1179656 | tf_op jit(solution)/shard_map/ppermute | solution.py:38
  93.5 17.8 %collective-permute-start.20 = (bf16[2,384,256]{2,1,0:T(8,128)(2,1)S(1)}, bf16[2,384,256]{2,1,0:T(8,128)(2,1)S(1)}, u32[]{:S(2)}, u32[]{:S(2)}) collective-permute-start(bf16[2,384,256]{2,1,0:T(8,128)(2,1)S(1)} %get-tuple-element.43), channel_id=1, source_target_pairs={{0,96},{16,48},{32,64},{48,16},{64,32},{80,112},{96,0},{112,80},{1... | collective-permute-start | bytes 1179656 | tf_op jit(solution)/shard_map/ppermute | solution.py:38
  107.4 17.2 %collective-permute-start.21 = (bf16[2,384,256]{2,1,0:T(8,128)(2,1)S(1)}, bf16[2,384,256]{2,1,0:T(8,128)(2,1)S(1)}, u32[]{:S(2)}, u32[]{:S(2)}) collective-permute-start(bf16[2,384,256]{2,1,0:T(8,128)(2,1)S(1)} %get-tuple-element.44), channel_id=1, source_target_pairs={{0,32},{16,112},{32,0},{48,80},{64,96},{80,48},{96,64},{112,16},{1... | collective-permute-start | bytes 1179656 | tf_op jit(solution)/shard_map/ppermute | solution.py:38
  109.9 14.6 %collective-permute-start.22 = (bf16[2,384,256]{2,1,0:T(8,128)(2,1)S(1)}, bf16[2,384,256]{2,1,0:T(8,128)(2,1)S(1)}, u32[]{:S(2)}, u32[]{:S(2)}) collective-permute-start(bf16[2,384,256]{2,1,0:T(8,128)(2,1)S(1)} %get-tuple-element.45), channel_id=1, source_target_pairs={{0,96},{16,48},{32,64},{48,16},{64,32},{80,112},{96,0},{112,80},{1... | collective-permute-start | bytes 1179656 | tf_op jit(solution)/shard_map/ppermute | solution.py:38
  110.8 13.8 %collective-permute-start.23 = (bf16[2,384,256]{2,1,0:T(8,128)(2,1)S(1)}, bf16[2,384,256]{2,1,0:T(8,128)(2,1)S(1)}, u32[]{:S(2)}, u32[]{:S(2)}) collective-permute-start(bf16[2,384,256]{2,1,0:T(8,128)(2,1)S(1)} %get-tuple-element.46), channel_id=1, source_target_pairs={{0,64},{16,80},{32,96},{48,112},{64,0},{80,16},{96,32},{112,48},{1... | collective-permute-start | bytes 1179656 | tf_op jit(solution)/shard_map/ppermute | solution.py:38
  111.4 19.4 %collective-permute-start.26 = (bf16[4,384,256]{2,1,0:T(8,128)(2,1)S(1)}, bf16[4,384,256]{2,1,0:T(8,128)(2,1)S(1)}, u32[]{:S(2)}, u32[]{:S(2)}) collective-permute-start(bf16[4,384,256]{2,1,0:T(8,128)(2,1)S(1)} %choose.5), channel_id=1, source_target_pairs={{0,16},{16,0},{32,48},{48,32},{64,80},{80,64},{96,112},{112,96},{1... | collective-permute-start | bytes 2359304 | tf_op jit(solution)/shard_map/ppermute | solution.py:42
  119.7 11.2 %copy-start = (bf16[8192,256]{1,0:T(8,128)(2,1)S(1)}, bf16[8192,256]{1,0:T(8,128)(2,1)}, u32[]{:S(2)}) copy-start(bf16[8192,256]{1,0:T(8,128)(2,1)} %prev.5) | copy-start | bytes 12582916
  124.6 10.7 %collective-permute-start.24 = (bf16[4,384,256]{2,1,0:T(8,128)(2,1)S(1)}, bf16[4,384,256]{2,1,0:T(8,128)(2,1)S(1)}, u32[]{:S(2)}, u32[]{:S(2)}) collective-permute-start(bf16[4,384,256]{2,1,0:T(8,128)(2,1)S(1)} %choose.3), channel_id=1, source_target_pairs={{0,16},{16,0},{32,48},{48,32},{64,80},{80,64},{96,112},{112,96},{1... | collective-permute-start | bytes 2359304 | tf_op jit(solution)/shard_map/ppermute | solution.py:42
  130.7 2.6 %collective-permute-start.25 = (bf16[4,256,256]{2,1,0:T(8,128)(2,1)S(1)}, bf16[4,256,256]{2,1,0:T(8,128)(2,1)S(1)}, u32[]{:S(2)}, u32[]{:S(2)}) collective-permute-start(bf16[4,256,256]{2,1,0:T(8,128)(2,1)S(1)} %choose.4), channel_id=1, source_target_pairs={{0,16},{16,0},{32,48},{48,32},{64,80},{80,64},{96,112},{112,96},{1... | collective-permute-start | bytes 1572872 | tf_op jit(solution)/shard_map/ppermute | solution.py:42
